TPU v7x, 256 devices: a whole 4x4x8 slice. The times are simulated.
256 devices in a mesh: ctx: 64 (over z, x, core), tp: 4 (over y).
Axes of the slice: x: 4, y: 4, z: 8, core: 2. Of those that a mesh axis runs over, the one named last changes fastest.
Arguments:
- inputs: bfloat16 [32768, 64, 128], P('ctx', 'tp'), may hold values from -6 to 6
- b_proj: bfloat16 [32768, 128], P('ctx'), may hold values from -0.5 to 0.5
- c_proj: bfloat16 [32768, 128], P('ctx'), may hold values from -0.5 to 0.5
- logdecay: float32 [32768, 64], P('ctx', 'tp'), may hold values from -1 to 0, as said below
- skip_gain: float32 [64], P('tp'), may hold values from 0.5 to 1.5
- grad_out: bfloat16 [32768, 64, 128], P('ctx', 'tp'), may hold values from -6 to 6
Outputs:
- outputs: bfloat16 [32768, 64, 128], P('ctx', 'tp')
- grad_inputs: bfloat16 [32768, 64, 128], P('ctx', 'tp')
- grad_logdecay: float32 [32768, 64], P('ctx', 'tp')
- grad_b: float32 [32768, 128], P('ctx')
- grad_c: float32 [32768, 128], P('ctx')
Inputs may be any that keep to these rules, and one draw needn't show every extreme that they name: `logdecay`: non-positive log decays.
All inputs are finite; a program needn't handle non-finite values.
Results may differ from a plain program's by a relative error of at most 0.0025.
Values sent between devices are 32-bit elements; how exact they have to be, the bound alone decides.
No kernel may reach another device: no remote copies, remote signals or barrier semaphores. Data moves between devices by JAX's collectives and lax.ppermute only.
A program may use at most 320 MiB of HBM per device.

v0:
```python
import functools

import jax
import jax.numpy as jnp
from jax import lax
from jax.experimental import pallas as pl
from jax.experimental.pallas import tpu as pltpu
from jax.sharding import PartitionSpec as P

SPAN = 256
HEADS = 16
HALF = 8
WIDTH = 128
CHIPS = 4
QUAD = 4
LOG_ROWS = 8
f32 = jnp.float32
bf16 = jnp.bfloat16
TALL = 2 * WIDTH + LOG_ROWS
anywhere = pl.BlockSpec(memory_space=pl.ANY)


def params():
    return pltpu.CompilerParams(vmem_limit_bytes=24 * 1024 * 1024)


def place():
    position = lax.axis_index("ctx")
    return position % 2, position // 2 % 4, position // 8


def dot(a, b, dims):
    return lax.dot_general(a, b, (dims, ((), ())), preferred_element_type=f32)


def split_two(a):
    high = a.astype(bf16)
    return high, (a - high.astype(f32)).astype(bf16)


def split_three(a):
    high = a.astype(bf16)
    rest = a - high.astype(f32)
    middle = rest.astype(bf16)
    return high, middle, (rest - middle.astype(f32)).astype(bf16)


def triangle(strict):
    row = lax.broadcasted_iota(jnp.int32, (SPAN, SPAN), 0)
    column = lax.broadcasted_iota(jnp.int32, (SPAN, SPAN), 1)
    kept = column < row if strict else column <= row
    return jnp.where(kept, 1.0, 0.0).astype(bf16)


def running_sum(rows, strict):
    tri = triangle(strict)
    return sum(dot(part, tri, ((1,), (1,))) for part in split_three(rows))


def slot_of(head):
    _, chip, _ = place()
    return (head % HALF // 2 - chip + 4) % 4 * 2 + head % 2


def summary_body(reverse, values, proj, logdecay, *refs):
    if reverse:
        heads_out, send, keep, middle, stage = refs
    else:
        heads_out, send, keep, middle, levels_out, level_rows_out, stage = refs
    step = pl.program_id(0)
    span = 1 - step if reverse else step
    level_rows = running_sum(logdecay[:, pl.ds(pl.multiple_of(span * SPAN, SPAN), SPAN)], False)
    if not reverse:
        levels_out[...] = jnp.transpose(level_rows)
        level_rows_out[...] = level_rows
    weight = jnp.exp(level_rows) if reverse else jnp.exp(level_rows[:, SPAN - 1 : SPAN] - level_rows)
    proj_t = jnp.transpose(proj[...]).astype(f32)
    swapped = jnp.swapaxes(values[...], 0, 1)
    heads_out[...] = swapped
    for head in range(HEADS):
        weighted = jnp.concatenate(split_two(proj_t * weight[head : head + 1, :]), axis=0)
        both = dot(weighted, swapped[head], ((1,), (0,)))
        stage[step, head] = both[:WIDTH] + both[WIDTH:]

    @pl.when(step == 1)
    def _():
        core, _, _ = place()
        carried = jnp.exp(level_rows[:, SPAN - 1 : SPAN])
        all_log = jnp.sum(logdecay[...], axis=1, keepdims=True)
        middle[...] = stage[0]
        for own, out in ((False, send), (True, keep)):
            half = core if own else 1 - core
            crossed = jnp.where(half == 0, carried[:HALF], carried[HALF:])
            log = jnp.where(half == 0, all_log[:HALF], all_log[HALF:])
            for at in range(HALF):
                slot = slot_of(at)
                head = half * HALF + at
                out[slot, :WIDTH, :] = stage[1, head] + crossed[at : at + 1, :] * stage[0, head]
                if not reverse:
                    out[slot, WIDTH:, :] = jnp.broadcast_to(log[at : at + 1, :], (LOG_ROWS, WIDTH))


def summary(reverse, *arrays):
    values, proj, log_rows = [pltpu.with_memory_space_constraint(array, pltpu.HBM) for array in arrays]
    tokens = values.shape[0]

    def turn(step):
        return 1 - step if reverse else step

    rows = WIDTH if reverse else WIDTH + LOG_ROWS
    packed = jax.ShapeDtypeStruct((HALF, rows, WIDTH), f32)
    packed_spec = pl.BlockSpec((HALF, rows, WIDTH), lambda s: (0, 0, 0))
    shapes = [
        jax.ShapeDtypeStruct((HEADS, tokens, WIDTH), bf16),
        packed,
        packed,
        jax.ShapeDtypeStruct((HEADS, WIDTH, WIDTH), f32),
    ]
    specs = [
        pl.BlockSpec((HEADS, SPAN, WIDTH), lambda s: (0, turn(s), 0)),
        packed_spec,
        packed_spec,
        pl.BlockSpec((HEADS, WIDTH, WIDTH), lambda s: (0, 0, 0)),
    ]
    if not reverse:
        shapes += [
            jax.ShapeDtypeStruct((tokens, HEADS), f32),
            jax.ShapeDtypeStruct((HEADS, tokens), f32),
        ]
        specs += [
            pl.BlockSpec((SPAN, HEADS), lambda s: (turn(s), 0)),
            pl.BlockSpec((HEADS, SPAN), lambda s: (0, turn(s))),
        ]
    return pl.pallas_call(
        functools.partial(summary_body, reverse),
        grid=(2,),
        in_specs=[
            pl.BlockSpec((SPAN, HEADS, WIDTH), lambda s: (turn(s), 0, 0)),
            pl.BlockSpec((SPAN, WIDTH), lambda s: (turn(s), 0)),
            pl.BlockSpec((HEADS, tokens), lambda s: (0, 0)),
        ],
        out_specs=specs,
        out_shape=shapes,
        scratch_shapes=[pltpu.VMEM((2, HEADS, WIDTH, WIDTH), f32)],
        compiler_params=params(),
        name="summary_b" if reverse else "summary_f",
    )(values, proj, log_rows)


def line_sums(product, head):
    row = lax.broadcasted_iota(jnp.int32, (2 * WIDTH, WIDTH), 1)
    picked = jnp.where(row == head, 1.0, 0.0).astype(bf16)
    return dot(jnp.concatenate(split_two(product), axis=1), picked, ((1,), (0,)))


def intra_body(x_ref, dy_ref, b_ref, c_ref, lev_ref, lev_rows_ref, gain_ref, *refs):
    y_out, dx_out, x_t_out, dy_t_out, cross_out, grads_out = refs[-6:]
    b = b_ref[...]
    c = c_ref[...]
    low, high = slice(0, 128), slice(128, 256)
    blocks = ((low, low), (high, low), (high, high))
    scores = [dot(c[t], b[s], ((1,), (1,))) for t, s in blocks]
    row = lax.broadcasted_iota(jnp.int32, (128, 128), 0)
    column = lax.broadcasted_iota(jnp.int32, (128, 128), 1)
    causal = column <= row
    score_grad = [jnp.zeros((128, 128), f32) for _ in blocks]
    cross = jnp.zeros((SPAN, WIDTH), f32)
    for head in range(HEADS):
        x = x_ref[head]
        dy = dy_ref[head]
        gain = gain_ref[:, head : head + 1]
        level = lev_ref[:, head : head + 1]
        level_row = lev_rows_ref[head : head + 1, :]
        mixing = []
        for at, (t, s) in enumerate(blocks):
            distance = level[t] - level_row[:, s]
            if t == s:
                distance = jnp.where(causal, distance, -1e30)
            decay = jnp.exp(distance)
            mixing.append((scores[at] * decay).astype(bf16))
            score_grad[at] = score_grad[at] + decay * dot(dy[t], x[s], ((1,), (1,)))
        lower = jnp.concatenate(mixing[1:], axis=1)
        left = jnp.concatenate(mixing[:2], axis=0)
        y = jnp.concatenate([dot(mixing[0], x[low], ((1,), (0,))), dot(lower, x, ((1,), (0,)))], axis=0)
        dx = jnp.concatenate([dot(left, dy, ((0,), (0,))), dot(mixing[2], dy[high], ((0,), (0,)))], axis=0)
        x32 = x.astype(f32)
        dy32 = dy.astype(f32)
        cross = cross + line_sums(y * dy32 - dx * x32, head)
        x_t_out[head] = jnp.transpose(x)
        dy_t_out[head] = jnp.transpose(dy)
        y_out[head] = y + gain * x32
        dx_out[head] = dx + gain * dy32
    cross_out[...] = cross[:, :HEADS]
    g00, g10, g11 = [split_two(g) for g in score_grad]
    grad_c0 = sum(dot(g, b[low], ((1,), (0,))) for g in g00)
    grad_c1 = sum(dot(g, b[low], ((1,), (0,))) for g in g10) + sum(dot(g, b[high], ((1,), (0,))) for g in g11)
    grad_b0 = sum(dot(g, c[low], ((0,), (0,))) for g in g00) + sum(dot(g, c[high], ((0,), (0,))) for g in g10)
    grad_b1 = sum(dot(g, c[high], ((0,), (0,))) for g in g11)
    grads_out[:WIDTH, low] = jnp.transpose(grad_c0)
    grads_out[:WIDTH, high] = jnp.transpose(grad_c1)
    grads_out[WIDTH:, low] = jnp.transpose(grad_b0)
    grads_out[WIDTH:, high] = jnp.transpose(grad_b1)


def intra(span, x_heads, dy_heads, b_proj, c_proj, levels, level_rows, gain, after, so_far=()):
    tokens = x_heads.shape[1]
    by_head = pl.BlockSpec((HEADS, SPAN, WIDTH), lambda s: (0, span, 0))
    flat = pl.BlockSpec((SPAN, WIDTH), lambda s: (span, 0))
    thin = pl.BlockSpec((SPAN, HEADS), lambda s: (span, 0))
    turned = pl.BlockSpec((HEADS, WIDTH, SPAN), lambda s: (0, 0, span))
    turned_shape = jax.ShapeDtypeStruct((HEADS, WIDTH, tokens), bf16)
    return pl.pallas_call(
        intra_body,
        grid=(1,),
        in_specs=[
            by_head,
            by_head,
            flat,
            flat,
            thin,
            pl.BlockSpec((HEADS, SPAN), lambda s: (0, span)),
            pl.BlockSpec((1, HEADS), lambda s: (0, 0)),
            anywhere,
        ]
        + [anywhere] * len(so_far),
        out_specs=[by_head, by_head, turned, turned, thin, pl.BlockSpec((2 * WIDTH, SPAN), lambda s: (0, span))],
        out_shape=[
            jax.ShapeDtypeStruct((HEADS, tokens, WIDTH), f32),
            jax.ShapeDtypeStruct((HEADS, tokens, WIDTH), f32),
            turned_shape,
            turned_shape,
            jax.ShapeDtypeStruct((tokens, HEADS), f32),
            jax.ShapeDtypeStruct((2 * WIDTH, tokens), f32),
        ],
        input_output_aliases={8 + at: at for at in range(len(so_far))},
        compiler_params=params(),
        name="intra%d" % span,
    )(x_heads, dy_heads, b_proj, c_proj, levels, level_rows, gain, after, *so_far)


def weigh(orders, logs, after, before):
    exponent = jnp.zeros_like(logs[0])
    for order, log in zip(orders, logs):
        exponent = exponent + jnp.where((order > after) & (order < before), log, 0.0)
    return jnp.exp(exponent)


def ranks(reverse, mine):
    spots = [(mine - k + 4) % 4 for k in range(4)]
    return [3 - spot for spot in spots] if reverse else spots


def whole_of(orders, logs, states):
    return sum(weigh(orders, logs, order, 4) * state for order, state in zip(orders, states))


def prefix_of(orders, logs, states, at, entering):
    out = weigh(orders, logs, -1, orders[at]) * entering
    for k in range(4):
        if k != at:
            weight = weigh(orders, logs, orders[k], orders[at])
            out = out + jnp.where(orders[k] < orders[at], weight, 0.0) * states[k]
    return out


def small(body, outs, name, *args, scratch=(), after=()):
    count = len(args)

    def with_after(*refs):
        body(*refs[:count], *refs[count + len(after) :])

    return pl.pallas_call(
        with_after,
        in_specs=[pl.BlockSpec(memory_space=pltpu.VMEM)] * count + [anywhere] * len(after),
        out_shape=[jax.ShapeDtypeStruct(shape, f32) for shape in outs],
        scratch_shapes=[pltpu.VMEM(shape, f32) for shape in scratch],
        compiler_params=params(),
        name=name,
    )(*args, *after)


def core_up_body(keep_f, other_f, keep_b, other_b, *outs):
    first = place()[0] == 0
    for head in range(HALF):
        own_log = keep_f[head, WIDTH : WIDTH + 1, :]
        other_log = other_f[head, WIDTH : WIDTH + 1, :]
        own_forward = jnp.exp(jnp.where(first, other_log, 0.0))
        other_forward = jnp.exp(jnp.where(first, 0.0, own_log))
        own_backward = jnp.exp(jnp.where(first, 0.0, other_log))
        other_backward = jnp.exp(jnp.where(first, own_log, 0.0))
        out = outs[head // 2]
        at = head % 2
        out[at, :WIDTH, :] = own_forward * keep_f[head, :WIDTH, :] + other_forward * other_f[head, :WIDTH, :]
        out[at, WIDTH : 2 * WIDTH, :] = own_backward * keep_b[head] + other_backward * other_b[head]
        out[at, 2 * WIDTH :, :] = keep_f[head, WIDTH:, :] + other_f[head, WIDTH:, :]


def chip_up_body(*refs):
    parts, outs, units = refs[:4], refs[4:8], refs[8]
    _, chip, depth = place()
    for head in range(2):
        logs = [part[head, 2 * WIDTH : 2 * WIDTH + 1, :] for part in parts]
        for way in range(2):
            orders = ranks(way == 1, chip)
            state = whole_of(orders, logs, [part[head, way * WIDTH : way * WIDTH + WIDTH, :] for part in parts])
            for side in range(2):
                units[2 * head + side, 64 * way : 64 * way + 64, :] = state[64 * side : 64 * side + 64]
        for side in range(2):
            units[2 * head + side, 128:, :] = jnp.broadcast_to(sum(logs), (LOG_ROWS, WIDTH))
    for k in range(4):
        outs[k][...] = units[(depth + k) % 4]


def depth_up_body(*refs):
    parts, out = refs[:4], refs[4]
    depth = place()[2]
    logs = [part[128:129, :] for part in parts]
    ahead = whole_of(ranks(False, depth % 4), logs, [part[:64, :] for part in parts])
    behind = whole_of(ranks(True, depth % 4), logs, [part[64:128, :] for part in parts])
    out[...] = jnp.where(depth < 4, ahead, behind)


def depth_down_body(*refs):
    parts, came, outs = refs[:4], refs[4], refs[5:]
    depth = place()[2]
    logs = [part[128:129, :] for part in parts]
    for way in range(2):
        orders = ranks(way == 1, depth % 4)
        states = [part[64 * way : 64 * way + 64, :] for part in parts]
        entering = jnp.where((depth >= 4) == (way == 0), came[...], 0.0)
        for k in range(4):
            outs[k][64 * way : 64 * way + 64, :] = prefix_of(orders, logs, states, k, entering)


def chip_down_body(*refs):
    parts, pieces, outs, units = refs[:4], refs[4:8], refs[8:12], refs[12]
    _, chip, depth = place()
    for k in range(4):
        units[(depth + k) % 4] = pieces[k][...]
    for head in range(2):
        logs = [part[head, 2 * WIDTH : 2 * WIDTH + 1, :] for part in parts]
        for way in range(2):
            orders = ranks(way == 1, chip)
            rows = slice(way * WIDTH, way * WIDTH + WIDTH)
            entering = jnp.concatenate(
                [units[2 * head + side, 64 * way : 64 * way + 64, :] for side in range(2)], axis=0
            )
            states = [part[head, rows, :] for part in parts]
            for k in range(4):
                outs[k][head, rows, :] = prefix_of(orders, logs, states, k, entering)


def core_down_body(keep_f, other_f, keep_b, other_b, *refs):
    pieces, mine, theirs = refs[:4], refs[4], refs[5]
    first = place()[0] == 0
    for head in range(HALF):
        forward = pieces[head // 2][head % 2, :WIDTH, :]
        backward = pieces[head // 2][head % 2, WIDTH:, :]
        own_decay = jnp.exp(keep_f[head, WIDTH : WIDTH + 1, :])
        other_decay = jnp.exp(other_f[head, WIDTH : WIDTH + 1, :])
        mine[head, :WIDTH, :] = jnp.where(first, forward, other_decay * forward + other_f[head, :WIDTH, :])
        mine[head, WIDTH:, :] = jnp.where(first, other_decay * backward + other_b[head], backward)
        theirs[head, :WIDTH, :] = jnp.where(first, own_decay * forward + keep_f[head, :WIDTH, :], forward)
        theirs[head, WIDTH:, :] = jnp.where(first, backward, own_decay * backward + keep_b[head])


def over_ctx(array, target):
    return lax.ppermute(array, "ctx", [(i, target(i)) for i in range(64)])


def swap_cores(array):
    return over_ctx(array, lambda i: i ^ 1)


def along_x(array, k):
    return over_ctx(array, lambda i: i // 8 * 8 + (i // 2 + k) % 4 * 2 + i % 2)


def along_z(array, k):
    return over_ctx(array, lambda i: i // 32 * 32 + (i // 8 + k) % 4 * 8 + i % 8)


def across_z(array):
    return over_ctx(array, lambda i: i ^ 32)


def spread(parts, move, sign):
    return [parts[0]] + [move(parts[k], sign * k) for k in (1, 2, 3)]


def state_at(span, way, incoming, middle, crossed):
    return jnp.where(span == 1 - way, crossed * incoming + middle, incoming)


def row_weight(way, levels):
    return jnp.exp(levels[SPAN - 1 : SPAN, :] - levels) if way else jnp.exp(levels)


def half_of(own, array):
    core, _, _ = place()
    half = core if own else 1 - core
    return jnp.where(half == 0, array[:HALF], array[HALF:])


def grad_body(own, states, middle_f, middle_b, level_rows, x_turned, dy_turned, base, *refs):
    core, _, _ = place()
    half = core if own else 1 - core
    for span in range(2):
        lanes = slice(span * SPAN, span * SPAN + SPAN)
        rows = half_of(own, level_rows[:, lanes])
        for way, middle, values in ((0, middle_f, dy_turned), (1, middle_b, x_turned)):
            weight = jnp.exp(rows[:, SPAN - 1 : SPAN] - rows) if way else jnp.exp(rows)
            last = 2 * SPAN - 1 if way else SPAN - 1
            crossed = half_of(own, jnp.exp(level_rows[:, last : last + 1]))
            of_way = slice(way * WIDTH, way * WIDTH + WIDTH)
            acc = base[of_way, lanes]
            for at in range(HALF):
                head = half * HALF + at
                state = states[slot_of(at), of_way, :]
                if span == 1 - way:
                    state = crossed[at : at + 1, :] * state + middle[head]
                value = values[head, :, lanes]
                line = dot(
                    jnp.concatenate(split_two(state), axis=1),
                    jnp.concatenate([value, value], axis=0),
                    ((1,), (0,)),
                )
                acc = acc + weight[at : at + 1, :] * line
            if own:
                refs[0][of_way, lanes] = acc
            else:
                refs[4][lanes, of_way] = jnp.transpose(acc)
    if not own:
        mine_tp = lax.axis_index("tp")
        for k in range(4):
            start = pl.multiple_of((mine_tp + k) % 4 * 128, 128)
            refs[k][...] = refs[4][pl.ds(start, 128), :]


def grad_call(own, states, middle_f, middle_b, level_rows, x_turned, dy_turned, base):
    tokens = base.shape[1]
    outs = [base.shape] if own else [(tokens // 4, 2 * WIDTH)] * 4
    return small(
        functools.partial(grad_body, own),
        outs,
        "grads_own" if own else "grads_other",
        states,
        middle_f,
        middle_b,
        level_rows,
        x_turned,
        dy_turned,
        base,
        scratch=[] if own else [(tokens, 2 * WIDTH)],
    )


def value_body(way, got, mine, middle, levels_all, levels_ref, proj, part, values, _, out, cross_out, wide):
    core, _, _ = place()
    span = pl.program_id(0)
    weight = row_weight(way, levels_ref[...])
    row = 2 * SPAN - 1 if way else SPAN - 1
    crossed = jnp.exp(levels_all[row : row + 1, :])
    doubled = jnp.concatenate([proj[...], proj[...]], axis=1)
    cross = jnp.zeros((SPAN, WIDTH), f32)
    rows = slice(way * WIDTH, way * WIDTH + WIDTH)
    for head in range(HEADS):
        slot = slot_of(head)
        incoming = jnp.where(head // HALF == core, mine[slot, rows, :], got[slot, rows, :])
        state = state_at(span, way, incoming, middle[head], crossed[:, head : head + 1])
        far = dot(doubled, jnp.concatenate(split_two(state), axis=0), ((1,), (0,)))
        far = far * weight[:, head : head + 1]
        cross = cross + line_sums(far * values[head].astype(f32), head)
        wide[head] = (part[head] + far).astype(bf16)
    out[...] = jnp.swapaxes(wide[...], 0, 1)
    cross_out[...] = cross[:, :HEADS]


def value_call(way, got, mine, middle, levels, proj, part, values, after):
    tokens = levels.shape[0]
    states = pl.BlockSpec((HALF, 2 * WIDTH, WIDTH), lambda s: (0, 0, 0))
    by_head = pl.BlockSpec((HEADS, SPAN, WIDTH), lambda s: (0, s, 0))
    thin = pl.BlockSpec((SPAN, HEADS), lambda s: (s, 0))
    return pl.pallas_call(
        functools.partial(value_body, way),
        grid=(2,),
        in_specs=[
            states,
            states,
            pl.BlockSpec((HEADS, WIDTH, WIDTH), lambda s: (0, 0, 0)),
            pl.BlockSpec((tokens, HEADS), lambda s: (0, 0)),
            thin,
            pl.BlockSpec((SPAN, WIDTH), lambda s: (s, 0)),
            by_head,
            by_head,
            anywhere,
        ],
        out_specs=[pl.BlockSpec((SPAN, HEADS, WIDTH), lambda s: (s, 0, 0)), thin],
        out_shape=[
            jax.ShapeDtypeStruct((tokens, HEADS, WIDTH), bf16),
            jax.ShapeDtypeStruct((tokens, HEADS), f32),
        ],
        scratch_shapes=[pltpu.VMEM((HEADS, SPAN, WIDTH), bf16)],
        compiler_params=params(),
        name="values_b" if way else "values_f",
    )(got, mine, middle, levels, levels, proj, part, values, after)


def decay_body(near, forward, backward, got, mine, send_b, keep_b, level_rows, out, done):
    core, _, _ = place()
    sublane = lax.broadcasted_iota(jnp.int32, (HEADS, 1), 0)
    start = jnp.zeros((HEADS, 1), f32)
    all_log = level_rows[:, SPAN - 1 : SPAN] + level_rows[:, 2 * SPAN - 1 : 2 * SPAN]
    for head in range(HEADS):
        slot = slot_of(head)
        own = head // HALF == core
        incoming = jnp.where(own, mine[slot], got[slot])
        local = jnp.where(own, keep_b[slot], send_b[slot])
        pulled = local + jnp.exp(all_log[head : head + 1, :]) * incoming[WIDTH:]
        line = jnp.sum(jnp.sum(incoming[:WIDTH] * pulled, axis=0, keepdims=True), axis=1, keepdims=True)
        start = jnp.where(sublane == head, line, start)
    for span in range(2):
        rows = slice(span * SPAN, span * SPAN + SPAN)
        cross = jnp.transpose(near[rows, :] + forward[rows, :] - backward[rows, :])
        out[:, rows] = start - running_sum(cross, True)
        start = start - jnp.sum(cross, axis=1, keepdims=True)
    done[...] = jnp.zeros_like(done)


def over_tp(array, k):
    return lax.ppermute(array, "tp", [(i, (i + k) % 4) for i in range(4)])


def add_body(p0, p1, p2, p3, out):
    out[...] = p0[...] + p1[...] + p2[...] + p3[...]


def join_body(p0, p1, p2, p3, c_out, b_out):
    mine = lax.axis_index("tp")
    for k, piece in enumerate((p0, p1, p2, p3)):
        rows = pl.ds(pl.multiple_of((mine - k + 4) % 4 * 128, 128), 128)
        c_out[rows, :] = piece[:, :WIDTH]
        b_out[rows, :] = piece[:, WIDTH:]


def on_device(inputs, b_proj, c_proj, logdecay, skip_gain, grad_out):
    tokens = inputs.shape[0]
    log_rows = logdecay.T
    gain = skip_gain.reshape(1, HEADS)
    x_heads, send_f, keep_f, middle_f, levels, level_rows = summary(False, inputs, b_proj, log_rows)
    other_f = swap_cores(send_f)
    dy_heads, send_b, keep_b, middle_b = summary(True, grad_out, c_proj, log_rows)
    other_b = swap_cores(send_b)

    chips = small(core_up_body, [(2, TALL, WIDTH)] * 4, "core_up", keep_f, other_f, keep_b, other_b)
    local = (x_heads, dy_heads, b_proj, c_proj, levels, level_rows, gain)
    first = intra(0, *local, chips[0])
    chips = spread(chips, along_x, 1)
    unit = (WIDTH + LOG_ROWS, WIDTH)
    units = small(chip_up_body, [unit] * 4, "chip_up", *chips, scratch=[(4,) + unit], after=[first[-1]])
    units = spread(units, along_z, 1)
    (quad,) = small(depth_up_body, [(64, WIDTH)], "depth_up", *units)
    quad = across_z(quad)
    back = small(depth_down_body, [(WIDTH, WIDTH)] * 4, "depth_down", *units, quad)
    back = spread(back, along_z, -1)
    entering = small(
        chip_down_body, [(2, 2 * WIDTH, WIDTH)] * 4, "chip_down", *chips, *back, scratch=[(4, WIDTH, WIDTH)]
    )
    y_part, dx_part, x_turned, dy_turned, near, base = intra(1, *local, entering[0], first)
    entering = spread(entering, along_x, -1)
    mine, theirs = small(
        core_down_body,
        [(HALF, 2 * WIDTH, WIDTH)] * 2,
        "core_down",
        keep_f,
        other_f,
        keep_b,
        other_b,
        *entering,
        after=[base],
    )
    got = swap_cores(theirs)

    (base,) = grad_call(True, mine, middle_f, middle_b, level_rows, x_turned, dy_turned, base)
    pieces = grad_call(False, got, middle_f, middle_b, level_rows, x_turned, dy_turned, base)
    outputs, cross_f = value_call(0, got, mine, middle_f, levels, c_proj, y_part, dy_heads, pieces[0])
    pieces = spread(pieces, over_tp, 1)
    (summed,) = small(add_body, [pieces[0].shape], "add", *pieces, after=[cross_f])
    grad_inputs, cross_b = value_call(1, got, mine, middle_b, levels, b_proj, dx_part, x_heads, summed)
    decays, done = small(
        decay_body,
        [(HEADS, tokens), (8, WIDTH)],
        "decay",
        near,
        cross_f,
        cross_b,
        got,
        mine,
        send_b,
        keep_b,
        level_rows,
    )
    joined = [summed] + [over_tp(summed, k) for k in (1, 2, 3)]
    grad_c, grad_b = small(join_body, [(tokens, WIDTH)] * 2, "join", *joined, after=[done])
    return outputs, grad_inputs, decays.T, grad_b, grad_c


def solution(mesh):
    placed = (
        P("ctx", "tp", None),
        P("ctx", None),
        P("ctx", None),
        P("ctx", "tp"),
        P("tp"),
        P("ctx", "tp", None),
    )
    return jax.shard_map(
        on_device,
        mesh=mesh,
        in_specs=placed,
        out_specs=(
            P("ctx", "tp", None),
            P("ctx", "tp", None),
            P("ctx", "tp"),
            P("ctx", None),
            P("ctx", None),
        ),
        check_vma=False,
    )
```

profile of v0, /device:TPU:1, one launch (start us, length us, event | category | flops | bytes accessed | tf_op | source)
XLA Modules:
  0.0 99.3 jit_solution(9796485079580905285)
XLA Ops:
  0.6 4.3 %summary_f.1 = (bf16[16,512,128]{2,1,0:T(8,128)(2,1)S(1)}, f32[8,136,128]{2,1,0:T(8,128)S(1)}, f32[8,136,128]{2,1,0:T(8,128)S(1)}, f32[16,128,128]{2,1,0:T(8,128...) custom-call(bf16[512,16,128]{2,1,0:T(8,128)(2,1)} %values.2, bf16[512,128]{1,0:T(8,128)(2,1)} %proj.7, f32[16,512]{1,0:T(8,128)} %bitcast.5), custom_call_target="tpu_custom_call" | custom-call | tf_op jit(solution)/shard_map/summary_f/pallas_call | solution.py:134
  5.0 3.3 %collective-permute-start = (f32[8,136,128]{2,1,0:T(8,128)S(1)}, f32[8,136,128]{2,1,0:T(8,128)S(1)}, u32[]{:S(2)}, u32[]{:S(2)}) collective-permute-start(f32[8,136,128]{2,1,0:T(8,128)S(1)} %get-tuple-element.58), channel_id=1, source_target_pairs={{0,4},{4,0},{8,12},{12,8},{16,20},{20,16},{24,28},{28,24},{32,36},... | collective-permute-start | bytes 1671176 | tf_op jit(solution)/shard_map/ppermute | solution.py:368
  8.3 4.1 %summary_b.1 = (bf16[16,512,128]{2,1,0:T(8,128)(2,1)S(1)}, f32[8,128,128]{2,1,0:T(8,128)S(1)}, f32[8,128,128]{2,1,0:T(8,128)S(1)}, f32[16,128,128]{2,1,0:T(8,128)S(1)}) custom-call(bf16[512,16,128]{2,1,0:T(8,128)(2,1)} %values.3, bf16[512,128]{1,0:T(8,128)(2,1)} %proj.6, f32[16,512]{1,0:T(8,128)} %bitcast.6), custom_call_target="tpu_custom_call" | custom-call | tf_op jit(solution)/shard_map/summary_b/pallas_call | solution.py:134
  12.5 1.9 %collective-permute-done.1.refs_3_ = f32[8,128,128]{2,1,0:T(8,128)S(1)} collective-permute-done((f32[8,128,128]{2,1,0:T(8,128)S(1)}, f32[8,128,128]{2,1,0:T(8,128)S(1)}, u32[]{:S(2)}, u32[]{:S(2)}) %collective-permute-start.1) | collective-permute-done | bytes 524320 | tf_op jit(solution)/shard_map/ppermute | solution.py:368
  14.6 1.9 %collective-permute-start.3 = (f32[2,264,128]{2,1,0:T(8,128)S(1)}, f32[2,264,128]{2,1,0:T(8,128)S(1)}, u32[]{:S(2)}, u32[]{:S(2)}) collective-permute-start(f32[2,264,128]{2,1,0:T(8,128)S(1)} %get-tuple-element.63), channel_id=1, source_target_pairs={{0,16},{4,20},{8,24},{12,28},{16,0},{20,4},{24,8},{28,12},{32,48},... | collective-permute-start | bytes 811016 | tf_op jit(solution)/shard_map/ppermute | solution.py:368
  16.6 1.2 %collective-permute-start.4 = (f32[2,264,128]{2,1,0:T(8,128)S(1)}, f32[2,264,128]{2,1,0:T(8,128)S(1)}, u32[]{:S(2)}, u32[]{:S(2)}) collective-permute-start(f32[2,264,128]{2,1,0:T(8,128)S(1)} %get-tuple-element.64), channel_id=1, source_target_pairs={{0,24},{4,28},{8,0},{12,4},{16,8},{20,12},{24,16},{28,20},{32,56},... | collective-permute-start | bytes 811016 | tf_op jit(solution)/shard_map/ppermute | solution.py:368
  17.7 4.4 %intra0.1 = (f32[16,512,128]{2,1,0:T(8,128)S(1)}, f32[16,512,128]{2,1,0:T(8,128)S(1)}, bf16[16,128,512]{2,1,0:T(8,128)(2,1)S(1)}, bf16[16,128,512]{2,1,0:T(8,128...) custom-call(bf16[16,512,128]{2,1,0:T(8,128)(2,1)S(1)} %get-tuple-element.65.x_ref.values, ...), custom_call_target="tpu_custom_call" | custom-call | tf_op jit(solution)/shard_map/intra0/pallas_call | solution.py:212
  22.2 7.4 %collective-permute-done.2.refs_1_ = f32[2,264,128]{2,1,0:T(8,128)S(1)} collective-permute-done((f32[2,264,128]{2,1,0:T(8,128)S(1)}, f32[2,264,128]{2,1,0:T(8,128)S(1)}, u32[]{:S(2)}, u32[]{:S(2)}) %collective-permute-start.2) | collective-permute-done | bytes 270368 | tf_op jit(solution)/shard_map/ppermute | solution.py:368
  30.7 3.0 %collective-permute-start.6 = (f32[136,128]{1,0:T(8,128)S(1)}, f32[136,128]{1,0:T(8,128)S(1)}, u32[]{:S(2)}, u32[]{:S(2)}) collective-permute-start(f32[136,128]{1,0:T(8,128)S(1)} %get-tuple-element.72), channel_id=1, source_target_pairs={{0,64},{4,68},{8,72},{12,76},{16,80},{20,84},{24,88},{28,92},{32,9... | collective-permute-start | bytes 208904 | tf_op jit(solution)/shard_map/ppermute | solution.py:368
  35.2 3.8 %collective-permute-done.6.refs_2_ = f32[136,128]{1,0:T(8,128)S(1)} collective-permute-done((f32[136,128]{1,0:T(8,128)S(1)}, f32[136,128]{1,0:T(8,128)S(1)}, u32[]{:S(2)}, u32[]{:S(2)}) %collective-permute-start.6) | collective-permute-done | bytes 69664 | tf_op jit(solution)/shard_map/ppermute | solution.py:368
  39.0 5.7 %collective-permute-start.8 = (f32[64,128]{1,0:T(8,128)S(1)}, f32[64,128]{1,0:T(8,128)S(1)}, u32[]{:S(2)}, u32[]{:S(2)}) collective-permute-start(f32[64,128]{1,0:T(8,128)S(1)} %depth_up.1), channel_id=1, source_target_pairs={{0,128},{4,132},{8,136},{12,140},{16,144},{20,148},{24,152},{28,15... | collective-permute-start | bytes 98312 | tf_op jit(solution)/shard_map/ppermute | solution.py:368
  44.7 1.3 %collective-permute-done.8.refs_4_ = f32[64,128]{1,0:T(8,128)S(1)} collective-permute-done((f32[64,128]{1,0:T(8,128)S(1)}, f32[64,128]{1,0:T(8,128)S(1)}, u32[]{:S(2)}, u32[]{:S(2)}) %collective-permute-start.8) | collective-permute-done | bytes 32800 | tf_op jit(solution)/shard_map/ppermute | solution.py:368
  46.1 2.6 %collective-permute-start.9 = (f32[128,128]{1,0:T(8,128)S(1)}, f32[128,128]{1,0:T(8,128)S(1)}, u32[]{:S(2)}, u32[]{:S(2)}) collective-permute-start(f32[128,128]{1,0:T(8,128)S(1)} %get-tuple-element.75), channel_id=1, source_target_pairs={{0,96},{4,100},{8,104},{12,108},{16,112},{20,116},{24,120},{28,124... | collective-permute-start | bytes 196616 | tf_op jit(solution)/shard_map/ppermute | solution.py:368
  49.2 0.9 collective-permute-done.9.refs_5_
  50.1 3.0 %collective-permute-done.10.refs_6_ = f32[128,128]{1,0:T(8,128)S(1)} collective-permute-done((f32[128,128]{1,0:T(8,128)S(1)}, f32[128,128]{1,0:T(8,128)S(1)}, u32[]{:S(2)}, u32[]{:S(2)}) %collective-permute-start.10) | collective-permute-done | bytes 65568 | tf_op jit(solution)/shard_map/ppermute | solution.py:368
  53.1 1.5 %collective-permute-done.11.refs_7_ = f32[128,128]{1,0:T(8,128)S(1)} collective-permute-done((f32[128,128]{1,0:T(8,128)S(1)}, f32[128,128]{1,0:T(8,128)S(1)}, u32[]{:S(2)}, u32[]{:S(2)}) %collective-permute-start.11) | collective-permute-done | bytes 65568 | tf_op jit(solution)/shard_map/ppermute | solution.py:368
  55.0 2.4 %collective-permute-start.12 = (f32[2,256,128]{2,1,0:T(8,128)S(1)}, f32[2,256,128]{2,1,0:T(8,128)S(1)}, u32[]{:S(2)}, u32[]{:S(2)}) collective-permute-start(f32[2,256,128]{2,1,0:T(8,128)S(1)} %get-tuple-element.79), channel_id=1, source_target_pairs={{0,24},{4,28},{8,0},{12,4},{16,8},{20,12},{24,16},{28,20},{32,56},... | collective-permute-start | bytes 786440 | tf_op jit(solution)/shard_map/ppermute | solution.py:368
  58.2 4.4 %intra1.1 = (f32[16,512,128]{2,1,0:T(8,128)S(1)}, f32[16,512,128]{2,1,0:T(8,128)S(1)}, bf16[16,128,512]{2,1,0:T(8,128)(2,1)S(1)}, bf16[16,128,512]{2,1,0:T(8,128...) custom-call(bf16[16,512,128]{2,1,0:T(8,128)(2,1)S(1)} %get-tuple-ele, ...), custom_call_target="tpu_custom_call", output_to_operand_aliasing={{0}: (8, {}), {1}: (9, {}), {2}: (10, {}), {3}: (11, {}), {... | custom-call | tf_op jit(solution)/shard_map/intra1/pallas_call | solution.py:212
  63.1 1.1 %collective-permute-done.13.refs_6_ = f32[2,256,128]{2,1,0:T(8,128)S(1)} collective-permute-done((f32[2,256,128]{2,1,0:T(8,128)S(1)}, f32[2,256,128]{2,1,0:T(8,128)S(1)}, u32[]{:S(2)}, u32[]{:S(2)}) %collective-permute-start.13) | collective-permute-done | bytes 262176 | tf_op jit(solution)/shard_map/ppermute | solution.py:368
  64.2 7.4 %collective-permute-done.14.refs_7_ = f32[2,256,128]{2,1,0:T(8,128)S(1)} collective-permute-done((f32[2,256,128]{2,1,0:T(8,128)S(1)}, f32[2,256,128]{2,1,0:T(8,128)S(1)}, u32[]{:S(2)}, u32[]{:S(2)}) %collective-permute-start.14) | collective-permute-done | bytes 262176 | tf_op jit(solution)/shard_map/ppermute | solution.py:368
  71.8 1.9 %collective-permute-start.15 = (f32[8,256,128]{2,1,0:T(8,128)S(1)}, f32[8,256,128]{2,1,0:T(8,128)S(1)}, u32[]{:S(2)}, u32[]{:S(2)}) collective-permute-start(f32[8,256,128]{2,1,0:T(8,128)S(1)} %get-tuple-element.88), channel_id=1, source_target_pairs={{0,4},{4,0},{8,12},{12,8},{16,20},{20,16},{24,28},{28,24},{32,36},... | collective-permute-start | bytes 3145736 | tf_op jit(solution)/shard_map/ppermute | solution.py:368
  73.8 0.9 grads_own.1.refs_6_
  74.7 1.4 %collective-permute-done.15.refs_0_.got.refs_3_ = f32[8,256,128]{2,1,0:T(8,128)S(1)} collective-permute-done((f32[8,256,128]{2,1,0:T(8,128)S(1)}, f32[8,256,128]{2,1,0:T(8,128)S(1)}, u32[]{:S(2)}, u32[]{:S(2)}) %collective-permute-start.15) | collective-permute-done | bytes 1048608 | tf_op jit(solution)/shard_map/ppermute | solution.py:368
  76.1 1.0 %grads_other.1 = (f32[128,256]{1,0:T(8,128)S(1)}, f32[128,256]{1,0:T(8,128)S(1)}, f32[128,256]{1,0:T(8,128)S(1)}, f32[128,256]{1,0:T(8,128)S(1)}) custom-call(f32[8,256,128]{2,1,0:T(8,128)S(1)} %collective-permute-done.15.refs_0_.got.refs_3_, f32[16,128,128]{2,1,0:T(8,128)S(1)} %get-tuple-element.90.refs_1_.middle, ...), custom_call_target="tpu_custom_call" | custom-call | tf_op jit(solution)/shard_map/grads_other/pallas_call | solution.py:272
  77.1 1.6 %collective-permute-start.16 = (f32[128,256]{1,0:T(8,128)S(1)}, f32[128,256]{1,0:T(8,128)S(1)}, u32[]{:S(2)}, u32[]{:S(2)}) collective-permute-start(f32[128,256]{1,0:T(8,128)S(1)} %get-tuple-element.98), channel_id=1, source_target_pairs={{0,1},{1,2},{2,3},{3,0},{4,5},{5,6},{6,7},{7,4},{8,9},{9,10},{10,1... | collective-permute-start | bytes 393224 | tf_op jit(solution)/shard_map/ppermute | solution.py:531
  78.8 2.6 %collective-permute-start.17 = (f32[128,256]{1,0:T(8,128)S(1)}, f32[128,256]{1,0:T(8,128)S(1)}, u32[]{:S(2)}, u32[]{:S(2)}) collective-permute-start(f32[128,256]{1,0:T(8,128)S(1)} %get-tuple-element.99), channel_id=1, source_target_pairs={{0,2},{1,3},{2,0},{3,1},{4,6},{5,7},{6,4},{7,5},{8,10},{9,11},{10,... | collective-permute-start | bytes 393224 | tf_op jit(solution)/shard_map/ppermute | solution.py:531
  81.4 1.1 %collective-permute-start.18 = (f32[128,256]{1,0:T(8,128)S(1)}, f32[128,256]{1,0:T(8,128)S(1)}, u32[]{:S(2)}, u32[]{:S(2)}) collective-permute-start(f32[128,256]{1,0:T(8,128)S(1)} %get-tuple-element.100), channel_id=1, source_target_pairs={{0,3},{1,0},{2,1},{3,2},{4,7},{5,4},{6,5},{7,6},{8,11},{9,8},{10,9... | collective-permute-start | bytes 393224 | tf_op jit(solution)/shard_map/ppermute | solution.py:531
  82.5 4.7 %values_f.1 = (bf16[512,16,128]{2,1,0:T(8,128)(2,1)}, f32[512,16]{1,0:T(8,128)S(1)}) custom-call(f32[8,256,128]{2,1,0:T(8,128)S(1)} %collective-permute-done.15.refs_0_.got.refs_3_, f32[8,256,128]{2,1,0:T(8,128)S(1)} %get-tuple-element.89.refs_0_.mine.refs_4_, f32[16,128,128]{2,1,0:T(8,128)S(1)} %get-tuple-element.90.refs_1_.middle, ...), custom_call_target="tpu_custom_call" | custom-call | tf_op jit(solution)/shard_map/values_f/pallas_call | solution.py:484
  87.5 2.1 %collective-permute-start.21 = (f32[128,256]{1,0:T(8,128)S(1)}, f32[128,256]{1,0:T(8,128)S(1)}, u32[]{:S(2)}, u32[]{:S(2)}) collective-permute-start(f32[128,256]{1,0:T(8,128)S(1)} %add.1._.refs_0_), channel_id=1, source_target_pairs={{0,3},{1,0},{2,1},{3,2},{4,7},{5,4},{6,5},{7,6},{8,11},{9,8},{10,9... | collective-permute-start | bytes 393224 | tf_op jit(solution)/shard_map/ppermute | solution.py:531
  90.4 4.7 %values_b.1 = (bf16[512,16,128]{2,1,0:T(8,128)(2,1)}, f32[512,16]{1,0:T(8,128)S(1)}) custom-call(f32[8,256,128]{2,1,0:T(8,128)S(1)} %collective-permute-done.15.refs_0_.got.refs_3_, f32[8,256,128]{2,1,0:T(8,128)S(1)} %get-tuple-element.89.refs_0_.mine.refs_4_, f32[16,128,128]{2,1,0:T(8,128)S(1)} %get-tuple-element.92.refs_2_.middle, ...), custom_call_target="tpu_custom_call" | custom-call | tf_op jit(solution)/shard_map/values_b/pallas_call | solution.py:484
  95.1 1.7 %decay.1 = (f32[16,512]{1,0:T(8,128)}, f32[8,128]{1,0:T(8,128)S(1)}) custom-call(f32[512,16]{1,0:T(8,128)S(1)} %get-tuple-element.103.refs_0_, f32[512,16]{1,0:T(8,128)S(1)} %get-tuple-element.101.refs_4_.refs_1_, f32[512,16]{1,0:T(8,128)S(1)} %get-tuple-element.104.refs_2_, f32[8,256,128]{2,1,0:T(8,128)S(1)} %collective-permute-done.15.refs_0_.got.refs_3_, ...), custom_call_target="tpu_custom_call" | custom-call | tf_op jit(solution)/shard_map/decay/pallas_call | solution.py:272
  96.8 1.7 %collective-permute-done.19.refs_1_ = f32[128,256]{1,0:T(8,128)S(1)} collective-permute-done((f32[128,256]{1,0:T(8,128)S(1)}, f32[128,256]{1,0:T(8,128)S(1)}, u32[]{:S(2)}, u32[]{:S(2)}) %collective-permute-start.19) | collective-permute-done | bytes 131104 | tf_op jit(solution)/shard_map/ppermute | solution.py:531
  (35 shorter events, 7.6 us)
Async XLA Ops:
  5.0 12.7 %copy-start = (bf16[512,128]{1,0:T(8,128)(2,1)S(1)}, bf16[512,128]{1,0:T(8,128)(2,1)}, u32[]{:S(2)}) copy-start(bf16[512,128]{1,0:T(8,128)(2,1)} %proj.6) | copy-start | bytes 393220
  5.0 12.7 %copy-start.1 = (bf16[512,128]{1,0:T(8,128)(2,1)S(1)}, bf16[512,128]{1,0:T(8,128)(2,1)}, u32[]{:S(2)}) copy-start(bf16[512,128]{1,0:T(8,128)(2,1)} %proj.7) | copy-start | bytes 393220
  5.0 12.7 %copy-start.2 = (f32[16]{0:T(128)S(1)}, f32[16]{0:T(128)}, u32[]{:S(2)}) copy-start(f32[16]{0:T(128)} %param.10) | copy-start | bytes 196
  5.0 9.4 %collective-permute-start = (f32[8,136,128]{2,1,0:T(8,128)S(1)}, f32[8,136,128]{2,1,0:T(8,128)S(1)}, u32[]{:S(2)}, u32[]{:S(2)}) collective-permute-start(f32[8,136,128]{2,1,0:T(8,128)S(1)} %get-tuple-element.58), channel_id=1, source_target_pairs={{0,4},{4,0},{8,12},{12,8},{16,20},{20,16},{24,28},{28,24},{32,36},... | collective-permute-start | bytes 1671176 | tf_op jit(solution)/shard_map/ppermute | solution.py:368
  12.4 2.0 %collective-permute-start.1 = (f32[8,128,128]{2,1,0:T(8,128)S(1)}, f32[8,128,128]{2,1,0:T(8,128)S(1)}, u32[]{:S(2)}, u32[]{:S(2)}) collective-permute-start(f32[8,128,128]{2,1,0:T(8,128)S(1)} %get-tuple-element.60.refs_5_), channel_id=1, source_target_pairs={{0,4},{4,0},{8,12},{12,8},{16,20},{20,16},{24,28},{28,24},{32,36},... | collective-permute-start | bytes 1572872 | tf_op jit(solution)/shard_map/ppermute | solution.py:368
  14.6 15.0 %collective-permute-start.2 = (f32[2,264,128]{2,1,0:T(8,128)S(1)}, f32[2,264,128]{2,1,0:T(8,128)S(1)}, u32[]{:S(2)}, u32[]{:S(2)}) collective-permute-start(f32[2,264,128]{2,1,0:T(8,128)S(1)} %get-tuple-element.62), channel_id=1, source_target_pairs={{0,8},{4,12},{8,16},{12,20},{16,24},{20,28},{24,0},{28,4},{32,40},... | collective-permute-start | bytes 811016 | tf_op jit(solution)/shard_map/ppermute | solution.py:368
  14.6 14.9 %collective-permute-start.3 = (f32[2,264,128]{2,1,0:T(8,128)S(1)}, f32[2,264,128]{2,1,0:T(8,128)S(1)}, u32[]{:S(2)}, u32[]{:S(2)}) collective-permute-start(f32[2,264,128]{2,1,0:T(8,128)S(1)} %get-tuple-element.63), channel_id=1, source_target_pairs={{0,16},{4,20},{8,24},{12,28},{16,0},{20,4},{24,8},{28,12},{32,48},... | collective-permute-start | bytes 811016 | tf_op jit(solution)/shard_map/ppermute | solution.py:368
  16.6 13.3 %collective-permute-start.4 = (f32[2,264,128]{2,1,0:T(8,128)S(1)}, f32[2,264,128]{2,1,0:T(8,128)S(1)}, u32[]{:S(2)}, u32[]{:S(2)}) collective-permute-start(f32[2,264,128]{2,1,0:T(8,128)S(1)} %get-tuple-element.64), channel_id=1, source_target_pairs={{0,24},{4,28},{8,0},{12,4},{16,8},{20,12},{24,16},{28,20},{32,56},... | collective-permute-start | bytes 811016 | tf_op jit(solution)/shard_map/ppermute | solution.py:368
  30.0 5.1 %collective-permute-start.5 = (f32[136,128]{1,0:T(8,128)S(1)}, f32[136,128]{1,0:T(8,128)S(1)}, u32[]{:S(2)}, u32[]{:S(2)}) collective-permute-start(f32[136,128]{1,0:T(8,128)S(1)} %get-tuple-element.71), channel_id=1, source_target_pairs={{0,32},{4,36},{8,40},{12,44},{16,48},{20,52},{24,56},{28,60},{32,6... | collective-permute-start | bytes 208904 | tf_op jit(solution)/shard_map/ppermute | solution.py:368
  30.7 8.2 %collective-permute-start.6 = (f32[136,128]{1,0:T(8,128)S(1)}, f32[136,128]{1,0:T(8,128)S(1)}, u32[]{:S(2)}, u32[]{:S(2)}) collective-permute-start(f32[136,128]{1,0:T(8,128)S(1)} %get-tuple-element.72), channel_id=1, source_target_pairs={{0,64},{4,68},{8,72},{12,76},{16,80},{20,84},{24,88},{28,92},{32,9... | collective-permute-start | bytes 208904 | tf_op jit(solution)/shard_map/ppermute | solution.py:368
  33.7 5.2 %collective-permute-start.7 = (f32[136,128]{1,0:T(8,128)S(1)}, f32[136,128]{1,0:T(8,128)S(1)}, u32[]{:S(2)}, u32[]{:S(2)}) collective-permute-start(f32[136,128]{1,0:T(8,128)S(1)} %get-tuple-element.73), channel_id=1, source_target_pairs={{0,96},{4,100},{8,104},{12,108},{16,112},{20,116},{24,120},{28,124... | collective-permute-start | bytes 208904 | tf_op jit(solution)/shard_map/ppermute | solution.py:368
  39.0 7.0 %collective-permute-start.8 = (f32[64,128]{1,0:T(8,128)S(1)}, f32[64,128]{1,0:T(8,128)S(1)}, u32[]{:S(2)}, u32[]{:S(2)}) collective-permute-start(f32[64,128]{1,0:T(8,128)S(1)} %depth_up.1), channel_id=1, source_target_pairs={{0,128},{4,132},{8,136},{12,140},{16,144},{20,148},{24,152},{28,15... | collective-permute-start | bytes 98312 | tf_op jit(solution)/shard_map/ppermute | solution.py:368
  46.1 4.0 %collective-permute-start.9 = (f32[128,128]{1,0:T(8,128)S(1)}, f32[128,128]{1,0:T(8,128)S(1)}, u32[]{:S(2)}, u32[]{:S(2)}) collective-permute-start(f32[128,128]{1,0:T(8,128)S(1)} %get-tuple-element.75), channel_id=1, source_target_pairs={{0,96},{4,100},{8,104},{12,108},{16,112},{20,116},{24,120},{28,124... | collective-permute-start | bytes 196616 | tf_op jit(solution)/shard_map/ppermute | solution.py:368
  48.7 4.4 %collective-permute-start.10 = (f32[128,128]{1,0:T(8,128)S(1)}, f32[128,128]{1,0:T(8,128)S(1)}, u32[]{:S(2)}, u32[]{:S(2)}) collective-permute-start(f32[128,128]{1,0:T(8,128)S(1)} %get-tuple-element.76), channel_id=1, source_target_pairs={{0,64},{4,68},{8,72},{12,76},{16,80},{20,84},{24,88},{28,92},{32,9... | collective-permute-start | bytes 196616 | tf_op jit(solution)/shard_map/ppermute | solution.py:368
  49.2 5.4 %collective-permute-start.11 = (f32[128,128]{1,0:T(8,128)S(1)}, f32[128,128]{1,0:T(8,128)S(1)}, u32[]{:S(2)}, u32[]{:S(2)}) collective-permute-start(f32[128,128]{1,0:T(8,128)S(1)} %get-tuple-element.77), channel_id=1, source_target_pairs={{0,32},{4,36},{8,40},{12,44},{16,48},{20,52},{24,56},{28,60},{32,6... | collective-permute-start | bytes 196616 | tf_op jit(solution)/shard_map/ppermute | solution.py:368
  55.0 8.1 %collective-permute-start.12 = (f32[2,256,128]{2,1,0:T(8,128)S(1)}, f32[2,256,128]{2,1,0:T(8,128)S(1)}, u32[]{:S(2)}, u32[]{:S(2)}) collective-permute-start(f32[2,256,128]{2,1,0:T(8,128)S(1)} %get-tuple-element.79), channel_id=1, source_target_pairs={{0,24},{4,28},{8,0},{12,4},{16,8},{20,12},{24,16},{28,20},{32,56},... | collective-permute-start | bytes 786440 | tf_op jit(solution)/shard_map/ppermute | solution.py:368
  57.4 6.8 %collective-permute-start.13 = (f32[2,256,128]{2,1,0:T(8,128)S(1)}, f32[2,256,128]{2,1,0:T(8,128)S(1)}, u32[]{:S(2)}, u32[]{:S(2)}) collective-permute-start(f32[2,256,128]{2,1,0:T(8,128)S(1)} %get-tuple-element.80), channel_id=1, source_target_pairs={{0,16},{4,20},{8,24},{12,28},{16,0},{20,4},{24,8},{28,12},{32,48},... | collective-permute-start | bytes 786440 | tf_op jit(solution)/shard_map/ppermute | solution.py:368
  58.0 13.6 %collective-permute-start.14 = (f32[2,256,128]{2,1,0:T(8,128)S(1)}, f32[2,256,128]{2,1,0:T(8,128)S(1)}, u32[]{:S(2)}, u32[]{:S(2)}) collective-permute-start(f32[2,256,128]{2,1,0:T(8,128)S(1)} %get-tuple-element.81), channel_id=1, source_target_pairs={{0,8},{4,12},{8,16},{12,20},{16,24},{20,28},{24,0},{28,4},{32,40},... | collective-permute-start | bytes 786440 | tf_op jit(solution)/shard_map/ppermute | solution.py:368
  71.8 4.2 %collective-permute-start.15 = (f32[8,256,128]{2,1,0:T(8,128)S(1)}, f32[8,256,128]{2,1,0:T(8,128)S(1)}, u32[]{:S(2)}, u32[]{:S(2)}) collective-permute-start(f32[8,256,128]{2,1,0:T(8,128)S(1)} %get-tuple-element.88), channel_id=1, source_target_pairs={{0,4},{4,0},{8,12},{12,8},{16,20},{20,16},{24,28},{28,24},{32,36},... | collective-permute-start | bytes 3145736 | tf_op jit(solution)/shard_map/ppermute | solution.py:368
  77.1 10.0 %collective-permute-start.16 = (f32[128,256]{1,0:T(8,128)S(1)}, f32[128,256]{1,0:T(8,128)S(1)}, u32[]{:S(2)}, u32[]{:S(2)}) collective-permute-start(f32[128,256]{1,0:T(8,128)S(1)} %get-tuple-element.98), channel_id=1, source_target_pairs={{0,1},{1,2},{2,3},{3,0},{4,5},{5,6},{6,7},{7,4},{8,9},{9,10},{10,1... | collective-permute-start | bytes 393224 | tf_op jit(solution)/shard_map/ppermute | solution.py:531
  78.8 8.7 %collective-permute-start.17 = (f32[128,256]{1,0:T(8,128)S(1)}, f32[128,256]{1,0:T(8,128)S(1)}, u32[]{:S(2)}, u32[]{:S(2)}) collective-permute-start(f32[128,256]{1,0:T(8,128)S(1)} %get-tuple-element.99), channel_id=1, source_target_pairs={{0,2},{1,3},{2,0},{3,1},{4,6},{5,7},{6,4},{7,5},{8,10},{9,11},{10,... | collective-permute-start | bytes 393224 | tf_op jit(solution)/shard_map/ppermute | solution.py:531
  81.4 6.1 %collective-permute-start.18 = (f32[128,256]{1,0:T(8,128)S(1)}, f32[128,256]{1,0:T(8,128)S(1)}, u32[]{:S(2)}, u32[]{:S(2)}) collective-permute-start(f32[128,256]{1,0:T(8,128)S(1)} %get-tuple-element.100), channel_id=1, source_target_pairs={{0,3},{1,0},{2,1},{3,2},{4,7},{5,4},{6,5},{7,6},{8,11},{9,8},{10,9... | collective-permute-start | bytes 393224 | tf_op jit(solution)/shard_map/ppermute | solution.py:531
  87.5 9.3 %collective-permute-start.21 = (f32[128,256]{1,0:T(8,128)S(1)}, f32[128,256]{1,0:T(8,128)S(1)}, u32[]{:S(2)}, u32[]{:S(2)}) collective-permute-start(f32[128,256]{1,0:T(8,128)S(1)} %add.1._.refs_0_), channel_id=1, source_target_pairs={{0,3},{1,0},{2,1},{3,2},{4,7},{5,4},{6,5},{7,6},{8,11},{9,8},{10,9... | collective-permute-start | bytes 393224 | tf_op jit(solution)/shard_map/ppermute | solution.py:531
  89.6 7.2 %collective-permute-start.20 = (f32[128,256]{1,0:T(8,128)S(1)}, f32[128,256]{1,0:T(8,128)S(1)}, u32[]{:S(2)}, u32[]{:S(2)}) collective-permute-start(f32[128,256]{1,0:T(8,128)S(1)} %add.1._.refs_0_), channel_id=1, source_target_pairs={{0,2},{1,3},{2,0},{3,1},{4,6},{5,7},{6,4},{7,5},{8,10},{9,11},{10,... | collective-permute-start | bytes 393224 | tf_op jit(solution)/shard_map/ppermute | solution.py:531
  90.3 8.2 %collective-permute-start.19 = (f32[128,256]{1,0:T(8,128)S(1)}, f32[128,256]{1,0:T(8,128)S(1)}, u32[]{:S(2)}, u32[]{:S(2)}) collective-permute-start(f32[128,256]{1,0:T(8,128)S(1)} %add.1._.refs_0_), channel_id=1, source_target_pairs={{0,1},{1,2},{2,3},{3,0},{4,5},{5,6},{6,7},{7,4},{8,9},{9,10},{10,1... | collective-permute-start | bytes 393224 | tf_op jit(solution)/shard_map/ppermute | solution.py:531
where the time goes:
time: 99.4 us; the launch traced here: 99.3 us
  starting transfers between devices  33.2 us (33%)
  waiting for transfers between devices  33.1 us (33%)
  Pallas kernels  32.3 us (32%)
    ppermute x16, waiting for transfers between devices, over_ctx(): return lax.ppermute(array, 'ctx', [(i, target(i)) for i in range(64)])  31.1 us
    ppermute x16, starting transfers between devices, over_ctx(): return lax.ppermute(array, 'ctx', [(i, target(i)) for i in range(64)])  24.9 us
    pallas_call x2, Pallas kernels, value_call(): pl.pallas_call(functools.partial(value_body, way), grid=(2,), in_specs=[s...  9.36 us
    pallas_call x2, Pallas kernels, intra(): pl.pallas_call(intra_body, grid=(1,), in_specs=[by_head, by_head, flat, f...  8.88 us
    pallas_call x2, Pallas kernels, summary(): pl.pallas_call(functools.partial(summary_body, reverse), grid=(2,), in_sp...  8.39 us
    ppermute x6, starting transfers between devices, over_tp(): return lax.ppermute(array, 'tp', [(i, (i + k) % 4) for i in range(4)])  8.3 us
    pallas_call x11, Pallas kernels, small(): pl.pallas_call(with_after, in_specs=[pl.BlockSpec(memory_space=pltpu.VMEM...  5.64 us
  transfers between devices with their start and end apart: 22, of which 15 were waited for; matrix products, arithmetic and copies ran while one was open for 0% of the time, Pallas kernels for 25%

commit v1 on v0

v1 whole, which is shorter than its diff:
```python
import functools

import jax
import jax.numpy as jnp
from jax import lax
from jax.experimental import pallas as pl
from jax.experimental.pallas import tpu as pltpu
from jax.sharding import PartitionSpec as P

SPAN = 256
HEADS = 16
HALF = 8
WIDTH = 128
CHIPS = 4
QUAD = 4
LOG_ROWS = 8
f32 = jnp.float32
bf16 = jnp.bfloat16
TALL = 2 * WIDTH + LOG_ROWS
anywhere = pl.BlockSpec(memory_space=pl.ANY)


def params():
    return pltpu.CompilerParams(vmem_limit_bytes=24 * 1024 * 1024)


def place():
    position = lax.axis_index("ctx")
    return position % 2, position // 2 % 4, position // 8


def dot(a, b, dims):
    return lax.dot_general(a, b, (dims, ((), ())), preferred_element_type=f32)


def split_two(a):
    high = a.astype(bf16)
    return high, (a - high.astype(f32)).astype(bf16)


def split_three(a):
    high = a.astype(bf16)
    rest = a - high.astype(f32)
    middle = rest.astype(bf16)
    return high, middle, (rest - middle.astype(f32)).astype(bf16)


def triangle(strict):
    row = lax.broadcasted_iota(jnp.int32, (SPAN, SPAN), 0)
    column = lax.broadcasted_iota(jnp.int32, (SPAN, SPAN), 1)
    kept = column < row if strict else column <= row
    return jnp.where(kept, 1.0, 0.0).astype(bf16)


def running_sum(rows, strict):
    tri = triangle(strict)
    return sum(dot(part, tri, ((1,), (1,))) for part in split_three(rows))


def kept_half():
    core, _, depth = place()
    return jnp.bitwise_xor(core, depth % 2)


def summary_body(reverse, *refs):
    if reverse:
        here, proj, rows_all, heads_out, send, keep, middle, total = refs
        order = (1, 0)
    else:
        values, proj_far, log_rows, heads_out, send, keep, middle, levels_out, rows_all, here, proj, logs, total, arrived = refs
        order = (0, 1)
        copies = [
            pltpu.make_async_copy(log_rows, logs, arrived.at[0]),
            pltpu.make_async_copy(proj_far, proj, arrived.at[1]),
        ]
        copies += [
            pltpu.make_async_copy(values.at[pl.ds(span * SPAN, SPAN)], here.at[span], arrived.at[2 + span])
            for span in order
        ]
        for copy in copies:
            copy.start()
        copies[0].wait()
        for span in order:
            tokens = slice(span * SPAN, span * SPAN + SPAN)
            level_rows = running_sum(logs[:, tokens], False)
            levels_out[tokens, :] = jnp.transpose(level_rows)
            rows_all[:, tokens] = level_rows
        copies[1].wait()
    last = [rows_all[:, SPAN * span + SPAN - 1 : SPAN * span + SPAN] for span in (0, 1)]
    carried = jnp.exp(last[order[1]])
    all_log = last[0] + last[1]
    for span in order:
        tokens = slice(span * SPAN, span * SPAN + SPAN)
        level_rows = rows_all[:, tokens]
        weight = jnp.exp(level_rows) if reverse else jnp.exp(last[span] - level_rows)
        proj_t = jnp.transpose(proj[tokens, :]).astype(f32)
        if reverse:
            swapped = jnp.swapaxes(here[tokens], 0, 1)
        else:
            copies[2 + span].wait()
            swapped = jnp.swapaxes(here[span], 0, 1)
        heads_out[:, tokens, :] = swapped
        for head in range(HEADS):
            weighted = jnp.concatenate(split_two(proj_t * weight[head : head + 1, :]), axis=0)
            both = dot(weighted, swapped[head], ((1,), (0,)))
            fresh = both[:WIDTH] + both[WIDTH:]
            if span == order[0]:
                middle[head] = fresh
            else:
                total[head] = fresh + carried[head : head + 1, :] * middle[head]
    kept = kept_half()
    for value in (0, 1):

        @pl.when(kept == value)
        def _():
            for out, half in ((keep, value), (send, 1 - value)):
                for at in range(HALF):
                    head = half * HALF + at
                    out[at, :WIDTH, :] = total[head]
                    if not reverse:
                        out[at, WIDTH:, :] = jnp.broadcast_to(all_log[head : head + 1, :], (LOG_ROWS, WIDTH))


def summary(reverse, values, proj, row_values):
    tokens = values.shape[0]
    rows = WIDTH if reverse else WIDTH + LOG_ROWS
    shapes = [
        jax.ShapeDtypeStruct((HEADS, tokens, WIDTH), bf16),
        jax.ShapeDtypeStruct((HALF, rows, WIDTH), f32),
        jax.ShapeDtypeStruct((HALF, rows, WIDTH), f32),
        jax.ShapeDtypeStruct((HEADS, WIDTH, WIDTH), f32),
    ]
    scratch = [pltpu.VMEM((HEADS, WIDTH, WIDTH), f32)]
    arrays = [values, proj, row_values]
    if not reverse:
        shapes += [
            jax.ShapeDtypeStruct((tokens, HEADS), f32),
            jax.ShapeDtypeStruct((HEADS, tokens), f32),
        ]
        scratch = [
            pltpu.VMEM((2, SPAN, HEADS, WIDTH), bf16),
            pltpu.VMEM((tokens, WIDTH), bf16),
            pltpu.VMEM((HEADS, tokens), f32),
            *scratch,
            pltpu.SemaphoreType.DMA((4,)),
        ]
        arrays = [pltpu.with_memory_space_constraint(array, pltpu.HBM) for array in arrays]
    return pl.pallas_call(
        functools.partial(summary_body, reverse),
        in_specs=[pl.BlockSpec(memory_space=pltpu.VMEM) if reverse else anywhere] * 3,
        out_shape=shapes,
        scratch_shapes=scratch,
        compiler_params=params(),
        name="summary_b" if reverse else "summary_f",
    )(*arrays)


def line_sums(product, head):
    row = lax.broadcasted_iota(jnp.int32, (2 * WIDTH, WIDTH), 1)
    picked = jnp.where(row == head, 1.0, 0.0).astype(bf16)
    return dot(jnp.concatenate(split_two(product), axis=1), picked, ((1,), (0,)))


def intra_body(x_ref, dy_ref, b_ref, c_ref, lev_ref, lev_rows_ref, gain_ref, *refs):
    y_out, dx_out, x_t_out, dy_t_out, cross_out, grads_out = refs[-6:]
    b = b_ref[...]
    c = c_ref[...]
    low, high = slice(0, 128), slice(128, 256)
    blocks = ((low, low), (high, low), (high, high))
    scores = [dot(c[t], b[s], ((1,), (1,))) for t, s in blocks]
    row = lax.broadcasted_iota(jnp.int32, (128, 128), 0)
    column = lax.broadcasted_iota(jnp.int32, (128, 128), 1)
    causal = column <= row
    score_grad = [jnp.zeros((128, 128), f32) for _ in blocks]
    cross = jnp.zeros((SPAN, WIDTH), f32)
    for head in range(HEADS):
        x = x_ref[head]
        dy = dy_ref[head]
        gain = gain_ref[:, head : head + 1]
        level = lev_ref[:, head : head + 1]
        level_row = lev_rows_ref[head : head + 1, :]
        mixing = []
        for at, (t, s) in enumerate(blocks):
            distance = level[t] - level_row[:, s]
            if t == s:
                distance = jnp.where(causal, distance, -1e30)
            decay = jnp.exp(distance)
            mixing.append((scores[at] * decay).astype(bf16))
            score_grad[at] = score_grad[at] + decay * dot(dy[t], x[s], ((1,), (1,)))
        lower = jnp.concatenate(mixing[1:], axis=1)
        left = jnp.concatenate(mixing[:2], axis=0)
        y = jnp.concatenate([dot(mixing[0], x[low], ((1,), (0,))), dot(lower, x, ((1,), (0,)))], axis=0)
        dx = jnp.concatenate([dot(left, dy, ((0,), (0,))), dot(mixing[2], dy[high], ((0,), (0,)))], axis=0)
        x32 = x.astype(f32)
        dy32 = dy.astype(f32)
        cross = cross + line_sums(y * dy32 - dx * x32, head)
        x_t_out[head] = jnp.transpose(x)
        dy_t_out[head] = jnp.transpose(dy)
        y_out[head] = y + gain * x32
        dx_out[head] = dx + gain * dy32
    cross_out[...] = cross[:, :HEADS]
    g00, g10, g11 = [split_two(g) for g in score_grad]
    grad_c0 = sum(dot(g, b[low], ((1,), (0,))) for g in g00)
    grad_c1 = sum(dot(g, b[low], ((1,), (0,))) for g in g10) + sum(dot(g, b[high], ((1,), (0,))) for g in g11)
    grad_b0 = sum(dot(g, c[low], ((0,), (0,))) for g in g00) + sum(dot(g, c[high], ((0,), (0,))) for g in g10)
    grad_b1 = sum(dot(g, c[high], ((0,), (0,))) for g in g11)
    grads_out[:WIDTH, low] = jnp.transpose(grad_c0)
    grads_out[:WIDTH, high] = jnp.transpose(grad_c1)
    grads_out[WIDTH:, low] = jnp.transpose(grad_b0)
    grads_out[WIDTH:, high] = jnp.transpose(grad_b1)


def intra(span, x_heads, dy_heads, b_proj, c_proj, levels, level_rows, gain, after, so_far=()):
    tokens = x_heads.shape[1]
    by_head = pl.BlockSpec((HEADS, SPAN, WIDTH), lambda s: (0, span, 0))
    flat = pl.BlockSpec((SPAN, WIDTH), lambda s: (span, 0))
    thin = pl.BlockSpec((SPAN, HEADS), lambda s: (span, 0))
    turned = pl.BlockSpec((HEADS, WIDTH, SPAN), lambda s: (0, 0, span))
    turned_shape = jax.ShapeDtypeStruct((HEADS, WIDTH, tokens), bf16)
    return pl.pallas_call(
        intra_body,
        grid=(1,),
        in_specs=[
            by_head,
            by_head,
            flat,
            flat,
            thin,
            pl.BlockSpec((HEADS, SPAN), lambda s: (0, span)),
            pl.BlockSpec((1, HEADS), lambda s: (0, 0)),
            anywhere,
        ]
        + [anywhere] * len(so_far),
        out_specs=[by_head, by_head, turned, turned, thin, pl.BlockSpec((2 * WIDTH, SPAN), lambda s: (0, span))],
        out_shape=[
            jax.ShapeDtypeStruct((HEADS, tokens, WIDTH), f32),
            jax.ShapeDtypeStruct((HEADS, tokens, WIDTH), f32),
            turned_shape,
            turned_shape,
            jax.ShapeDtypeStruct((tokens, HEADS), f32),
            jax.ShapeDtypeStruct((2 * WIDTH, tokens), f32),
        ],
        input_output_aliases={8 + at: at for at in range(len(so_far))},
        compiler_params=params(),
        name="intra%d" % span,
    )(x_heads, dy_heads, b_proj, c_proj, levels, level_rows, gain, after, *so_far)


def small(body, outs, name, *args, scratch=(), after=()):
    count = len(args)

    def with_after(*refs):
        body(*refs[:count], *refs[count + len(after) :])

    return pl.pallas_call(
        with_after,
        in_specs=[pl.BlockSpec(memory_space=pltpu.VMEM)] * count + [anywhere] * len(after),
        out_shape=[jax.ShapeDtypeStruct(shape, f32) for shape in outs],
        scratch_shapes=[pltpu.VMEM(shape, f32) for shape in scratch],
        compiler_params=params(),
        name=name,
    )(*args, *after)


FORWARD = slice(0, WIDTH)
BACKWARD = slice(WIDTH, 2 * WIDTH)
LOGS = slice(2 * WIDTH, TALL)


def core_up_body(keep_f, other_f, keep_b, other_b, *outs):
    core, chip, _ = place()
    first = core == 0
    for k in range(CHIPS):
        for at in range(2):
            head = jnp.bitwise_xor(chip, k) * 2 + at
            own_log = keep_f[head, WIDTH:, :]
            other_log = other_f[head, WIDTH:, :]
            own_decay = jnp.exp(own_log)[:1]
            other_decay = jnp.exp(other_log)[:1]
            own_forward = jnp.where(first, other_decay, 1.0)
            other_forward = jnp.where(first, 1.0, own_decay)
            own_backward = jnp.where(first, 1.0, other_decay)
            other_backward = jnp.where(first, own_decay, 1.0)
            outs[k][at, FORWARD, :] = own_forward * keep_f[head, :WIDTH, :] + other_forward * other_f[head, :WIDTH, :]
            outs[k][at, BACKWARD, :] = own_backward * keep_b[head] + other_backward * other_b[head]
            outs[k][at, LOGS, :] = own_log + other_log


def chain(places, decays, states, entering):
    befores = {}
    for at in places:
        befores[at] = entering
        entering = decays[at] * entering + states(at)
    return befores, entering


TAKEN = (2, 1, 3, 0)


def taken(parts):
    return [parts[k] for k in TAKEN]


def untaken(parts):
    return [parts[TAKEN.index(k)] for k in range(4)]


def slab_up_body(*refs):
    parts, out, ordered = untaken(refs[:4]), refs[4], refs[5]
    _, chip, _ = place()
    zero = jnp.zeros((WIDTH, WIDTH), f32)
    for k in range(CHIPS):
        ordered[jnp.bitwise_xor(chip, k)] = parts[k][...]
    for head in range(2):
        logs = [ordered[at, head, LOGS, :] for at in range(CHIPS)]
        decays = [jnp.exp(log)[:1] for log in logs]
        out[head, FORWARD, :] = chain(range(4), decays, lambda at: ordered[at, head, FORWARD, :], zero)[1]
        out[head, BACKWARD, :] = chain(range(3, -1, -1), decays, lambda at: ordered[at, head, BACKWARD, :], zero)[1]
        out[head, LOGS, :] = sum(logs)


def in_slab_order(own, other):
    kept = kept_half()
    return jnp.where(kept == 0, own, other), jnp.where(kept == 0, other, own)


def block_up_body(own, other, both, single):
    core, _, depth = place()
    block = depth // 2
    near = jnp.bitwise_xor(block, jnp.where(core == 0, 1, 3))
    far = jnp.bitwise_xor(block, 2)
    for head in range(2):
        log0, log1 = in_slab_order(own[head, LOGS, :], other[head, LOGS, :])
        ahead0, ahead1 = in_slab_order(own[head, FORWARD, :], other[head, FORWARD, :])
        behind0, behind1 = in_slab_order(own[head, BACKWARD, :], other[head, BACKWARD, :])
        ahead = jnp.exp(log1)[:1] * ahead0 + ahead1
        behind = behind0 + jnp.exp(log0)[:1] * behind1
        both[head, :WIDTH, :] = jnp.where(near > block, ahead, behind)
        both[head, WIDTH:, :] = log0 + log1

        @pl.when(core == head)
        def _():
            single[:WIDTH, :] = jnp.where(far > block, ahead, behind)
            single[WIDTH:, :] = log0 + log1


def chip_down_body(*refs):
    parts, (own, other, single, both, other_single, other_both) = untaken(refs[:4]), refs[4:10]
    outs, ordered, came, entered = refs[10:14], *refs[14:]
    core, chip, depth = place()
    block = depth // 2
    kept = kept_half()
    for k in range(CHIPS):
        ordered[jnp.bitwise_xor(chip, k)] = parts[k][...]
    came[block] = jnp.zeros_like(came[0])
    came[jnp.bitwise_xor(block, jnp.where(core == 0, 1, 3))] = both[...]
    came[jnp.bitwise_xor(block, jnp.where(core == 0, 3, 1))] = other_both[...]
    far = jnp.bitwise_xor(block, 2)
    came[far, core] = single[...]
    came[far, 1 - core] = other_single[...]
    for head in range(2):
        decays = [jnp.exp(ordered[at, head, LOGS, :])[:1] for at in range(CHIPS)]
        for way, rows in ((0, FORWARD), (1, BACKWARD)):
            entering = jnp.zeros((WIDTH, WIDTH), f32)
            for at in range(3, -1, -1) if way else range(4):
                counts = at > block if way else at < block
                passed = jnp.exp(came[at, head, WIDTH:, :])[:1] * entering + came[at, head, :WIDTH, :]
                entering = jnp.where(counts, passed, entering)
            crossed = jnp.exp(other[head, LOGS, :])[:1] * entering + other[head, rows, :]
            entering = jnp.where(kept == 1 - way, crossed, entering)
            places = range(3, -1, -1) if way else range(4)
            befores, _ = chain(places, decays, lambda at: ordered[at, head, rows, :], entering)
            for at, before in befores.items():
                entered[at, head, rows, :] = before
    for k in range(CHIPS):
        outs[k][...] = entered[jnp.bitwise_xor(chip, k)]


def core_down_body(keep_f, other_f, keep_b, other_b, *refs):
    pieces, mine, theirs = untaken(refs[:4]), refs[4], refs[5]
    core, chip, _ = place()
    first = core == 0
    for k in range(CHIPS):
        for at in range(2):
            head = jnp.bitwise_xor(chip, k) * 2 + at
            forward = pieces[k][at, FORWARD, :]
            backward = pieces[k][at, BACKWARD, :]
            own_decay = jnp.exp(keep_f[head, WIDTH:, :])[:1]
            other_decay = jnp.exp(other_f[head, WIDTH:, :])[:1]
            mine[head, FORWARD, :] = jnp.where(first, forward, other_decay * forward + other_f[head, :WIDTH, :])
            mine[head, BACKWARD, :] = jnp.where(first, other_decay * backward + other_b[head], backward)
            theirs[head, FORWARD, :] = jnp.where(first, own_decay * forward + keep_f[head, :WIDTH, :], forward)
            theirs[head, BACKWARD, :] = jnp.where(first, backward, own_decay * backward + keep_b[head])


def over_ctx(array, target):
    return lax.ppermute(array, "ctx", [(i, target(i)) for i in range(64)])


def swap_cores(array):
    return over_ctx(array, lambda i: i ^ 1)


def along_chips(array, k):
    return over_ctx(array, lambda i: i ^ 2 * k ^ (8 if i % 2 else 0))


def to_near_blocks(array):
    return over_ctx(array, lambda i: i ^ (48 if i % 2 else 16))


def to_far_block(array):
    return over_ctx(array, lambda i: i ^ 32)


def spread(parts, move):
    return [parts[0]] + [move(parts[k], k) for k in range(1, len(parts))]


def half_of(own, array):
    half = kept_half() if own else 1 - kept_half()
    return jnp.where(half == 0, array[:HALF], array[HALF:])


def grad_body(own, states, middle_f, middle_b, level_rows, x_turned, dy_turned, base, *refs):
    half = kept_half() if own else 1 - kept_half()
    for span in range(2):
        lanes = slice(span * SPAN, span * SPAN + SPAN)
        rows = half_of(own, level_rows[:, lanes])
        for way, middle, values in ((0, middle_f, dy_turned), (1, middle_b, x_turned)):
            weight = jnp.exp(rows[:, SPAN - 1 : SPAN] - rows) if way else jnp.exp(rows)
            last = 2 * SPAN - 1 if way else SPAN - 1
            crossed = half_of(own, jnp.exp(level_rows[:, last : last + 1]))
            of_way = slice(way * WIDTH, way * WIDTH + WIDTH)
            acc = base[of_way, lanes]
            for at in range(HALF):
                head = half * HALF + at
                state = states[at, of_way, :]
                if span == 1 - way:
                    state = crossed[at : at + 1, :] * state + middle[head]
                value = values[head, :, lanes]
                line = dot(
                    jnp.concatenate(split_two(state), axis=1),
                    jnp.concatenate([value, value], axis=0),
                    ((1,), (0,)),
                )
                acc = acc + weight[at : at + 1, :] * line
            if own:
                refs[0][of_way, lanes] = acc
            else:
                refs[4][lanes, of_way] = jnp.transpose(acc)
    if not own:
        mine_tp = lax.axis_index("tp")
        for k in range(4):
            start = pl.multiple_of(jnp.bitwise_xor(mine_tp, k) * 128, 128)
            refs[k][...] = refs[4][pl.ds(start, 128), :]


def grad_call(own, states, middle_f, middle_b, level_rows, x_turned, dy_turned, base):
    tokens = base.shape[1]
    outs = [base.shape] if own else [(tokens // 4, 2 * WIDTH)] * 4
    return small(
        functools.partial(grad_body, own),
        outs,
        "grads_own" if own else "grads_other",
        states,
        middle_f,
        middle_b,
        level_rows,
        x_turned,
        dy_turned,
        base,
        scratch=[] if own else [(tokens, 2 * WIDTH)],
    )


def value_body(way, got, mine, middle, levels, proj, part, values, _, out, cross_out, wide, turned, left):
    kept = kept_half()
    states = slice(way * WIDTH, way * WIDTH + WIDTH)
    last = 2 * SPAN - 1 if way else SPAN - 1
    crossed = jnp.exp(levels[last : last + 1, :])
    copies = []
    for span in range(2):
        tokens = slice(span * SPAN, span * SPAN + SPAN)
        level = levels[tokens, :]
        weight = jnp.exp(level[SPAN - 1 : SPAN, :] - level) if way else jnp.exp(level)
        doubled = jnp.concatenate([proj[tokens, :], proj[tokens, :]], axis=1)
        cross = jnp.zeros((SPAN, WIDTH), f32)
        for head in range(HEADS):
            at = head % HALF
            state = jnp.where(head // HALF == kept, mine[at, states, :], got[at, states, :])
            if span == 1 - way:
                state = crossed[:, head : head + 1] * state + middle[head]
            far = dot(doubled, jnp.concatenate(split_two(state), axis=0), ((1,), (0,)))
            far = far * weight[:, head : head + 1]
            cross = cross + line_sums(far * values[head, tokens, :].astype(f32), head)
            wide[span, head] = (part[head, tokens, :] + far).astype(bf16)
        cross_out[tokens, :] = cross[:, :HEADS]
        turned[span] = jnp.swapaxes(wide[span], 0, 1)
        copies.append(pltpu.make_async_copy(turned.at[span], out.at[pl.ds(span * SPAN, SPAN)], left.at[span]))
        copies[-1].start()
    for copy in copies:
        copy.wait()


def value_call(way, got, mine, middle, levels, proj, part, values, after):
    tokens = levels.shape[0]
    return pl.pallas_call(
        functools.partial(value_body, way),
        in_specs=[pl.BlockSpec(memory_space=pltpu.VMEM)] * 7 + [anywhere],
        out_specs=[anywhere, pl.BlockSpec(memory_space=pltpu.VMEM)],
        out_shape=[
            jax.ShapeDtypeStruct((tokens, HEADS, WIDTH), bf16),
            jax.ShapeDtypeStruct((tokens, HEADS), f32),
        ],
        scratch_shapes=[
            pltpu.VMEM((2, HEADS, SPAN, WIDTH), bf16),
            pltpu.VMEM((2, SPAN, HEADS, WIDTH), bf16),
            pltpu.SemaphoreType.DMA((2,)),
        ],
        compiler_params=params(),
        name="values_b" if way else "values_f",
    )(got, mine, middle, levels, proj, part, values, after)


def decay_body(near, forward, backward, got, mine, send_b, keep_b, level_rows, out, done):
    kept = kept_half()
    sublane = lax.broadcasted_iota(jnp.int32, (HEADS, 1), 0)
    start = jnp.zeros((HEADS, 1), f32)
    all_log = level_rows[:, SPAN - 1 : SPAN] + level_rows[:, 2 * SPAN - 1 : 2 * SPAN]
    for head in range(HEADS):
        at = head % HALF
        own = head // HALF == kept
        incoming = jnp.where(own, mine[at], got[at])
        local = jnp.where(own, keep_b[at], send_b[at])
        pulled = local + jnp.exp(all_log[head : head + 1, :]) * incoming[WIDTH:]
        line = jnp.sum(jnp.sum(incoming[:WIDTH] * pulled, axis=0, keepdims=True), axis=1, keepdims=True)
        start = jnp.where(sublane == head, line, start)
    for span in range(2):
        rows = slice(span * SPAN, span * SPAN + SPAN)
        cross = jnp.transpose(near[rows, :] + forward[rows, :] - backward[rows, :])
        out[:, rows] = start - running_sum(cross, True)
        start = start - jnp.sum(cross, axis=1, keepdims=True)
    done[...] = jnp.zeros_like(done)


def over_tp(array, k):
    return lax.ppermute(array, "tp", [(i, i ^ k) for i in range(4)])


def add_body(p2, p1, p3, p0, out):
    out[...] = p0[...] + p1[...] + p2[...] + p3[...]


def join_body(p2, p1, p3, p0, c_out, b_out):
    mine = lax.axis_index("tp")
    for k, piece in enumerate((p0, p1, p2, p3)):
        rows = pl.ds(pl.multiple_of(jnp.bitwise_xor(mine, k) * 128, 128), 128)
        c_out[rows, :] = piece[:, :WIDTH]
        b_out[rows, :] = piece[:, WIDTH:]


def on_device(inputs, b_proj, c_proj, logdecay, skip_gain, grad_out):
    tokens = inputs.shape[0]
    log_rows = logdecay.T
    gain = skip_gain.reshape(1, HEADS)
    x_heads, send_f, keep_f, middle_f, levels, level_rows = summary(False, inputs, b_proj, log_rows)
    other_f = swap_cores(send_f)
    dy_heads, send_b, keep_b, middle_b = summary(True, grad_out, c_proj, level_rows)
    other_b = swap_cores(send_b)

    cores = (keep_f, other_f, keep_b, other_b)
    packed = (2, TALL, WIDTH)
    chips = small(core_up_body, [packed] * CHIPS, "core_up", *cores)
    local = (x_heads, dy_heads, b_proj, c_proj, levels, level_rows, gain)
    first = intra(0, *local, chips[0])
    chips = [along_chips(chips[k], k) for k in range(CHIPS)]
    (slab,) = small(slab_up_body, [packed], "slab_up", *taken(chips), scratch=[(CHIPS,) + packed], after=[first[-1]])
    other_slab = swap_cores(slab)
    unit = (WIDTH + LOG_ROWS, WIDTH)
    both, single = small(block_up_body, [(2,) + unit, unit], "block_up", slab, other_slab)
    single = to_far_block(single)
    both = to_near_blocks(both)
    entering = small(
        chip_down_body,
        [(2, 2 * WIDTH, WIDTH)] * CHIPS,
        "chip_down",
        *taken(chips),
        slab,
        other_slab,
        single,
        both,
        swap_cores(single),
        swap_cores(both),
        scratch=[(CHIPS,) + packed, (4, 2) + unit, (CHIPS, 2, 2 * WIDTH, WIDTH)],
    )
    y_part, dx_part, x_turned, dy_turned, near, base = intra(1, *local, entering[0], first)
    entering = [along_chips(entering[k], k) for k in range(CHIPS)]
    mine, theirs = small(
        core_down_body, [(HALF, 2 * WIDTH, WIDTH)] * 2, "core_down", *cores, *taken(entering), after=[base]
    )
    got = swap_cores(theirs)

    (base,) = grad_call(True, mine, middle_f, middle_b, level_rows, x_turned, dy_turned, base)
    pieces = grad_call(False, got, middle_f, middle_b, level_rows, x_turned, dy_turned, base)
    outputs, cross_f = value_call(0, got, mine, middle_f, levels, c_proj, y_part, dy_heads, pieces[0])
    pieces = spread(pieces, over_tp)
    (summed,) = small(add_body, [pieces[0].shape], "add", *taken(pieces), after=[cross_f])
    grad_inputs, cross_b = value_call(1, got, mine, middle_b, levels, b_proj, dx_part, x_heads, summed)
    decays, done = small(
        decay_body,
        [(HEADS, tokens), (8, WIDTH)],
        "decay",
        near,
        cross_f,
        cross_b,
        got,
        mine,
        send_b,
        keep_b,
        level_rows,
    )
    joined = spread([summed] * 4, over_tp)
    grad_c, grad_b = small(join_body, [(tokens, WIDTH)] * 2, "join", *taken(joined), after=[done])
    return outputs, grad_inputs, decays.T, grad_b, grad_c


def solution(mesh):
    placed = (
        P("ctx", "tp", None),
        P("ctx", None),
        P("ctx", None),
        P("ctx", "tp"),
        P("tp"),
        P("ctx", "tp", None),
    )
    return jax.shard_map(
        on_device,
        mesh=mesh,
        in_specs=placed,
        out_specs=(
            P("ctx", "tp", None),
            P("ctx", "tp", None),
            P("ctx", "tp"),
            P("ctx", None),
            P("ctx", None),
        ),
        check_vma=False,
    )
```

time: 99.4 us -> 89.3 us (0.90)
  waiting for transfers between devices: 33.1 us -> 24.2 us
  Pallas kernels: 32.3 us -> 29.6 us
  starting transfers between devices: 33.2 us -> 34.2 us
    ppermute x16, waiting for transfers between devices: 31.1 us -> 23 us  [over_ctx(): return lax.ppermute(array, 'ctx', [(i, target(i)) for i in range(64)])]
    pallas_call x4, Pallas kernels: 17.8 us -> 15.1 us  [the longest x2 9.43 us: value_call(): pl.pallas_call(functools.partial(value_body, way), in_specs=[pl.BlockSpec...]
    ppermute x16, starting transfers between devices: 24.9 us -> 26.2 us  [over_ctx(): return lax.ppermute(array, 'ctx', [(i, target(i)) for i in range(64)])]
    pallas_call x11 -> x10, Pallas kernels: 5.64 us -> 5.6 us  [small(): pl.pallas_call(with_after, in_specs=[pl.BlockSpec(memory_space=pltpu.VMEM...]
  transfers between devices with their start and end apart: 22 -> 22, of which waited for: 15 -> 11; matrix products, arithmetic and copies ran while one was open for 0% -> 0% of each run, Pallas kernels for 25% -> 26%
where the time goes in v1:
time: 89.3 us; the launch traced here: 89 us
  starting transfers between devices  34.2 us (38%)
  Pallas kernels  29.6 us (33%)
  waiting for transfers between devices  24.2 us (27%)
    ppermute x16, starting transfers between devices, over_ctx(): return lax.ppermute(array, 'ctx', [(i, target(i)) for i in range(64)])  26.2 us
    ppermute x16, waiting for transfers between devices, over_ctx(): return lax.ppermute(array, 'ctx', [(i, target(i)) for i in range(64)])  23 us
    pallas_call x2, Pallas kernels, value_call(): pl.pallas_call(functools.partial(value_body, way), in_specs=[pl.BlockSpec...  9.43 us
    pallas_call x2, Pallas kernels, intra(): pl.pallas_call(intra_body, grid=(1,), in_specs=[by_head, by_head, flat, f...  8.9 us
    ppermute x6, starting transfers between devices, over_tp(): return lax.ppermute(array, 'tp', [(i, i ^ k) for i in range(4)])  8 us
    pallas_call x2, Pallas kernels, summary(): pl.pallas_call(functools.partial(summary_body, reverse), in_specs=[pl.Blo...  5.71 us
    pallas_call x10, Pallas kernels, small(): pl.pallas_call(with_after, in_specs=[pl.BlockSpec(memory_space=pltpu.VMEM...  5.6 us
  transfers between devices with their start and end apart: 22, of which 11 were waited for; matrix products, arithmetic and copies ran while one was open for 0% of the time, Pallas kernels for 26%

profile of v1, /device:TPU:1, one launch (start us, length us, event | category | flops | bytes accessed | tf_op | source)
XLA Modules:
  0.0 89.0 jit_solution(3098913722600268083)
XLA Ops:
  0.7 3.7 %summary_f.1 = (bf16[16,512,128]{2,1,0:T(8,128)(2,1)S(1)}, f32[8,136,128]{2,1,0:T(8,128)S(1)}, f32[8,136,128]{2,1,0:T(8,128)S(1)}, f32[16,128,128]{2,1,0:T(8,128...) custom-call(bf16[512,16,128]{2,1,0:T(8,128)(2,1)} %refs_0_.2, bf16[512,128]{1,0:T(8,128)(2,1)} %proj.3, f32[16,512]{1,0:T(8,128)} %bitcast.5), custom_call_target="tpu_custom_call" | custom-call | tf_op jit(solution)/shard_map/summary_f/pallas_call | solution.py:148
  4.3 3.3 %collective-permute-start = (f32[8,136,128]{2,1,0:T(8,128)S(1)}, f32[8,136,128]{2,1,0:T(8,128)S(1)}, u32[]{:S(2)}, u32[]{:S(2)}) collective-permute-start(f32[8,136,128]{2,1,0:T(8,128)S(1)} %get-tuple-element.52), channel_id=1, source_target_pairs={{0,4},{4,0},{8,12},{12,8},{16,20},{20,16},{24,28},{28,24},{32,36},... | collective-permute-start | bytes 1671176 | tf_op jit(solution)/shard_map/ppermute | solution.py:397
  7.7 2.0 %summary_b.1 = (bf16[16,512,128]{2,1,0:T(8,128)(2,1)S(1)}, f32[8,128,128]{2,1,0:T(8,128)S(1)}, f32[8,128,128]{2,1,0:T(8,128)S(1)}, f32[16,128,128]{2,1,0:T(8,128)S(1)}) custom-call(bf16[512,16,128]{2,1,0:T(8,128)(2,1)S(1)} %copy-done.2, bf16[512,128]{1,0:T(8,128)(2,1)S(1)} %copy-done, f32[16,512]{1,0:T(8,128)S(1)} %get-tuple-element.53.refs_2_.lev_rows_ref.refs_3_.refs_7_), custom_call_target="tpu_custom_call" | custom-call | tf_op jit(solution)/shard_map/summary_b/pallas_call | solution.py:148
  9.8 1.9 %collective-permute-done.1.refs_3_ = f32[8,128,128]{2,1,0:T(8,128)S(1)} collective-permute-done((f32[8,128,128]{2,1,0:T(8,128)S(1)}, f32[8,128,128]{2,1,0:T(8,128)S(1)}, u32[]{:S(2)}, u32[]{:S(2)}) %collective-permute-start.1) | collective-permute-done | bytes 524320 | tf_op jit(solution)/shard_map/ppermute | solution.py:397
  11.9 2.4 %collective-permute-start.2 = (f32[2,264,128]{2,1,0:T(8,128)S(1)}, f32[2,264,128]{2,1,0:T(8,128)S(1)}, u32[]{:S(2)}, u32[]{:S(2)}) collective-permute-start(f32[2,264,128]{2,1,0:T(8,128)S(1)} %get-tuple-element.56), channel_id=1, source_target_pairs={{0,16},{4,52},{8,24},{12,60},{16,0},{20,36},{24,8},{28,44},{32,48}... | collective-permute-start | bytes 811016 | tf_op jit(solution)/shard_map/ppermute | solution.py:397
  14.3 1.4 %collective-permute-start.4 = (f32[2,264,128]{2,1,0:T(8,128)S(1)}, f32[2,264,128]{2,1,0:T(8,128)S(1)}, u32[]{:S(2)}, u32[]{:S(2)}) collective-permute-start(f32[2,264,128]{2,1,0:T(8,128)S(1)} %get-tuple-element.58), channel_id=1, source_target_pairs={{0,24},{4,60},{8,16},{12,52},{16,8},{20,44},{24,0},{28,36},{32,56}... | collective-permute-start | bytes 811016 | tf_op jit(solution)/shard_map/ppermute | solution.py:397
  15.7 3.5 %collective-permute-start.5 = (f32[2,264,128]{2,1,0:T(8,128)S(1)}, f32[2,264,128]{2,1,0:T(8,128)S(1)}, u32[]{:S(2)}, u32[]{:S(2)}) collective-permute-start(f32[2,264,128]{2,1,0:T(8,128)S(1)} %get-tuple-element.59.refs_0_), channel_id=1, source_target_pairs={{0,0},{4,36},{8,8},{12,44},{16,16},{20,52},{24,24},{28,60},{32,32}... | collective-permute-start | bytes 811016 | tf_op jit(solution)/shard_map/ppermute | solution.py:397
  19.2 4.5 %intra0.1 = (f32[16,512,128]{2,1,0:T(8,128)S(1)}, f32[16,512,128]{2,1,0:T(8,128)S(1)}, bf16[16,128,512]{2,1,0:T(8,128)(2,1)S(1)}, bf16[16,128,512]{2,1,0:T(8,128...) custom-call(bf16[16,512,128]{2,1,0:T(8,128)(2,1)S(1)} %get-tuple-element.60.x_ref.values, ...), custom_call_target="tpu_custom_call" | custom-call | tf_op jit(solution)/shard_map/intra0/pallas_call | solution.py:220
  23.7 2.6 %collective-permute-done.4.refs_2_ = f32[2,264,128]{2,1,0:T(8,128)S(1)} collective-permute-done((f32[2,264,128]{2,1,0:T(8,128)S(1)}, f32[2,264,128]{2,1,0:T(8,128)S(1)}, u32[]{:S(2)}, u32[]{:S(2)}) %collective-permute-start.4) | collective-permute-done | bytes 270368 | tf_op jit(solution)/shard_map/ppermute | solution.py:397
  26.3 2.4 %collective-permute-done.5.refs_3_ = f32[2,264,128]{2,1,0:T(8,128)S(1)} collective-permute-done((f32[2,264,128]{2,1,0:T(8,128)S(1)}, f32[2,264,128]{2,1,0:T(8,128)S(1)}, u32[]{:S(2)}, u32[]{:S(2)}) %collective-permute-start.5) | collective-permute-done | bytes 270368 | tf_op jit(solution)/shard_map/ppermute | solution.py:397
  29.2 1.5 %collective-permute-done.6.refs_1_.refs_5_ = f32[2,264,128]{2,1,0:T(8,128)S(1)} collective-permute-done((f32[2,264,128]{2,1,0:T(8,128)S(1)}, f32[2,264,128]{2,1,0:T(8,128)S(1)}, u32[]{:S(2)}, u32[]{:S(2)}) %collective-permute-start.6) | collective-permute-done | bytes 270368 | tf_op jit(solution)/shard_map/ppermute | solution.py:397
  30.7 6.1 %collective-permute-start.8 = (f32[2,136,128]{2,1,0:T(8,128)S(1)}, f32[2,136,128]{2,1,0:T(8,128)S(1)}, u32[]{:S(2)}, u32[]{:S(2)}) collective-permute-start(f32[2,136,128]{2,1,0:T(8,128)S(1)} %get-tuple-element.65), channel_id=1, source_target_pairs={{0,64},{4,196},{8,72},{12,204},{16,80},{20,212},{24,88},{28,220},{... | collective-permute-start | bytes 417800 | tf_op jit(solution)/shard_map/ppermute | solution.py:397
  36.8 1.0 %collective-permute-start.7 = (f32[136,128]{1,0:T(8,128)S(1)}, f32[136,128]{1,0:T(8,128)S(1)}, u32[]{:S(2)}, u32[]{:S(2)}) collective-permute-start(f32[136,128]{1,0:T(8,128)S(1)} %get-tuple-element.64), channel_id=1, source_target_pairs={{0,128},{4,132},{8,136},{12,140},{16,144},{20,148},{24,152},{28,15... | collective-permute-start | bytes 208904 | tf_op jit(solution)/shard_map/ppermute | solution.py:397
  37.8 4.8 %collective-permute-done.8.refs_7_ = f32[2,136,128]{2,1,0:T(8,128)S(1)} collective-permute-done((f32[2,136,128]{2,1,0:T(8,128)S(1)}, f32[2,136,128]{2,1,0:T(8,128)S(1)}, u32[]{:S(2)}, u32[]{:S(2)}) %collective-permute-start.8) | collective-permute-done | bytes 139296 | tf_op jit(solution)/shard_map/ppermute | solution.py:397
  42.6 2.4 %collective-permute-done.7.refs_6_ = f32[136,128]{1,0:T(8,128)S(1)} collective-permute-done((f32[136,128]{1,0:T(8,128)S(1)}, f32[136,128]{1,0:T(8,128)S(1)}, u32[]{:S(2)}, u32[]{:S(2)}) %collective-permute-start.7) | collective-permute-done | bytes 69664 | tf_op jit(solution)/shard_map/ppermute | solution.py:397
  45.6 0.9 %collective-permute-done.9.refs_8_ = f32[136,128]{1,0:T(8,128)S(1)} collective-permute-done((f32[136,128]{1,0:T(8,128)S(1)}, f32[136,128]{1,0:T(8,128)S(1)}, u32[]{:S(2)}, u32[]{:S(2)}) %collective-permute-start.9) | collective-permute-done | bytes 69664 | tf_op jit(solution)/shard_map/ppermute | solution.py:397
  47.0 1.4 %collective-permute-start.11 = (f32[2,256,128]{2,1,0:T(8,128)S(1)}, f32[2,256,128]{2,1,0:T(8,128)S(1)}, u32[]{:S(2)}, u32[]{:S(2)}) collective-permute-start(f32[2,256,128]{2,1,0:T(8,128)S(1)} %get-tuple-element.66), channel_id=1, source_target_pairs={{0,16},{4,52},{8,24},{12,60},{16,0},{20,36},{24,8},{28,44},{32,48}... | collective-permute-start | bytes 786440 | tf_op jit(solution)/shard_map/ppermute | solution.py:397
  48.4 1.0 %collective-permute-start.12 = (f32[2,256,128]{2,1,0:T(8,128)S(1)}, f32[2,256,128]{2,1,0:T(8,128)S(1)}, u32[]{:S(2)}, u32[]{:S(2)}) collective-permute-start(f32[2,256,128]{2,1,0:T(8,128)S(1)} %get-tuple-element.67), channel_id=1, source_target_pairs={{0,8},{4,44},{8,0},{12,36},{16,24},{20,60},{24,16},{28,52},{32,40}... | collective-permute-start | bytes 786440 | tf_op jit(solution)/shard_map/ppermute | solution.py:397
  49.4 2.0 %collective-permute-start.13 = (f32[2,256,128]{2,1,0:T(8,128)S(1)}, f32[2,256,128]{2,1,0:T(8,128)S(1)}, u32[]{:S(2)}, u32[]{:S(2)}) collective-permute-start(f32[2,256,128]{2,1,0:T(8,128)S(1)} %get-tuple-element.68), channel_id=1, source_target_pairs={{0,24},{4,60},{8,16},{12,52},{16,8},{20,44},{24,0},{28,36},{32,56}... | collective-permute-start | bytes 786440 | tf_op jit(solution)/shard_map/ppermute | solution.py:397
  51.4 2.9 %collective-permute-start.14 = (f32[2,256,128]{2,1,0:T(8,128)S(1)}, f32[2,256,128]{2,1,0:T(8,128)S(1)}, u32[]{:S(2)}, u32[]{:S(2)}) collective-permute-start(f32[2,256,128]{2,1,0:T(8,128)S(1)} %get-tuple-element.69.refs_0_), channel_id=1, source_target_pairs={{0,0},{4,36},{8,8},{12,44},{16,16},{20,52},{24,24},{28,60},{32,32}... | collective-permute-start | bytes 786440 | tf_op jit(solution)/shard_map/ppermute | solution.py:397
  54.3 4.5 %intra1.1 = (f32[16,512,128]{2,1,0:T(8,128)S(1)}, f32[16,512,128]{2,1,0:T(8,128)S(1)}, bf16[16,128,512]{2,1,0:T(8,128)(2,1)S(1)}, bf16[16,128,512]{2,1,0:T(8,128...) custom-call(bf16[16,512,128]{2,1,0:T(8,128)(2,1)S(1)} %get-tuple-ele, ...), custom_call_target="tpu_custom_call", output_to_operand_aliasing={{0}: (8, {}), {1}: (9, {}), {2}: (10, {}), {3}: (11, {}), {... | custom-call | tf_op jit(solution)/shard_map/intra1/pallas_call | solution.py:220
  58.8 4.2 %collective-permute-done.13.refs_6_ = f32[2,256,128]{2,1,0:T(8,128)S(1)} collective-permute-done((f32[2,256,128]{2,1,0:T(8,128)S(1)}, f32[2,256,128]{2,1,0:T(8,128)S(1)}, u32[]{:S(2)}, u32[]{:S(2)}) %collective-permute-start.13) | collective-permute-done | bytes 262176 | tf_op jit(solution)/shard_map/ppermute | solution.py:397
  64.1 0.9 %grads_own.1.refs_6_ = f32[256,512]{1,0:T(8,128)S(1)} custom-call(f32[8,256,128]{2,1,0:T(8,128)S(1)} %get-tuple-element.77.refs_0_.mine.refs_4_, f32[16,128,128]{2,1,0:T(8,128)S(1)} %get-tuple-element.78.refs_1_.middle, f32[16,128,128]{2,1,0:T(8,128)S(1)} %get-tuple-element.80.refs_2_.middle, ...), custom_call_target="tpu_custom_call" | custom-call | tf_op jit(solution)/shard_map/grads_own/pallas_call | solution.py:255
  65.0 1.7 %collective-permute-done.15.refs_0_.got.refs_3_ = f32[8,256,128]{2,1,0:T(8,128)S(1)} collective-permute-done((f32[8,256,128]{2,1,0:T(8,128)S(1)}, f32[8,256,128]{2,1,0:T(8,128)S(1)}, u32[]{:S(2)}, u32[]{:S(2)}) %collective-permute-start.15) | collective-permute-done | bytes 1048608 | tf_op jit(solution)/shard_map/ppermute | solution.py:397
  66.7 1.0 %grads_other.1 = (f32[128,256]{1,0:T(8,128)S(1)}, f32[128,256]{1,0:T(8,128)S(1)}, f32[128,256]{1,0:T(8,128)S(1)}, f32[128,256]{1,0:T(8,128)S(1)}) custom-call(f32[8,256,128]{2,1,0:T(8,128)S(1)} %collective-permute-done.15.refs_0_.got.refs_3_, f32[16,128,128]{2,1,0:T(8,128)S(1)} %get-tuple-element.78.refs_1_.middle, ...), custom_call_target="tpu_custom_call" | custom-call | tf_op jit(solution)/shard_map/grads_other/pallas_call | solution.py:255
  67.8 3.0 %collective-permute-start.16 = (f32[128,256]{1,0:T(8,128)S(1)}, f32[128,256]{1,0:T(8,128)S(1)}, u32[]{:S(2)}, u32[]{:S(2)}) collective-permute-start(f32[128,256]{1,0:T(8,128)S(1)} %get-tuple-element.86), channel_id=1, source_target_pairs={{0,2},{1,3},{2,0},{3,1},{4,6},{5,7},{6,4},{7,5},{8,10},{9,11},{10,... | collective-permute-start | bytes 393224 | tf_op jit(solution)/shard_map/ppermute | solution.py:548
  71.5 4.7 %values_f.1 = (bf16[512,16,128]{2,1,0:T(8,128)(2,1)}, f32[512,16]{1,0:T(8,128)S(1)}) custom-call(f32[8,256,128]{2,1,0:T(8,128)S(1)} %collective-permute-done.15.refs_0_.got.refs_3_, f32[8,256,128]{2,1,0:T(8,128)S(1)} %get-tuple-element.77.refs_0_.mine.refs_4_, f32[16,128,128]{2,1,0:T(8,128)S(1)} %get-tuple-element.78.refs_1_.middle, ...), custom_call_target="tpu_custom_call" | custom-call | tf_op jit(solution)/shard_map/values_f/pallas_call | solution.py:508
  76.2 1.2 %collective-permute-done.17.refs_1_ = f32[128,256]{1,0:T(8,128)S(1)} collective-permute-done((f32[128,256]{1,0:T(8,128)S(1)}, f32[128,256]{1,0:T(8,128)S(1)}, u32[]{:S(2)}, u32[]{:S(2)}) %collective-permute-start.17) | collective-permute-done | bytes 131104 | tf_op jit(solution)/shard_map/ppermute | solution.py:548
  77.5 2.9 %collective-permute-start.21 = (f32[128,256]{1,0:T(8,128)S(1)}, f32[128,256]{1,0:T(8,128)S(1)}, u32[]{:S(2)}, u32[]{:S(2)}) collective-permute-start(f32[128,256]{1,0:T(8,128)S(1)} %add.1._.refs_3_), channel_id=1, source_target_pairs={{0,3},{1,2},{2,1},{3,0},{4,7},{5,6},{6,5},{7,4},{8,11},{9,10},{10,... | collective-permute-start | bytes 393224 | tf_op jit(solution)/shard_map/ppermute | solution.py:548
  80.5 1.3 %collective-permute-start.19 = (f32[128,256]{1,0:T(8,128)S(1)}, f32[128,256]{1,0:T(8,128)S(1)}, u32[]{:S(2)}, u32[]{:S(2)}) collective-permute-start(f32[128,256]{1,0:T(8,128)S(1)} %add.1._.refs_3_), channel_id=1, source_target_pairs={{0,2},{1,3},{2,0},{3,1},{4,6},{5,7},{6,4},{7,5},{8,10},{9,11},{10,... | collective-permute-start | bytes 393224 | tf_op jit(solution)/shard_map/ppermute | solution.py:548
  81.7 4.8 %values_b.1 = (bf16[512,16,128]{2,1,0:T(8,128)(2,1)}, f32[512,16]{1,0:T(8,128)S(1)}) custom-call(f32[8,256,128]{2,1,0:T(8,128)S(1)} %collective-permute-done.15.refs_0_.got.refs_3_, f32[8,256,128]{2,1,0:T(8,128)S(1)} %get-tuple-element.77.refs_0_.mine.refs_4_, f32[16,128,128]{2,1,0:T(8,128)S(1)} %get-tuple-element.80.refs_2_.middle, ...), custom_call_target="tpu_custom_call" | custom-call | tf_op jit(solution)/shard_map/values_b/pallas_call | solution.py:508
  86.5 1.7 %decay.1 = (f32[16,512]{1,0:T(8,128)}, f32[8,128]{1,0:T(8,128)S(1)}) custom-call(f32[512,16]{1,0:T(8,128)S(1)} %get-tuple-element.91.refs_0_, f32[512,16]{1,0:T(8,128)S(1)} %get-tuple-element.89.refs_4_.refs_1_, f32[512,16]{1,0:T(8,128)S(1)} %get-tuple-element.92.refs_2_, f32[8,256,128]{2,1,0:T(8,128)S(1)} %collective-permute-done.15.refs_0_.got.refs_3_, ...), custom_call_target="tpu_custom_call" | custom-call | tf_op jit(solution)/shard_map/decay/pallas_call | solution.py:255
  (36 shorter events, 4.6 us)
Async XLA Ops:
  0.6 7.0 %copy-start = (bf16[512,128]{1,0:T(8,128)(2,1)S(1)}, bf16[512,128]{1,0:T(8,128)(2,1)}, u32[]{:S(2)}) copy-start(bf16[512,128]{1,0:T(8,128)(2,1)} %proj.2) | copy-start | bytes 393220
  0.6 7.0 %copy-start.2 = (bf16[512,16,128]{2,1,0:T(8,128)(2,1)S(1)}, bf16[512,16,128]{2,1,0:T(8,128)(2,1)}, u32[]{:S(2)}) copy-start(bf16[512,16,128]{2,1,0:T(8,128)(2,1)} %refs_0_.3) | copy-start | bytes 6291460
  4.3 7.4 %collective-permute-start = (f32[8,136,128]{2,1,0:T(8,128)S(1)}, f32[8,136,128]{2,1,0:T(8,128)S(1)}, u32[]{:S(2)}, u32[]{:S(2)}) collective-permute-start(f32[8,136,128]{2,1,0:T(8,128)S(1)} %get-tuple-element.52), channel_id=1, source_target_pairs={{0,4},{4,0},{8,12},{12,8},{16,20},{20,16},{24,28},{28,24},{32,36},... | collective-permute-start | bytes 1671176 | tf_op jit(solution)/shard_map/ppermute | solution.py:397
  7.7 11.5 %copy-start.1 = (bf16[512,128]{1,0:T(8,128)(2,1)S(1)}, bf16[512,128]{1,0:T(8,128)(2,1)}, u32[]{:S(2)}) copy-start(bf16[512,128]{1,0:T(8,128)(2,1)} %proj.3) | copy-start | bytes 393220
  7.7 11.5 %copy-start.3 = (f32[16]{0:T(128)S(1)}, f32[16]{0:T(128)}, u32[]{:S(2)}) copy-start(f32[16]{0:T(128)} %param.10) | copy-start | bytes 196
  9.7 2.0 %collective-permute-start.1 = (f32[8,128,128]{2,1,0:T(8,128)S(1)}, f32[8,128,128]{2,1,0:T(8,128)S(1)}, u32[]{:S(2)}, u32[]{:S(2)}) collective-permute-start(f32[8,128,128]{2,1,0:T(8,128)S(1)} %get-tuple-element.55.refs_5_), channel_id=1, source_target_pairs={{0,4},{4,0},{8,12},{12,8},{16,20},{20,16},{24,28},{28,24},{32,36},... | collective-permute-start | bytes 1572872 | tf_op jit(solution)/shard_map/ppermute | solution.py:397
  11.9 11.8 %collective-permute-start.2 = (f32[2,264,128]{2,1,0:T(8,128)S(1)}, f32[2,264,128]{2,1,0:T(8,128)S(1)}, u32[]{:S(2)}, u32[]{:S(2)}) collective-permute-start(f32[2,264,128]{2,1,0:T(8,128)S(1)} %get-tuple-element.56), channel_id=1, source_target_pairs={{0,16},{4,52},{8,24},{12,60},{16,0},{20,36},{24,8},{28,44},{32,48}... | collective-permute-start | bytes 811016 | tf_op jit(solution)/shard_map/ppermute | solution.py:397
  14.3 9.4 %collective-permute-start.3 = (f32[2,264,128]{2,1,0:T(8,128)S(1)}, f32[2,264,128]{2,1,0:T(8,128)S(1)}, u32[]{:S(2)}, u32[]{:S(2)}) collective-permute-start(f32[2,264,128]{2,1,0:T(8,128)S(1)} %get-tuple-element.57), channel_id=1, source_target_pairs={{0,8},{4,44},{8,0},{12,36},{16,24},{20,60},{24,16},{28,52},{32,40}... | collective-permute-start | bytes 811016 | tf_op jit(solution)/shard_map/ppermute | solution.py:397
  14.3 12.0 %collective-permute-start.4 = (f32[2,264,128]{2,1,0:T(8,128)S(1)}, f32[2,264,128]{2,1,0:T(8,128)S(1)}, u32[]{:S(2)}, u32[]{:S(2)}) collective-permute-start(f32[2,264,128]{2,1,0:T(8,128)S(1)} %get-tuple-element.58), channel_id=1, source_target_pairs={{0,24},{4,60},{8,16},{12,52},{16,8},{20,44},{24,0},{28,36},{32,56}... | collective-permute-start | bytes 811016 | tf_op jit(solution)/shard_map/ppermute | solution.py:397
  15.7 12.9 %collective-permute-start.5 = (f32[2,264,128]{2,1,0:T(8,128)S(1)}, f32[2,264,128]{2,1,0:T(8,128)S(1)}, u32[]{:S(2)}, u32[]{:S(2)}) collective-permute-start(f32[2,264,128]{2,1,0:T(8,128)S(1)} %get-tuple-element.59.refs_0_), channel_id=1, source_target_pairs={{0,0},{4,36},{8,8},{12,44},{16,16},{20,52},{24,24},{28,60},{32,32}... | collective-permute-start | bytes 811016 | tf_op jit(solution)/shard_map/ppermute | solution.py:397
  28.8 1.8 %collective-permute-start.6 = (f32[2,264,128]{2,1,0:T(8,128)S(1)}, f32[2,264,128]{2,1,0:T(8,128)S(1)}, u32[]{:S(2)}, u32[]{:S(2)}) collective-permute-start(f32[2,264,128]{2,1,0:T(8,128)S(1)} %slab_up.1.refs_0_.refs_4_), channel_id=1, source_target_pairs={{0,4},{4,0},{8,12},{12,8},{16,20},{20,16},{24,28},{28,24},{32,36},... | collective-permute-start | bytes 811016 | tf_op jit(solution)/shard_map/ppermute | solution.py:397
  30.7 11.9 %collective-permute-start.8 = (f32[2,136,128]{2,1,0:T(8,128)S(1)}, f32[2,136,128]{2,1,0:T(8,128)S(1)}, u32[]{:S(2)}, u32[]{:S(2)}) collective-permute-start(f32[2,136,128]{2,1,0:T(8,128)S(1)} %get-tuple-element.65), channel_id=1, source_target_pairs={{0,64},{4,196},{8,72},{12,204},{16,80},{20,212},{24,88},{28,220},{... | collective-permute-start | bytes 417800 | tf_op jit(solution)/shard_map/ppermute | solution.py:397
  36.8 8.2 %collective-permute-start.7 = (f32[136,128]{1,0:T(8,128)S(1)}, f32[136,128]{1,0:T(8,128)S(1)}, u32[]{:S(2)}, u32[]{:S(2)}) collective-permute-start(f32[136,128]{1,0:T(8,128)S(1)} %get-tuple-element.64), channel_id=1, source_target_pairs={{0,128},{4,132},{8,136},{12,140},{16,144},{20,148},{24,152},{28,15... | collective-permute-start | bytes 208904 | tf_op jit(solution)/shard_map/ppermute | solution.py:397
  42.6 3.9 %collective-permute-start.10 = (f32[2,136,128]{2,1,0:T(8,128)S(1)}, f32[2,136,128]{2,1,0:T(8,128)S(1)}, u32[]{:S(2)}, u32[]{:S(2)}) collective-permute-start(f32[2,136,128]{2,1,0:T(8,128)S(1)} %collective-permute-done.8.refs_7_), channel_id=1, source_target_pairs={{0,4},{4,0},{8,12},{12,8},{16,20},{20,16},{24,28},{28,24},{32,36},... | collective-permute-start | bytes 417800 | tf_op jit(solution)/shard_map/ppermute | solution.py:397
  45.0 1.6 %collective-permute-start.9 = (f32[136,128]{1,0:T(8,128)S(1)}, f32[136,128]{1,0:T(8,128)S(1)}, u32[]{:S(2)}, u32[]{:S(2)}) collective-permute-start(f32[136,128]{1,0:T(8,128)S(1)} %collective-permute-done.7.refs_6_), channel_id=1, source_target_pairs={{0,4},{4,0},{8,12},{12,8},{16,20},{20,16},{24,28},{28,24},{32,36},... | collective-permute-start | bytes 208904 | tf_op jit(solution)/shard_map/ppermute | solution.py:397
  47.0 11.8 %collective-permute-start.11 = (f32[2,256,128]{2,1,0:T(8,128)S(1)}, f32[2,256,128]{2,1,0:T(8,128)S(1)}, u32[]{:S(2)}, u32[]{:S(2)}) collective-permute-start(f32[2,256,128]{2,1,0:T(8,128)S(1)} %get-tuple-element.66), channel_id=1, source_target_pairs={{0,16},{4,52},{8,24},{12,60},{16,0},{20,36},{24,8},{28,44},{32,48}... | collective-permute-start | bytes 786440 | tf_op jit(solution)/shard_map/ppermute | solution.py:397
  48.4 10.4 %collective-permute-start.12 = (f32[2,256,128]{2,1,0:T(8,128)S(1)}, f32[2,256,128]{2,1,0:T(8,128)S(1)}, u32[]{:S(2)}, u32[]{:S(2)}) collective-permute-start(f32[2,256,128]{2,1,0:T(8,128)S(1)} %get-tuple-element.67), channel_id=1, source_target_pairs={{0,8},{4,44},{8,0},{12,36},{16,24},{20,60},{24,16},{28,52},{32,40}... | collective-permute-start | bytes 786440 | tf_op jit(solution)/shard_map/ppermute | solution.py:397
  49.4 13.6 %collective-permute-start.13 = (f32[2,256,128]{2,1,0:T(8,128)S(1)}, f32[2,256,128]{2,1,0:T(8,128)S(1)}, u32[]{:S(2)}, u32[]{:S(2)}) collective-permute-start(f32[2,256,128]{2,1,0:T(8,128)S(1)} %get-tuple-element.68), channel_id=1, source_target_pairs={{0,24},{4,60},{8,16},{12,52},{16,8},{20,44},{24,0},{28,36},{32,56}... | collective-permute-start | bytes 786440 | tf_op jit(solution)/shard_map/ppermute | solution.py:397
  51.4 12.2 %collective-permute-start.14 = (f32[2,256,128]{2,1,0:T(8,128)S(1)}, f32[2,256,128]{2,1,0:T(8,128)S(1)}, u32[]{:S(2)}, u32[]{:S(2)}) collective-permute-start(f32[2,256,128]{2,1,0:T(8,128)S(1)} %get-tuple-element.69.refs_0_), channel_id=1, source_target_pairs={{0,0},{4,36},{8,8},{12,44},{16,16},{20,52},{24,24},{28,60},{32,32}... | collective-permute-start | bytes 786440 | tf_op jit(solution)/shard_map/ppermute | solution.py:397
  64.0 2.7 %collective-permute-start.15 = (f32[8,256,128]{2,1,0:T(8,128)S(1)}, f32[8,256,128]{2,1,0:T(8,128)S(1)}, u32[]{:S(2)}, u32[]{:S(2)}) collective-permute-start(f32[8,256,128]{2,1,0:T(8,128)S(1)} %get-tuple-element.76), channel_id=1, source_target_pairs={{0,4},{4,0},{8,12},{12,8},{16,20},{20,16},{24,28},{28,24},{32,36},... | collective-permute-start | bytes 3145736 | tf_op jit(solution)/shard_map/ppermute | solution.py:397
  67.8 8.5 %collective-permute-start.16 = (f32[128,256]{1,0:T(8,128)S(1)}, f32[128,256]{1,0:T(8,128)S(1)}, u32[]{:S(2)}, u32[]{:S(2)}) collective-permute-start(f32[128,256]{1,0:T(8,128)S(1)} %get-tuple-element.86), channel_id=1, source_target_pairs={{0,2},{1,3},{2,0},{3,1},{4,6},{5,7},{6,4},{7,5},{8,10},{9,11},{10,... | collective-permute-start | bytes 393224 | tf_op jit(solution)/shard_map/ppermute | solution.py:548
  70.8 6.7 %collective-permute-start.17 = (f32[128,256]{1,0:T(8,128)S(1)}, f32[128,256]{1,0:T(8,128)S(1)}, u32[]{:S(2)}, u32[]{:S(2)}) collective-permute-start(f32[128,256]{1,0:T(8,128)S(1)} %get-tuple-element.87), channel_id=1, source_target_pairs={{0,1},{1,0},{2,3},{3,2},{4,5},{5,4},{6,7},{7,6},{8,9},{9,8},{10,11... | collective-permute-start | bytes 393224 | tf_op jit(solution)/shard_map/ppermute | solution.py:548
  71.2 6.3 %collective-permute-start.18 = (f32[128,256]{1,0:T(8,128)S(1)}, f32[128,256]{1,0:T(8,128)S(1)}, u32[]{:S(2)}, u32[]{:S(2)}) collective-permute-start(f32[128,256]{1,0:T(8,128)S(1)} %get-tuple-element.88), channel_id=1, source_target_pairs={{0,3},{1,2},{2,1},{3,0},{4,7},{5,6},{6,5},{7,4},{8,11},{9,10},{10,... | collective-permute-start | bytes 393224 | tf_op jit(solution)/shard_map/ppermute | solution.py:548
  77.5 10.6 %collective-permute-start.21 = (f32[128,256]{1,0:T(8,128)S(1)}, f32[128,256]{1,0:T(8,128)S(1)}, u32[]{:S(2)}, u32[]{:S(2)}) collective-permute-start(f32[128,256]{1,0:T(8,128)S(1)} %add.1._.refs_3_), channel_id=1, source_target_pairs={{0,3},{1,2},{2,1},{3,0},{4,7},{5,6},{6,5},{7,4},{8,11},{9,10},{10,... | collective-permute-start | bytes 393224 | tf_op jit(solution)/shard_map/ppermute | solution.py:548
  80.4 7.7 %collective-permute-start.20 = (f32[128,256]{1,0:T(8,128)S(1)}, f32[128,256]{1,0:T(8,128)S(1)}, u32[]{:S(2)}, u32[]{:S(2)}) collective-permute-start(f32[128,256]{1,0:T(8,128)S(1)} %add.1._.refs_3_), channel_id=1, source_target_pairs={{0,1},{1,0},{2,3},{3,2},{4,5},{5,4},{6,7},{7,6},{8,9},{9,8},{10,11... | collective-permute-start | bytes 393224 | tf_op jit(solution)/shard_map/ppermute | solution.py:548
  80.5 7.7 %collective-permute-start.19 = (f32[128,256]{1,0:T(8,128)S(1)}, f32[128,256]{1,0:T(8,128)S(1)}, u32[]{:S(2)}, u32[]{:S(2)}) collective-permute-start(f32[128,256]{1,0:T(8,128)S(1)} %add.1._.refs_3_), channel_id=1, source_target_pairs={{0,2},{1,3},{2,0},{3,1},{4,6},{5,7},{6,4},{7,5},{8,10},{9,11},{10,... | collective-permute-start | bytes 393224 | tf_op jit(solution)/shard_map/ppermute | solution.py:548

commit v2 on v1

--- a/solution.py
+++ b/solution.py
@@ -53,8 +53,9 @@
 
 
 def running_sum(rows, strict):
-    tri = triangle(strict)
-    return sum(dot(part, tri, ((1,), (1,))) for part in split_three(rows))
+    count = rows.shape[0]
+    sums = dot(jnp.concatenate(split_three(rows), axis=0), triangle(strict), ((1,), (1,)))
+    return sums[:count] + sums[count : 2 * count] + sums[2 * count :]
 
 
 def kept_half():
@@ -62,49 +63,45 @@
     return jnp.bitwise_xor(core, depth % 2)
 
 
-def summary_body(reverse, *refs):
-    if reverse:
-        here, proj, rows_all, heads_out, send, keep, middle, total = refs
-        order = (1, 0)
-    else:
-        values, proj_far, log_rows, heads_out, send, keep, middle, levels_out, rows_all, here, proj, logs, total, arrived = refs
-        order = (0, 1)
-        copies = [
-            pltpu.make_async_copy(log_rows, logs, arrived.at[0]),
-            pltpu.make_async_copy(proj_far, proj, arrived.at[1]),
-        ]
-        copies += [
-            pltpu.make_async_copy(values.at[pl.ds(span * SPAN, SPAN)], here.at[span], arrived.at[2 + span])
-            for span in order
-        ]
-        for copy in copies:
-            copy.start()
-        copies[0].wait()
-        for span in order:
-            tokens = slice(span * SPAN, span * SPAN + SPAN)
-            level_rows = running_sum(logs[:, tokens], False)
-            levels_out[tokens, :] = jnp.transpose(level_rows)
-            rows_all[:, tokens] = level_rows
-        copies[1].wait()
+def fresh_state(proj_t, weight, value):
+    weighted = jnp.concatenate(split_two(proj_t * weight), axis=0)
+    both = dot(weighted, value, ((1,), (0,)))
+    return both[:WIDTH] + both[WIDTH:]
+
+
+def summary_body(values, proj_far, log_rows, *refs):
+    heads_out, send, keep, middle, proj_out, levels_out, rows_all, here, proj, logs, total, arrived = refs
+    copies = [
+        pltpu.make_async_copy(log_rows, logs, arrived.at[0]),
+        pltpu.make_async_copy(proj_far, proj, arrived.at[1]),
+    ]
+    copies += [
+        pltpu.make_async_copy(values.at[pl.ds(span * SPAN, SPAN)], here.at[span], arrived.at[2 + span]) for span in (0, 1)
+    ]
+    for copy in copies:
+        copy.start()
+    copies[0].wait()
+    sums = running_sum(jnp.concatenate([logs[:, :SPAN], logs[:, SPAN:]], axis=0), False)
+    for span in (0, 1):
+        tokens = slice(span * SPAN, span * SPAN + SPAN)
+        level_rows = sums[span * HEADS : span * HEADS + HEADS]
+        levels_out[tokens, :] = jnp.transpose(level_rows)
+        rows_all[:, tokens] = level_rows
+    copies[1].wait()
     last = [rows_all[:, SPAN * span + SPAN - 1 : SPAN * span + SPAN] for span in (0, 1)]
-    carried = jnp.exp(last[order[1]])
+    carried = jnp.exp(last[1])
     all_log = last[0] + last[1]
-    for span in order:
+    for span in (0, 1):
         tokens = slice(span * SPAN, span * SPAN + SPAN)
-        level_rows = rows_all[:, tokens]
-        weight = jnp.exp(level_rows) if reverse else jnp.exp(last[span] - level_rows)
+        weight = jnp.exp(last[span] - rows_all[:, tokens])
         proj_t = jnp.transpose(proj[tokens, :]).astype(f32)
-        if reverse:
-            swapped = jnp.swapaxes(here[tokens], 0, 1)
-        else:
-            copies[2 + span].wait()
-            swapped = jnp.swapaxes(here[span], 0, 1)
+        proj_out[:, tokens] = proj_t
+        copies[2 + span].wait()
+        swapped = jnp.swapaxes(here[span], 0, 1)
         heads_out[:, tokens, :] = swapped
         for head in range(HEADS):
-            weighted = jnp.concatenate(split_two(proj_t * weight[head : head + 1, :]), axis=0)
-            both = dot(weighted, swapped[head], ((1,), (0,)))
-            fresh = both[:WIDTH] + both[WIDTH:]
-            if span == order[0]:
+            fresh = fresh_state(proj_t, weight[head : head + 1, :], swapped[head])
+            if span == 0:
                 middle[head] = fresh
             else:
                 total[head] = fresh + carried[head : head + 1, :] * middle[head]
@@ -117,42 +114,82 @@
                 for at in range(HALF):
                     head = half * HALF + at
                     out[at, :WIDTH, :] = total[head]
-                    if not reverse:
-                        out[at, WIDTH:, :] = jnp.broadcast_to(all_log[head : head + 1, :], (LOG_ROWS, WIDTH))
-
-
-def summary(reverse, values, proj, row_values):
+                    out[at, WIDTH:, :] = jnp.broadcast_to(all_log[head : head + 1, :], (LOG_ROWS, WIDTH))
+
+
+def summary(values, proj, log_rows):
     tokens = values.shape[0]
-    rows = WIDTH if reverse else WIDTH + LOG_ROWS
-    shapes = [
-        jax.ShapeDtypeStruct((HEADS, tokens, WIDTH), bf16),
-        jax.ShapeDtypeStruct((HALF, rows, WIDTH), f32),
-        jax.ShapeDtypeStruct((HALF, rows, WIDTH), f32),
-        jax.ShapeDtypeStruct((HEADS, WIDTH, WIDTH), f32),
-    ]
-    scratch = [pltpu.VMEM((HEADS, WIDTH, WIDTH), f32)]
-    arrays = [values, proj, row_values]
-    if not reverse:
-        shapes += [
+    packed = jax.ShapeDtypeStruct((HALF, WIDTH + LOG_ROWS, WIDTH), f32)
+    return pl.pallas_call(
+        summary_body,
+        in_specs=[anywhere] * 3,
+        out_shape=[
+            jax.ShapeDtypeStruct((HEADS, tokens, WIDTH), bf16),
+            packed,
+            packed,
+            jax.ShapeDtypeStruct((HEADS, WIDTH, WIDTH), f32),
+            jax.ShapeDtypeStruct((WIDTH, tokens), f32),
             jax.ShapeDtypeStruct((tokens, HEADS), f32),
             jax.ShapeDtypeStruct((HEADS, tokens), f32),
-        ]
-        scratch = [
+        ],
+        scratch_shapes=[
             pltpu.VMEM((2, SPAN, HEADS, WIDTH), bf16),
             pltpu.VMEM((tokens, WIDTH), bf16),
             pltpu.VMEM((HEADS, tokens), f32),
-            *scratch,
+            pltpu.VMEM((HEADS, WIDTH, WIDTH), f32),
             pltpu.SemaphoreType.DMA((4,)),
-        ]
-        arrays = [pltpu.with_memory_space_constraint(array, pltpu.HBM) for array in arrays]
+        ],
+        compiler_params=params(),
+        name="summary_f",
+    )(*[pltpu.with_memory_space_constraint(array, pltpu.HBM) for array in (values, proj, log_rows)])
+
+
+def pulled_half(own, heads, proj_t, rows_all, middle, total):
+    half = kept_half() if own else 1 - kept_half()
+    rows = jnp.where(half == 0, rows_all[:HALF], rows_all[HALF:])
+    carried = jnp.exp(rows[:, SPAN - 1 : SPAN])
+    for span in (1, 0):
+        tokens = slice(span * SPAN, span * SPAN + SPAN)
+        weight = jnp.exp(rows[:, tokens])
+        for at in range(HALF):
+            fresh = fresh_state(proj_t[:, tokens], weight[at : at + 1, :], heads[half * HALF + at, tokens, :])
+            if span == 1:
+                middle[at] = fresh
+            else:
+                total[at] = fresh + carried[at : at + 1, :] * middle[at]
+
+
+def pulled_send_body(values, proj, rows_all, heads_out, proj_out, middle, send):
+    for span in (0, 1):
+        tokens = slice(span * SPAN, span * SPAN + SPAN)
+        proj_out[:, tokens] = jnp.transpose(proj[tokens, :]).astype(f32)
+        heads_out[:, tokens, :] = jnp.swapaxes(values[tokens], 0, 1)
+    pulled_half(False, heads_out, proj_out, rows_all, middle, send)
+
+
+def pulled_keep_body(heads, proj_t, rows_all, middle_send, middle, keep, scratch):
+    pulled_half(True, heads, proj_t, rows_all, scratch, keep)
+    kept = kept_half()
+    for at in range(HALF):
+        middle[kept * HALF + at] = scratch[at]
+        middle[(1 - kept) * HALF + at] = middle_send[at]
+
+
+def pulled_send(values, proj, rows_all):
+    tokens = values.shape[0]
+    half = jax.ShapeDtypeStruct((HALF, WIDTH, WIDTH), f32)
     return pl.pallas_call(
-        functools.partial(summary_body, reverse),
-        in_specs=[pl.BlockSpec(memory_space=pltpu.VMEM) if reverse else anywhere] * 3,
-        out_shape=shapes,
-        scratch_shapes=scratch,
+        pulled_send_body,
+        in_specs=[pl.BlockSpec(memory_space=pltpu.VMEM)] * 3,
+        out_shape=[
+            jax.ShapeDtypeStruct((HEADS, tokens, WIDTH), bf16),
+            jax.ShapeDtypeStruct((WIDTH, tokens), f32),
+            half,
+            half,
+        ],
         compiler_params=params(),
-        name="summary_b" if reverse else "summary_f",
-    )(*arrays)
+        name="summary_b_send",
+    )(values, proj, rows_all)
 
 
 def line_sums(product, head):
@@ -198,7 +235,7 @@
         dy_t_out[head] = jnp.transpose(dy)
         y_out[head] = y + gain * x32
         dx_out[head] = dx + gain * dy32
-    cross_out[...] = cross[:, :HEADS]
+    cross_out[...] = jnp.transpose(cross[:, :HEADS])
     g00, g10, g11 = [split_two(g) for g in score_grad]
     grad_c0 = sum(dot(g, b[low], ((1,), (0,))) for g in g00)
     grad_c1 = sum(dot(g, b[low], ((1,), (0,))) for g in g10) + sum(dot(g, b[high], ((1,), (0,))) for g in g11)
@@ -215,6 +252,7 @@
     by_head = pl.BlockSpec((HEADS, SPAN, WIDTH), lambda s: (0, span, 0))
     flat = pl.BlockSpec((SPAN, WIDTH), lambda s: (span, 0))
     thin = pl.BlockSpec((SPAN, HEADS), lambda s: (span, 0))
+    rows = pl.BlockSpec((HEADS, SPAN), lambda s: (0, span))
     turned = pl.BlockSpec((HEADS, WIDTH, SPAN), lambda s: (0, 0, span))
     turned_shape = jax.ShapeDtypeStruct((HEADS, WIDTH, tokens), bf16)
     return pl.pallas_call(
@@ -226,18 +264,18 @@
             flat,
             flat,
             thin,
-            pl.BlockSpec((HEADS, SPAN), lambda s: (0, span)),
+            rows,
             pl.BlockSpec((1, HEADS), lambda s: (0, 0)),
             anywhere,
         ]
         + [anywhere] * len(so_far),
-        out_specs=[by_head, by_head, turned, turned, thin, pl.BlockSpec((2 * WIDTH, SPAN), lambda s: (0, span))],
+        out_specs=[by_head, by_head, turned, turned, rows, pl.BlockSpec((2 * WIDTH, SPAN), lambda s: (0, span))],
         out_shape=[
             jax.ShapeDtypeStruct((HEADS, tokens, WIDTH), f32),
             jax.ShapeDtypeStruct((HEADS, tokens, WIDTH), f32),
             turned_shape,
             turned_shape,
-            jax.ShapeDtypeStruct((tokens, HEADS), f32),
+            jax.ShapeDtypeStruct((HEADS, tokens), f32),
             jax.ShapeDtypeStruct((2 * WIDTH, tokens), f32),
         ],
         input_output_aliases={8 + at: at for at in range(len(so_far))},
@@ -422,33 +460,46 @@
     return jnp.where(half == 0, array[:HALF], array[HALF:])
 
 
-def grad_body(own, states, middle_f, middle_b, level_rows, x_turned, dy_turned, base, *refs):
+def lines_of(own, span, way, states, middle, level_rows, values):
     half = kept_half() if own else 1 - kept_half()
+    lanes = slice(span * SPAN, span * SPAN + SPAN)
+    rows = half_of(own, level_rows[:, lanes])
+    weight = jnp.exp(rows[:, SPAN - 1 : SPAN] - rows) if way else jnp.exp(rows)
+    last = 2 * SPAN - 1 if way else SPAN - 1
+    crossed = half_of(own, jnp.exp(level_rows[:, last : last + 1]))
+    for at in range(HALF):
+        head = half * HALF + at
+        state = states[at, way * WIDTH : way * WIDTH + WIDTH, :]
+        if span == 1 - way:
+            state = crossed[at : at + 1, :] * state + middle[head]
+        value = values[head, :, lanes]
+        line = dot(
+            jnp.concatenate(split_two(state), axis=1),
+            jnp.concatenate([value, value], axis=0),
+            ((1,), (0,)),
+        )
+        yield weight[at : at + 1, :], line
+
+
+def grad_body(own, states, middle_f, middle_b, level_rows, x_turned, dy_turned, b_turned, c_turned, base, *refs):
     for span in range(2):
         lanes = slice(span * SPAN, span * SPAN + SPAN)
-        rows = half_of(own, level_rows[:, lanes])
-        for way, middle, values in ((0, middle_f, dy_turned), (1, middle_b, x_turned)):
-            weight = jnp.exp(rows[:, SPAN - 1 : SPAN] - rows) if way else jnp.exp(rows)
-            last = 2 * SPAN - 1 if way else SPAN - 1
-            crossed = half_of(own, jnp.exp(level_rows[:, last : last + 1]))
+        crosses = []
+        for way, middle, values, proj in ((0, middle_f, dy_turned, c_turned), (1, middle_b, x_turned, b_turned)):
             of_way = slice(way * WIDTH, way * WIDTH + WIDTH)
             acc = base[of_way, lanes]
-            for at in range(HALF):
-                head = half * HALF + at
-                state = states[at, of_way, :]
-                if span == 1 - way:
-                    state = crossed[at : at + 1, :] * state + middle[head]
-                value = values[head, :, lanes]
-                line = dot(
-                    jnp.concatenate(split_two(state), axis=1),
-                    jnp.concatenate([value, value], axis=0),
-                    ((1,), (0,)),
-                )
-                acc = acc + weight[at : at + 1, :] * line
+            crosses.append([])
+            for weight, line in lines_of(own, span, way, states, middle, level_rows, values):
+                acc = acc + weight * line
+                if own:
+                    crosses[way].append(weight * jnp.sum(proj[:, lanes] * line, axis=0, keepdims=True))
             if own:
                 refs[0][of_way, lanes] = acc
             else:
                 refs[4][lanes, of_way] = jnp.transpose(acc)
+        if own:
+            for at in range(HALF):
+                refs[1][at : at + 1, lanes] = crosses[0][at] - crosses[1][at]
     if not own:
         mine_tp = lax.axis_index("tp")
         for k in range(4):
@@ -456,25 +507,31 @@
             refs[k][...] = refs[4][pl.ds(start, 128), :]
 
 
-def grad_call(own, states, middle_f, middle_b, level_rows, x_turned, dy_turned, base):
-    tokens = base.shape[1]
-    outs = [base.shape] if own else [(tokens // 4, 2 * WIDTH)] * 4
+def cross_body(states, middle_f, middle_b, level_rows, x_turned, dy_turned, b_turned, c_turned, out):
+    for span in range(2):
+        lanes = slice(span * SPAN, span * SPAN + SPAN)
+        crosses = []
+        for way, middle, values, proj in ((0, middle_f, dy_turned, c_turned), (1, middle_b, x_turned, b_turned)):
+            lines = lines_of(False, span, way, states, middle, level_rows, values)
+            crosses.append([weight * jnp.sum(proj[:, lanes] * line, axis=0, keepdims=True) for weight, line in lines])
+        for at in range(HALF):
+            out[at : at + 1, lanes] = crosses[0][at] - crosses[1][at]
+
+
+def grad_call(own, states, *arrays):
+    tokens = arrays[-1].shape[1]
+    outs = [arrays[-1].shape, (HALF, tokens)] if own else [(tokens // 4, 2 * WIDTH)] * 4
     return small(
         functools.partial(grad_body, own),
         outs,
         "grads_own" if own else "grads_other",
         states,
-        middle_f,
-        middle_b,
-        level_rows,
-        x_turned,
-        dy_turned,
-        base,
+        *arrays,
         scratch=[] if own else [(tokens, 2 * WIDTH)],
     )
 
 
-def value_body(way, got, mine, middle, levels, proj, part, values, _, out, cross_out, wide, turned, left):
+def value_body(way, got, mine, middle, levels, proj, part, _, out, done, wide, turned, left):
     kept = kept_half()
     states = slice(way * WIDTH, way * WIDTH + WIDTH)
     last = 2 * SPAN - 1 if way else SPAN - 1
@@ -485,7 +542,6 @@
         level = levels[tokens, :]
         weight = jnp.exp(level[SPAN - 1 : SPAN, :] - level) if way else jnp.exp(level)
         doubled = jnp.concatenate([proj[tokens, :], proj[tokens, :]], axis=1)
-        cross = jnp.zeros((SPAN, WIDTH), f32)
         for head in range(HEADS):
             at = head % HALF
             state = jnp.where(head // HALF == kept, mine[at, states, :], got[at, states, :])
@@ -493,25 +549,24 @@
                 state = crossed[:, head : head + 1] * state + middle[head]
             far = dot(doubled, jnp.concatenate(split_two(state), axis=0), ((1,), (0,)))
             far = far * weight[:, head : head + 1]
-            cross = cross + line_sums(far * values[head, tokens, :].astype(f32), head)
             wide[span, head] = (part[head, tokens, :] + far).astype(bf16)
-        cross_out[tokens, :] = cross[:, :HEADS]
         turned[span] = jnp.swapaxes(wide[span], 0, 1)
         copies.append(pltpu.make_async_copy(turned.at[span], out.at[pl.ds(span * SPAN, SPAN)], left.at[span]))
         copies[-1].start()
+    done[...] = jnp.zeros_like(done)
     for copy in copies:
         copy.wait()
 
 
-def value_call(way, got, mine, middle, levels, proj, part, values, after):
+def value_call(way, got, mine, middle, levels, proj, part, after):
     tokens = levels.shape[0]
     return pl.pallas_call(
         functools.partial(value_body, way),
-        in_specs=[pl.BlockSpec(memory_space=pltpu.VMEM)] * 7 + [anywhere],
+        in_specs=[pl.BlockSpec(memory_space=pltpu.VMEM)] * 6 + [anywhere],
         out_specs=[anywhere, pl.BlockSpec(memory_space=pltpu.VMEM)],
         out_shape=[
             jax.ShapeDtypeStruct((tokens, HEADS, WIDTH), bf16),
-            jax.ShapeDtypeStruct((tokens, HEADS), f32),
+            jax.ShapeDtypeStruct((8, WIDTH), f32),
         ],
         scratch_shapes=[
             pltpu.VMEM((2, HEADS, SPAN, WIDTH), bf16),
@@ -520,13 +575,11 @@
         ],
         compiler_params=params(),
         name="values_b" if way else "values_f",
-    )(got, mine, middle, levels, proj, part, values, after)
-
-
-def decay_body(near, forward, backward, got, mine, send_b, keep_b, level_rows, out, done):
+    )(got, mine, middle, levels, proj, part, after)
+
+
+def start_body(got, mine, send_b, keep_b, level_rows, out):
     kept = kept_half()
-    sublane = lax.broadcasted_iota(jnp.int32, (HEADS, 1), 0)
-    start = jnp.zeros((HEADS, 1), f32)
     all_log = level_rows[:, SPAN - 1 : SPAN] + level_rows[:, 2 * SPAN - 1 : 2 * SPAN]
     for head in range(HEADS):
         at = head % HALF
@@ -535,10 +588,18 @@
         local = jnp.where(own, keep_b[at], send_b[at])
         pulled = local + jnp.exp(all_log[head : head + 1, :]) * incoming[WIDTH:]
         line = jnp.sum(jnp.sum(incoming[:WIDTH] * pulled, axis=0, keepdims=True), axis=1, keepdims=True)
-        start = jnp.where(sublane == head, line, start)
+        out[head : head + 1, :] = jnp.broadcast_to(line, (1, WIDTH))
+
+
+def decay_body(near, cross_own, cross_other, start_ref, out, done):
+    kept = kept_half()
+    start = start_ref[:, :1]
     for span in range(2):
         rows = slice(span * SPAN, span * SPAN + SPAN)
-        cross = jnp.transpose(near[rows, :] + forward[rows, :] - backward[rows, :])
+        own = cross_own[:, rows]
+        other = cross_other[:, rows]
+        far = jnp.concatenate([jnp.where(kept == 0, own, other), jnp.where(kept == 0, other, own)], axis=0)
+        cross = near[:, rows] + far
         out[:, rows] = start - running_sum(cross, True)
         start = start - jnp.sum(cross, axis=1, keepdims=True)
     done[...] = jnp.zeros_like(done)
@@ -552,7 +613,7 @@
     out[...] = p0[...] + p1[...] + p2[...] + p3[...]
 
 
-def join_body(p2, p1, p3, p0, c_out, b_out):
+def join_body(p0, p3, p1, p2, c_out, b_out):
     mine = lax.axis_index("tp")
     for k, piece in enumerate((p0, p1, p2, p3)):
         rows = pl.ds(pl.multiple_of(jnp.bitwise_xor(mine, k) * 128, 128), 128)
@@ -564,10 +625,21 @@
     tokens = inputs.shape[0]
     log_rows = logdecay.T
     gain = skip_gain.reshape(1, HEADS)
-    x_heads, send_f, keep_f, middle_f, levels, level_rows = summary(False, inputs, b_proj, log_rows)
+    x_heads, send_f, keep_f, middle_f, b_turned, levels, level_rows = summary(inputs, b_proj, log_rows)
     other_f = swap_cores(send_f)
-    dy_heads, send_b, keep_b, middle_b = summary(True, grad_out, c_proj, level_rows)
+    dy_heads, c_turned, middle_send, send_b = pulled_send(grad_out, c_proj, level_rows)
     other_b = swap_cores(send_b)
+    half = (HALF, WIDTH, WIDTH)
+    middle_b, keep_b = small(
+        pulled_keep_body,
+        [(HEADS, WIDTH, WIDTH), half],
+        "summary_b_keep",
+        dy_heads,
+        c_turned,
+        level_rows,
+        middle_send,
+        scratch=[half],
+    )
 
     cores = (keep_f, other_f, keep_b, other_b)
     packed = (2, TALL, WIDTH)
@@ -601,27 +673,20 @@
     )
     got = swap_cores(theirs)
 
-    (base,) = grad_call(True, mine, middle_f, middle_b, level_rows, x_turned, dy_turned, base)
-    pieces = grad_call(False, got, middle_f, middle_b, level_rows, x_turned, dy_turned, base)
-    outputs, cross_f = value_call(0, got, mine, middle_f, levels, c_proj, y_part, dy_heads, pieces[0])
+    turned = (middle_f, middle_b, level_rows, x_turned, dy_turned, b_turned, c_turned)
+    base, cross_own = grad_call(True, mine, *turned, base)
+    pieces = grad_call(False, got, *turned, base)
+    outputs, done = value_call(0, got, mine, middle_f, levels, c_proj, y_part, pieces[0])
     pieces = spread(pieces, over_tp)
-    (summed,) = small(add_body, [pieces[0].shape], "add", *taken(pieces), after=[cross_f])
-    grad_inputs, cross_b = value_call(1, got, mine, middle_b, levels, b_proj, dx_part, x_heads, summed)
+    (start,) = small(start_body, [(HEADS, WIDTH)], "start", got, mine, send_b, keep_b, level_rows, after=[done])
+    (cross_other,) = small(cross_body, [(HALF, tokens)], "cross_other", got, *turned, after=[start])
+    (summed,) = small(add_body, [pieces[0].shape], "add", *taken(pieces), after=[cross_other])
+    grad_inputs, done = value_call(1, got, mine, middle_b, levels, b_proj, dx_part, summed)
     decays, done = small(
-        decay_body,
-        [(HEADS, tokens), (8, WIDTH)],
-        "decay",
-        near,
-        cross_f,
-        cross_b,
-        got,
-        mine,
-        send_b,
-        keep_b,
-        level_rows,
+        decay_body, [(HEADS, tokens), (8, WIDTH)], "decay", near, cross_own, cross_other, start, after=[done]
     )
     joined = spread([summed] * 4, over_tp)
-    grad_c, grad_b = small(join_body, [(tokens, WIDTH)] * 2, "join", *taken(joined), after=[done])
+    grad_c, grad_b = small(join_body, [(tokens, WIDTH)] * 2, "join", *reversed(taken(joined)), after=[done])
     return outputs, grad_inputs, decays.T, grad_b, grad_c
 
 

time: 89.3 us -> 87.8 us (0.983)
  Pallas kernels: 29.6 us -> 28.5 us
    pallas_call x2, Pallas kernels: 9.43 us -> 6.91 us  [value_call(): pl.pallas_call(functools.partial(value_body, way), in_specs=[pl.BlockSpec...]
    pallas_call x10 -> x13, Pallas kernels: 5.6 us -> 7.41 us  [small(): pl.pallas_call(with_after, in_specs=[pl.BlockSpec(memory_space=pltpu.VMEM...]
    ppermute x16, waiting for transfers between devices: 23 us -> 21.5 us  [over_ctx(): return lax.ppermute(array, 'ctx', [(i, target(i)) for i in range(64)])]
    ppermute x6, waiting for transfers between devices: 1.25 us -> 2.5 us  [over_tp(): return lax.ppermute(array, 'tp', [(i, i ^ k) for i in range(4)])]
  transfers between devices with their start and end apart: 22 -> 22, of which waited for: 11 -> 13; matrix products, arithmetic and copies ran while one was open for 0% -> 0% of each run, Pallas kernels for 26% -> 25%
where the time goes in v2:
time: 87.8 us; the launch traced here: 87.4 us
  starting transfers between devices  34 us (39%)
  Pallas kernels  28.5 us (32%)
  waiting for transfers between devices  24 us (27%)
    ppermute x16, starting transfers between devices, over_ctx(): return lax.ppermute(array, 'ctx', [(i, target(i)) for i in range(64)])  26.5 us
    ppermute x16, waiting for transfers between devices, over_ctx(): return lax.ppermute(array, 'ctx', [(i, target(i)) for i in range(64)])  21.5 us
    pallas_call x2, Pallas kernels, intra(): pl.pallas_call(intra_body, grid=(1,), in_specs=[by_head, by_head, flat, f...  8.74 us
    ppermute x6, starting transfers between devices, over_tp(): return lax.ppermute(array, 'tp', [(i, i ^ k) for i in range(4)])  7.49 us
    pallas_call x13, Pallas kernels, small(): pl.pallas_call(with_after, in_specs=[pl.BlockSpec(memory_space=pltpu.VMEM...  7.41 us
    pallas_call x2, Pallas kernels, value_call(): pl.pallas_call(functools.partial(value_body, way), in_specs=[pl.BlockSpec...  6.91 us
    pallas_call x1, Pallas kernels, summary(): pl.pallas_call(summary_body, in_specs=[anywhere] * 3, out_shape=[jax.Shap...  3.72 us
    ppermute x6, waiting for transfers between devices, over_tp(): return lax.ppermute(array, 'tp', [(i, i ^ k) for i in range(4)])  2.5 us
  transfers between devices with their start and end apart: 22, of which 13 were waited for; matrix products, arithmetic and copies ran while one was open for 0% of the time, Pallas kernels for 25%

profile of v2, /device:TPU:1, one launch (start us, length us, event | category | flops | bytes accessed | tf_op | source)
XLA Modules:
  0.0 87.4 jit_solution(2668875194523428924)
XLA Ops:
  0.7 3.7 %summary_f.1 = (bf16[16,512,128]{2,1,0:T(8,128)(2,1)S(1)}, f32[8,136,128]{2,1,0:T(8,128)S(1)}, f32[8,136,128]{2,1,0:T(8,128)S(1)}, f32[16,128,128]{2,1,0:T(8,128...) custom-call(bf16[512,16,128]{2,1,0:T(8,128)(2,1)} %values.2, bf16[512,128]{1,0:T(8,128)(2,1)} %proj.5, ...), custom_call_target="tpu_custom_call" | custom-call | tf_op jit(solution)/shard_map/summary_f/pallas_call | solution.py:123
  4.4 3.3 %collective-permute-start = (f32[8,136,128]{2,1,0:T(8,128)S(1)}, f32[8,136,128]{2,1,0:T(8,128)S(1)}, u32[]{:S(2)}, u32[]{:S(2)}) collective-permute-start(f32[8,136,128]{2,1,0:T(8,128)S(1)} %get-tuple-element.57), channel_id=1, source_target_pairs={{0,4},{4,0},{8,12},{12,8},{16,20},{20,16},{24,28},{28,24},{32,36},... | collective-permute-start | bytes 1671176 | tf_op jit(solution)/shard_map/ppermute | solution.py:435
  7.7 1.7 %summary_b_send.1 = (bf16[16,512,128]{2,1,0:T(8,128)(2,1)S(1)}, f32[128,512]{1,0:T(8,128)S(1)}, f32[8,128,128]{2,1,0:T(8,128)S(1)}, f32[8,128,128]{2,1,0:T(8,128)S(1)}) custom-call(bf16[512,16,128]{2,1,0:T(8,128)(2,1)S(1)} %copy-done.2, bf16[512,128]{1,0:T(8,128)(2,1)S(1)} %copy-done, ...), custom_call_target="tpu_custom_call" | custom-call | tf_op jit(solution)/shard_map/summary_b_send/pallas_call | solution.py:181
  10.4 1.0 %collective-permute-done.1.refs_3_ = f32[8,128,128]{2,1,0:T(8,128)S(1)} collective-permute-done((f32[8,128,128]{2,1,0:T(8,128)S(1)}, f32[8,128,128]{2,1,0:T(8,128)S(1)}, u32[]{:S(2)}, u32[]{:S(2)}) %collective-permute-start.1) | collective-permute-done | bytes 524320 | tf_op jit(solution)/shard_map/ppermute | solution.py:435
  11.6 2.5 %collective-permute-start.2 = (f32[2,264,128]{2,1,0:T(8,128)S(1)}, f32[2,264,128]{2,1,0:T(8,128)S(1)}, u32[]{:S(2)}, u32[]{:S(2)}) collective-permute-start(f32[2,264,128]{2,1,0:T(8,128)S(1)} %get-tuple-element.64), channel_id=1, source_target_pairs={{0,16},{4,52},{8,24},{12,60},{16,0},{20,36},{24,8},{28,44},{32,48}... | collective-permute-start | bytes 811016 | tf_op jit(solution)/shard_map/ppermute | solution.py:435
  14.0 1.4 %collective-permute-start.4 = (f32[2,264,128]{2,1,0:T(8,128)S(1)}, f32[2,264,128]{2,1,0:T(8,128)S(1)}, u32[]{:S(2)}, u32[]{:S(2)}) collective-permute-start(f32[2,264,128]{2,1,0:T(8,128)S(1)} %get-tuple-element.66), channel_id=1, source_target_pairs={{0,24},{4,60},{8,16},{12,52},{16,8},{20,44},{24,0},{28,36},{32,56}... | collective-permute-start | bytes 811016 | tf_op jit(solution)/shard_map/ppermute | solution.py:435
  15.4 3.6 %collective-permute-start.5 = (f32[2,264,128]{2,1,0:T(8,128)S(1)}, f32[2,264,128]{2,1,0:T(8,128)S(1)}, u32[]{:S(2)}, u32[]{:S(2)}) collective-permute-start(f32[2,264,128]{2,1,0:T(8,128)S(1)} %get-tuple-element.67.refs_0_), channel_id=1, source_target_pairs={{0,0},{4,36},{8,8},{12,44},{16,16},{20,52},{24,24},{28,60},{32,32}... | collective-permute-start | bytes 811016 | tf_op jit(solution)/shard_map/ppermute | solution.py:435
  19.1 4.4 %intra0.1 = (f32[16,512,128]{2,1,0:T(8,128)S(1)}, f32[16,512,128]{2,1,0:T(8,128)S(1)}, bf16[16,128,512]{2,1,0:T(8,128)(2,1)S(1)}, bf16[16,128,512]{2,1,0:T(8,128...) custom-call(bf16[16,512,128]{2,1,0:T(8,128)(2,1)S(1)} %get-tuple-element.68.x_ref, ...), custom_call_target="tpu_custom_call" | custom-call | tf_op jit(solution)/shard_map/intra0/pallas_call | solution.py:258
  23.5 2.5 %collective-permute-done.4.refs_2_ = f32[2,264,128]{2,1,0:T(8,128)S(1)} collective-permute-done((f32[2,264,128]{2,1,0:T(8,128)S(1)}, f32[2,264,128]{2,1,0:T(8,128)S(1)}, u32[]{:S(2)}, u32[]{:S(2)}) %collective-permute-start.4) | collective-permute-done | bytes 270368 | tf_op jit(solution)/shard_map/ppermute | solution.py:435
  26.0 2.4 %collective-permute-done.5.refs_3_ = f32[2,264,128]{2,1,0:T(8,128)S(1)} collective-permute-done((f32[2,264,128]{2,1,0:T(8,128)S(1)}, f32[2,264,128]{2,1,0:T(8,128)S(1)}, u32[]{:S(2)}, u32[]{:S(2)}) %collective-permute-start.5) | collective-permute-done | bytes 270368 | tf_op jit(solution)/shard_map/ppermute | solution.py:435
  28.7 1.4 %collective-permute-done.6.refs_1_.refs_5_ = f32[2,264,128]{2,1,0:T(8,128)S(1)} collective-permute-done((f32[2,264,128]{2,1,0:T(8,128)S(1)}, f32[2,264,128]{2,1,0:T(8,128)S(1)}, u32[]{:S(2)}, u32[]{:S(2)}) %collective-permute-start.6) | collective-permute-done | bytes 270368 | tf_op jit(solution)/shard_map/ppermute | solution.py:435
  30.2 6.1 %collective-permute-start.8 = (f32[2,136,128]{2,1,0:T(8,128)S(1)}, f32[2,136,128]{2,1,0:T(8,128)S(1)}, u32[]{:S(2)}, u32[]{:S(2)}) collective-permute-start(f32[2,136,128]{2,1,0:T(8,128)S(1)} %get-tuple-element.72), channel_id=1, source_target_pairs={{0,64},{4,196},{8,72},{12,204},{16,80},{20,212},{24,88},{28,220},{... | collective-permute-start | bytes 417800 | tf_op jit(solution)/shard_map/ppermute | solution.py:435
  36.3 1.0 %collective-permute-start.7 = (f32[136,128]{1,0:T(8,128)S(1)}, f32[136,128]{1,0:T(8,128)S(1)}, u32[]{:S(2)}, u32[]{:S(2)}) collective-permute-start(f32[136,128]{1,0:T(8,128)S(1)} %get-tuple-element.71), channel_id=1, source_target_pairs={{0,128},{4,132},{8,136},{12,140},{16,144},{20,148},{24,152},{28,15... | collective-permute-start | bytes 208904 | tf_op jit(solution)/shard_map/ppermute | solution.py:435
  37.3 4.8 %collective-permute-done.8.refs_7_ = f32[2,136,128]{2,1,0:T(8,128)S(1)} collective-permute-done((f32[2,136,128]{2,1,0:T(8,128)S(1)}, f32[2,136,128]{2,1,0:T(8,128)S(1)}, u32[]{:S(2)}, u32[]{:S(2)}) %collective-permute-start.8) | collective-permute-done | bytes 139296 | tf_op jit(solution)/shard_map/ppermute | solution.py:435
  42.1 2.3 %collective-permute-done.7.refs_6_ = f32[136,128]{1,0:T(8,128)S(1)} collective-permute-done((f32[136,128]{1,0:T(8,128)S(1)}, f32[136,128]{1,0:T(8,128)S(1)}, u32[]{:S(2)}, u32[]{:S(2)}) %collective-permute-start.7) | collective-permute-done | bytes 69664 | tf_op jit(solution)/shard_map/ppermute | solution.py:435
  45.1 0.9 %collective-permute-done.9.refs_8_ = f32[136,128]{1,0:T(8,128)S(1)} collective-permute-done((f32[136,128]{1,0:T(8,128)S(1)}, f32[136,128]{1,0:T(8,128)S(1)}, u32[]{:S(2)}, u32[]{:S(2)}) %collective-permute-start.9) | collective-permute-done | bytes 69664 | tf_op jit(solution)/shard_map/ppermute | solution.py:435
  46.5 1.5 %collective-permute-start.11 = (f32[2,256,128]{2,1,0:T(8,128)S(1)}, f32[2,256,128]{2,1,0:T(8,128)S(1)}, u32[]{:S(2)}, u32[]{:S(2)}) collective-permute-start(f32[2,256,128]{2,1,0:T(8,128)S(1)} %get-tuple-element.73), channel_id=1, source_target_pairs={{0,16},{4,52},{8,24},{12,60},{16,0},{20,36},{24,8},{28,44},{32,48}... | collective-permute-start | bytes 786440 | tf_op jit(solution)/shard_map/ppermute | solution.py:435
  48.0 0.9 %collective-permute-start.12 = (f32[2,256,128]{2,1,0:T(8,128)S(1)}, f32[2,256,128]{2,1,0:T(8,128)S(1)}, u32[]{:S(2)}, u32[]{:S(2)}) collective-permute-start(f32[2,256,128]{2,1,0:T(8,128)S(1)} %get-tuple-element.74), channel_id=1, source_target_pairs={{0,8},{4,44},{8,0},{12,36},{16,24},{20,60},{24,16},{28,52},{32,40}... | collective-permute-start | bytes 786440 | tf_op jit(solution)/shard_map/ppermute | solution.py:435
  48.9 2.1 %collective-permute-start.13 = (f32[2,256,128]{2,1,0:T(8,128)S(1)}, f32[2,256,128]{2,1,0:T(8,128)S(1)}, u32[]{:S(2)}, u32[]{:S(2)}) collective-permute-start(f32[2,256,128]{2,1,0:T(8,128)S(1)} %get-tuple-element.75), channel_id=1, source_target_pairs={{0,24},{4,60},{8,16},{12,52},{16,8},{20,44},{24,0},{28,36},{32,56}... | collective-permute-start | bytes 786440 | tf_op jit(solution)/shard_map/ppermute | solution.py:435
  51.0 3.1 %collective-permute-start.14 = (f32[2,256,128]{2,1,0:T(8,128)S(1)}, f32[2,256,128]{2,1,0:T(8,128)S(1)}, u32[]{:S(2)}, u32[]{:S(2)}) collective-permute-start(f32[2,256,128]{2,1,0:T(8,128)S(1)} %get-tuple-element.76.refs_0_), channel_id=1, source_target_pairs={{0,0},{4,36},{8,8},{12,44},{16,16},{20,52},{24,24},{28,60},{32,32}... | collective-permute-start | bytes 786440 | tf_op jit(solution)/shard_map/ppermute | solution.py:435
  54.0 4.4 %intra1.1 = (f32[16,512,128]{2,1,0:T(8,128)S(1)}, f32[16,512,128]{2,1,0:T(8,128)S(1)}, bf16[16,128,512]{2,1,0:T(8,128)(2,1)S(1)}, bf16[16,128,512]{2,1,0:T(8,128...) custom-call(bf16[16,512,128]{2,1,0:T(8,128)(2,1)S(1)} %get-tuple-ele, ...), custom_call_target="tpu_custom_call", output_to_operand_aliasing={{0}: (8, {}), {1}: (9, {}), {2}: (10, {}), {3}: (11, {}), {... | custom-call | tf_op jit(solution)/shard_map/intra1/pallas_call | solution.py:258
  58.4 4.1 %collective-permute-done.13.refs_6_ = f32[2,256,128]{2,1,0:T(8,128)S(1)} collective-permute-done((f32[2,256,128]{2,1,0:T(8,128)S(1)}, f32[2,256,128]{2,1,0:T(8,128)S(1)}, u32[]{:S(2)}, u32[]{:S(2)}) %collective-permute-start.13) | collective-permute-done | bytes 262176 | tf_op jit(solution)/shard_map/ppermute | solution.py:435
  63.6 1.3 %grads_own.1 = (f32[256,512]{1,0:T(8,128)S(1)}, f32[8,512]{1,0:T(8,128)S(1)}) custom-call(f32[8,256,128]{2,1,0:T(8,128)S(1)} %get-tuple-element.84.refs_0_.mine.refs_1_, f32[16,128,128]{2,1,0:T(8,128)S(1)} %get-tuple-element.85.refs_1_.middle, f32[16,128,128]{2,1,0:T(8,128)S(1)} %get-tuple-element.87.refs_2_.middle, ...), custom_call_target="tpu_custom_call" | custom-call | tf_op jit(solution)/shard_map/grads_own/pallas_call | solution.py:293
  64.9 1.4 %collective-permute-done.15.refs_0_.got = f32[8,256,128]{2,1,0:T(8,128)S(1)} collective-permute-done((f32[8,256,128]{2,1,0:T(8,128)S(1)}, f32[8,256,128]{2,1,0:T(8,128)S(1)}, u32[]{:S(2)}, u32[]{:S(2)}) %collective-permute-start.15) | collective-permute-done | bytes 1048608 | tf_op jit(solution)/shard_map/ppermute | solution.py:435
  66.2 1.0 %grads_other.1 = (f32[128,256]{1,0:T(8,128)S(1)}, f32[128,256]{1,0:T(8,128)S(1)}, f32[128,256]{1,0:T(8,128)S(1)}, f32[128,256]{1,0:T(8,128)S(1)}) custom-call(f32[8,256,128]{2,1,0:T(8,128)S(1)} %collective-permute-done.15.refs_0_.got, f32[16,128,128]{2,1,0:T(8,128)S(1)} %get-tuple-element.85.refs_1_.middle, ...), custom_call_target="tpu_custom_call" | custom-call | tf_op jit(solution)/shard_map/grads_other/pallas_call | solution.py:293
  67.3 3.0 %collective-permute-start.16 = (f32[128,256]{1,0:T(8,128)S(1)}, f32[128,256]{1,0:T(8,128)S(1)}, u32[]{:S(2)}, u32[]{:S(2)}) collective-permute-start(f32[128,256]{1,0:T(8,128)S(1)} %get-tuple-element.95), channel_id=1, source_target_pairs={{0,2},{1,3},{2,0},{3,1},{4,6},{5,7},{6,4},{7,5},{8,10},{9,11},{10,... | collective-permute-start | bytes 393224 | tf_op jit(solution)/shard_map/ppermute | solution.py:609
  71.0 3.5 %values_f.1 = (bf16[512,16,128]{2,1,0:T(8,128)(2,1)}, f32[8,128]{1,0:T(8,128)S(1)}) custom-call(f32[8,256,128]{2,1,0:T(8,128)S(1)} %collective-permute-done.15.refs_0_.got, f32[8,256,128]{2,1,0:T(8,128)S(1)} %get-tuple-element.84.refs_0_.mine.refs_1_, f32[16,128,128]{2,1,0:T(8,128)S(1)} %get-tuple-element.85.refs_1_.middle, ...), custom_call_target="tpu_custom_call" | custom-call | tf_op jit(solution)/shard_map/values_f/pallas_call | solution.py:563
  75.1 1.0 %cross_other.1.refs_4_.refs_2_ = f32[8,512]{1,0:T(8,128)S(1)} custom-call(f32[8,256,128]{2,1,0:T(8,128)S(1)} %collective-permute-done.15.refs_0_.got, f32[16,128,128]{2,1,0:T(8,128)S(1)} %get-tuple-element.85.refs_1_.middle, f32[16,128,128]{2,1,0:T(8,128)S(1)} %get-tuple-element.87.refs_2_.middle, ...), custom_call_target="tpu_custom_call" | custom-call | tf_op jit(solution)/shard_map/cross_other/pallas_call | solution.py:293
  76.1 0.9 %collective-permute-done.17.refs_1_ = f32[128,256]{1,0:T(8,128)S(1)} collective-permute-done((f32[128,256]{1,0:T(8,128)S(1)}, f32[128,256]{1,0:T(8,128)S(1)}, u32[]{:S(2)}, u32[]{:S(2)}) %collective-permute-start.17) | collective-permute-done | bytes 131104 | tf_op jit(solution)/shard_map/ppermute | solution.py:609
  77.0 3.1 %collective-permute-start.21 = (f32[128,256]{1,0:T(8,128)S(1)}, f32[128,256]{1,0:T(8,128)S(1)}, u32[]{:S(2)}, u32[]{:S(2)}) collective-permute-start(f32[128,256]{1,0:T(8,128)S(1)} %add.1._.refs_0_), channel_id=1, source_target_pairs={{0,2},{1,3},{2,0},{3,1},{4,6},{5,7},{6,4},{7,5},{8,10},{9,11},{10,... | collective-permute-start | bytes 393224 | tf_op jit(solution)/shard_map/ppermute | solution.py:609
  80.7 3.4 %values_b.1 = (bf16[512,16,128]{2,1,0:T(8,128)(2,1)}, f32[8,128]{1,0:T(8,128)S(1)}) custom-call(f32[8,256,128]{2,1,0:T(8,128)S(1)} %collective-permute-done.15.refs_0_.got, f32[8,256,128]{2,1,0:T(8,128)S(1)} %get-tuple-element.84.refs_0_.mine.refs_1_, f32[16,128,128]{2,1,0:T(8,128)S(1)} %get-tuple-element.87.refs_2_.middle, ...), custom_call_target="tpu_custom_call" | custom-call | tf_op jit(solution)/shard_map/values_b/pallas_call | solution.py:563
  84.9 1.5 %collective-permute-done.20.refs_2_ = f32[128,256]{1,0:T(8,128)S(1)} collective-permute-done((f32[128,256]{1,0:T(8,128)S(1)}, f32[128,256]{1,0:T(8,128)S(1)}, u32[]{:S(2)}, u32[]{:S(2)}) %collective-permute-start.20) | collective-permute-done | bytes 131104 | tf_op jit(solution)/shard_map/ppermute | solution.py:609
  (39 shorter events, 7.3 us)
Async XLA Ops:
  0.6 7.1 %copy-start = (bf16[512,128]{1,0:T(8,128)(2,1)S(1)}, bf16[512,128]{1,0:T(8,128)(2,1)}, u32[]{:S(2)}) copy-start(bf16[512,128]{1,0:T(8,128)(2,1)} %proj.4) | copy-start | bytes 393220
  0.6 7.1 %copy-start.2 = (bf16[512,16,128]{2,1,0:T(8,128)(2,1)S(1)}, bf16[512,16,128]{2,1,0:T(8,128)(2,1)}, u32[]{:S(2)}) copy-start(bf16[512,16,128]{2,1,0:T(8,128)(2,1)} %values.3) | copy-start | bytes 6291460
  4.4 7.0 %collective-permute-start = (f32[8,136,128]{2,1,0:T(8,128)S(1)}, f32[8,136,128]{2,1,0:T(8,128)S(1)}, u32[]{:S(2)}, u32[]{:S(2)}) collective-permute-start(f32[8,136,128]{2,1,0:T(8,128)S(1)} %get-tuple-element.57), channel_id=1, source_target_pairs={{0,4},{4,0},{8,12},{12,8},{16,20},{20,16},{24,28},{28,24},{32,36},... | collective-permute-start | bytes 1671176 | tf_op jit(solution)/shard_map/ppermute | solution.py:435
  9.4 2.0 %collective-permute-start.1 = (f32[8,128,128]{2,1,0:T(8,128)S(1)}, f32[8,128,128]{2,1,0:T(8,128)S(1)}, u32[]{:S(2)}, u32[]{:S(2)}) collective-permute-start(f32[8,128,128]{2,1,0:T(8,128)S(1)} %get-tuple-element.63.refs_2_), channel_id=1, source_target_pairs={{0,4},{4,0},{8,12},{12,8},{16,20},{20,16},{24,28},{28,24},{32,36},... | collective-permute-start | bytes 1572872 | tf_op jit(solution)/shard_map/ppermute | solution.py:435
  9.5 9.5 %copy-start.1 = (bf16[512,128]{1,0:T(8,128)(2,1)S(1)}, bf16[512,128]{1,0:T(8,128)(2,1)}, u32[]{:S(2)}) copy-start(bf16[512,128]{1,0:T(8,128)(2,1)} %proj.5) | copy-start | bytes 393220
  9.5 9.6 %copy-start.3 = (f32[16]{0:T(128)S(1)}, f32[16]{0:T(128)}, u32[]{:S(2)}) copy-start(f32[16]{0:T(128)} %param.10) | copy-start | bytes 196
  11.6 11.9 %collective-permute-start.2 = (f32[2,264,128]{2,1,0:T(8,128)S(1)}, f32[2,264,128]{2,1,0:T(8,128)S(1)}, u32[]{:S(2)}, u32[]{:S(2)}) collective-permute-start(f32[2,264,128]{2,1,0:T(8,128)S(1)} %get-tuple-element.64), channel_id=1, source_target_pairs={{0,16},{4,52},{8,24},{12,60},{16,0},{20,36},{24,8},{28,44},{32,48}... | collective-permute-start | bytes 811016 | tf_op jit(solution)/shard_map/ppermute | solution.py:435
  14.0 9.5 %collective-permute-start.3 = (f32[2,264,128]{2,1,0:T(8,128)S(1)}, f32[2,264,128]{2,1,0:T(8,128)S(1)}, u32[]{:S(2)}, u32[]{:S(2)}) collective-permute-start(f32[2,264,128]{2,1,0:T(8,128)S(1)} %get-tuple-element.65), channel_id=1, source_target_pairs={{0,8},{4,44},{8,0},{12,36},{16,24},{20,60},{24,16},{28,52},{32,40}... | collective-permute-start | bytes 811016 | tf_op jit(solution)/shard_map/ppermute | solution.py:435
  14.0 11.9 %collective-permute-start.4 = (f32[2,264,128]{2,1,0:T(8,128)S(1)}, f32[2,264,128]{2,1,0:T(8,128)S(1)}, u32[]{:S(2)}, u32[]{:S(2)}) collective-permute-start(f32[2,264,128]{2,1,0:T(8,128)S(1)} %get-tuple-element.66), channel_id=1, source_target_pairs={{0,24},{4,60},{8,16},{12,52},{16,8},{20,44},{24,0},{28,36},{32,56}... | collective-permute-start | bytes 811016 | tf_op jit(solution)/shard_map/ppermute | solution.py:435
  15.4 12.9 %collective-permute-start.5 = (f32[2,264,128]{2,1,0:T(8,128)S(1)}, f32[2,264,128]{2,1,0:T(8,128)S(1)}, u32[]{:S(2)}, u32[]{:S(2)}) collective-permute-start(f32[2,264,128]{2,1,0:T(8,128)S(1)} %get-tuple-element.67.refs_0_), channel_id=1, source_target_pairs={{0,0},{4,36},{8,8},{12,44},{16,16},{20,52},{24,24},{28,60},{32,32}... | collective-permute-start | bytes 811016 | tf_op jit(solution)/shard_map/ppermute | solution.py:435
  28.5 1.6 %collective-permute-start.6 = (f32[2,264,128]{2,1,0:T(8,128)S(1)}, f32[2,264,128]{2,1,0:T(8,128)S(1)}, u32[]{:S(2)}, u32[]{:S(2)}) collective-permute-start(f32[2,264,128]{2,1,0:T(8,128)S(1)} %slab_up.1.refs_0_.refs_4_), channel_id=1, source_target_pairs={{0,4},{4,0},{8,12},{12,8},{16,20},{20,16},{24,28},{28,24},{32,36},... | collective-permute-start | bytes 811016 | tf_op jit(solution)/shard_map/ppermute | solution.py:435
  30.2 11.9 %collective-permute-start.8 = (f32[2,136,128]{2,1,0:T(8,128)S(1)}, f32[2,136,128]{2,1,0:T(8,128)S(1)}, u32[]{:S(2)}, u32[]{:S(2)}) collective-permute-start(f32[2,136,128]{2,1,0:T(8,128)S(1)} %get-tuple-element.72), channel_id=1, source_target_pairs={{0,64},{4,196},{8,72},{12,204},{16,80},{20,212},{24,88},{28,220},{... | collective-permute-start | bytes 417800 | tf_op jit(solution)/shard_map/ppermute | solution.py:435
  36.3 8.2 %collective-permute-start.7 = (f32[136,128]{1,0:T(8,128)S(1)}, f32[136,128]{1,0:T(8,128)S(1)}, u32[]{:S(2)}, u32[]{:S(2)}) collective-permute-start(f32[136,128]{1,0:T(8,128)S(1)} %get-tuple-element.71), channel_id=1, source_target_pairs={{0,128},{4,132},{8,136},{12,140},{16,144},{20,148},{24,152},{28,15... | collective-permute-start | bytes 208904 | tf_op jit(solution)/shard_map/ppermute | solution.py:435
  42.1 3.9 %collective-permute-start.10 = (f32[2,136,128]{2,1,0:T(8,128)S(1)}, f32[2,136,128]{2,1,0:T(8,128)S(1)}, u32[]{:S(2)}, u32[]{:S(2)}) collective-permute-start(f32[2,136,128]{2,1,0:T(8,128)S(1)} %collective-permute-done.8.refs_7_), channel_id=1, source_target_pairs={{0,4},{4,0},{8,12},{12,8},{16,20},{20,16},{24,28},{28,24},{32,36},... | collective-permute-start | bytes 417800 | tf_op jit(solution)/shard_map/ppermute | solution.py:435
  44.5 1.6 %collective-permute-start.9 = (f32[136,128]{1,0:T(8,128)S(1)}, f32[136,128]{1,0:T(8,128)S(1)}, u32[]{:S(2)}, u32[]{:S(2)}) collective-permute-start(f32[136,128]{1,0:T(8,128)S(1)} %collective-permute-done.7.refs_6_), channel_id=1, source_target_pairs={{0,4},{4,0},{8,12},{12,8},{16,20},{20,16},{24,28},{28,24},{32,36},... | collective-permute-start | bytes 208904 | tf_op jit(solution)/shard_map/ppermute | solution.py:435
  46.5 11.9 %collective-permute-start.11 = (f32[2,256,128]{2,1,0:T(8,128)S(1)}, f32[2,256,128]{2,1,0:T(8,128)S(1)}, u32[]{:S(2)}, u32[]{:S(2)}) collective-permute-start(f32[2,256,128]{2,1,0:T(8,128)S(1)} %get-tuple-element.73), channel_id=1, source_target_pairs={{0,16},{4,52},{8,24},{12,60},{16,0},{20,36},{24,8},{28,44},{32,48}... | collective-permute-start | bytes 786440 | tf_op jit(solution)/shard_map/ppermute | solution.py:435
  48.0 10.4 %collective-permute-start.12 = (f32[2,256,128]{2,1,0:T(8,128)S(1)}, f32[2,256,128]{2,1,0:T(8,128)S(1)}, u32[]{:S(2)}, u32[]{:S(2)}) collective-permute-start(f32[2,256,128]{2,1,0:T(8,128)S(1)} %get-tuple-element.74), channel_id=1, source_target_pairs={{0,8},{4,44},{8,0},{12,36},{16,24},{20,60},{24,16},{28,52},{32,40}... | collective-permute-start | bytes 786440 | tf_op jit(solution)/shard_map/ppermute | solution.py:435
  48.9 13.6 %collective-permute-start.13 = (f32[2,256,128]{2,1,0:T(8,128)S(1)}, f32[2,256,128]{2,1,0:T(8,128)S(1)}, u32[]{:S(2)}, u32[]{:S(2)}) collective-permute-start(f32[2,256,128]{2,1,0:T(8,128)S(1)} %get-tuple-element.75), channel_id=1, source_target_pairs={{0,24},{4,60},{8,16},{12,52},{16,8},{20,44},{24,0},{28,36},{32,56}... | collective-permute-start | bytes 786440 | tf_op jit(solution)/shard_map/ppermute | solution.py:435
  51.0 12.2 %collective-permute-start.14 = (f32[2,256,128]{2,1,0:T(8,128)S(1)}, f32[2,256,128]{2,1,0:T(8,128)S(1)}, u32[]{:S(2)}, u32[]{:S(2)}) collective-permute-start(f32[2,256,128]{2,1,0:T(8,128)S(1)} %get-tuple-element.76.refs_0_), channel_id=1, source_target_pairs={{0,0},{4,36},{8,8},{12,44},{16,16},{20,52},{24,24},{28,60},{32,32}... | collective-permute-start | bytes 786440 | tf_op jit(solution)/shard_map/ppermute | solution.py:435
  63.5 2.7 %collective-permute-start.15 = (f32[8,256,128]{2,1,0:T(8,128)S(1)}, f32[8,256,128]{2,1,0:T(8,128)S(1)}, u32[]{:S(2)}, u32[]{:S(2)}) collective-permute-start(f32[8,256,128]{2,1,0:T(8,128)S(1)} %get-tuple-element.83), channel_id=1, source_target_pairs={{0,4},{4,0},{8,12},{12,8},{16,20},{20,16},{24,28},{28,24},{32,36},... | collective-permute-start | bytes 3145736 | tf_op jit(solution)/shard_map/ppermute | solution.py:435
  67.3 8.8 %collective-permute-start.16 = (f32[128,256]{1,0:T(8,128)S(1)}, f32[128,256]{1,0:T(8,128)S(1)}, u32[]{:S(2)}, u32[]{:S(2)}) collective-permute-start(f32[128,256]{1,0:T(8,128)S(1)} %get-tuple-element.95), channel_id=1, source_target_pairs={{0,2},{1,3},{2,0},{3,1},{4,6},{5,7},{6,4},{7,5},{8,10},{9,11},{10,... | collective-permute-start | bytes 393224 | tf_op jit(solution)/shard_map/ppermute | solution.py:609
  70.3 6.7 %collective-permute-start.17 = (f32[128,256]{1,0:T(8,128)S(1)}, f32[128,256]{1,0:T(8,128)S(1)}, u32[]{:S(2)}, u32[]{:S(2)}) collective-permute-start(f32[128,256]{1,0:T(8,128)S(1)} %get-tuple-element.96), channel_id=1, source_target_pairs={{0,1},{1,0},{2,3},{3,2},{4,5},{5,4},{6,7},{7,6},{8,9},{9,8},{10,11... | collective-permute-start | bytes 393224 | tf_op jit(solution)/shard_map/ppermute | solution.py:609
  70.7 6.3 %collective-permute-start.18 = (f32[128,256]{1,0:T(8,128)S(1)}, f32[128,256]{1,0:T(8,128)S(1)}, u32[]{:S(2)}, u32[]{:S(2)}) collective-permute-start(f32[128,256]{1,0:T(8,128)S(1)} %get-tuple-element.97), channel_id=1, source_target_pairs={{0,3},{1,2},{2,1},{3,0},{4,7},{5,6},{6,5},{7,4},{8,11},{9,10},{10,... | collective-permute-start | bytes 393224 | tf_op jit(solution)/shard_map/ppermute | solution.py:609
  77.0 7.9 %collective-permute-start.21 = (f32[128,256]{1,0:T(8,128)S(1)}, f32[128,256]{1,0:T(8,128)S(1)}, u32[]{:S(2)}, u32[]{:S(2)}) collective-permute-start(f32[128,256]{1,0:T(8,128)S(1)} %add.1._.refs_0_), channel_id=1, source_target_pairs={{0,2},{1,3},{2,0},{3,1},{4,6},{5,7},{6,4},{7,5},{8,10},{9,11},{10,... | collective-permute-start | bytes 393224 | tf_op jit(solution)/shard_map/ppermute | solution.py:609
  80.1 6.3 %collective-permute-start.20 = (f32[128,256]{1,0:T(8,128)S(1)}, f32[128,256]{1,0:T(8,128)S(1)}, u32[]{:S(2)}, u32[]{:S(2)}) collective-permute-start(f32[128,256]{1,0:T(8,128)S(1)} %add.1._.refs_0_), channel_id=1, source_target_pairs={{0,1},{1,0},{2,3},{3,2},{4,5},{5,4},{6,7},{7,6},{8,9},{9,8},{10,11... | collective-permute-start | bytes 393224 | tf_op jit(solution)/shard_map/ppermute | solution.py:609
  80.5 6.0 %collective-permute-start.19 = (f32[128,256]{1,0:T(8,128)S(1)}, f32[128,256]{1,0:T(8,128)S(1)}, u32[]{:S(2)}, u32[]{:S(2)}) collective-permute-start(f32[128,256]{1,0:T(8,128)S(1)} %add.1._.refs_0_), channel_id=1, source_target_pairs={{0,3},{1,2},{2,1},{3,0},{4,7},{5,6},{6,5},{7,4},{8,11},{9,10},{10,... | collective-permute-start | bytes 393224 | tf_op jit(solution)/shard_map/ppermute | solution.py:609

commit v3 on v2

--- a/solution.py
+++ b/solution.py
@@ -332,7 +332,7 @@
     return befores, entering
 
 
-TAKEN = (2, 1, 3, 0)
+TAKEN = (1, 3, 2, 0)
 
 
 def taken(parts):
@@ -613,7 +613,7 @@
     out[...] = p0[...] + p1[...] + p2[...] + p3[...]
 
 
-def join_body(p0, p3, p1, p2, c_out, b_out):
+def join_body(p0, p2, p3, p1, c_out, b_out):
     mine = lax.axis_index("tp")
     for k, piece in enumerate((p0, p1, p2, p3)):
         rows = pl.ds(pl.multiple_of(jnp.bitwise_xor(mine, k) * 128, 128), 128)

time: 87.8 us -> 85.9 us (0.978)
  waiting for transfers between devices: 24 us -> 18.7 us
  starting transfers between devices: 34 us -> 37.7 us
    ppermute x16, waiting for transfers between devices: 21.5 us -> 16.8 us  [over_ctx(): return lax.ppermute(array, 'ctx', [(i, target(i)) for i in range(64)])]
    ppermute x16, starting transfers between devices: 26.5 us -> 30.3 us  [over_ctx(): return lax.ppermute(array, 'ctx', [(i, target(i)) for i in range(64)])]
  transfers between devices with their start and end apart: 22 -> 22, of which waited for: 13 -> 12; matrix products, arithmetic and copies ran while one was open for 0% -> 0% of each run, Pallas kernels for 25% -> 25%
where the time goes in v3:
time: 85.9 us; the launch traced here: 85.8 us
  starting transfers between devices  37.7 us (44%)
  Pallas kernels  28.5 us (33%)
  waiting for transfers between devices  18.7 us (22%)
  between operations  0.87 us (1%)
    ppermute x16, starting transfers between devices, over_ctx(): return lax.ppermute(array, 'ctx', [(i, target(i)) for i in range(64)])  30.3 us
    ppermute x16, waiting for transfers between devices, over_ctx(): return lax.ppermute(array, 'ctx', [(i, target(i)) for i in range(64)])  16.8 us
    pallas_call x2, Pallas kernels, intra(): pl.pallas_call(intra_body, grid=(1,), in_specs=[by_head, by_head, flat, f...  8.74 us
    pallas_call x13, Pallas kernels, small(): pl.pallas_call(with_after, in_specs=[pl.BlockSpec(memory_space=pltpu.VMEM...  7.39 us
    ppermute x6, starting transfers between devices, over_tp(): return lax.ppermute(array, 'tp', [(i, i ^ k) for i in range(4)])  7.35 us
    pallas_call x2, Pallas kernels, value_call(): pl.pallas_call(functools.partial(value_body, way), in_specs=[pl.BlockSpec...  6.92 us
    pallas_call x1, Pallas kernels, summary(): pl.pallas_call(summary_body, in_specs=[anywhere] * 3, out_shape=[jax.Shap...  3.72 us
    ppermute x6, waiting for transfers between devices, over_tp(): return lax.ppermute(array, 'tp', [(i, i ^ k) for i in range(4)])  1.91 us
  transfers between devices with their start and end apart: 22, of which 12 were waited for; matrix products, arithmetic and copies ran while one was open for 0% of the time, Pallas kernels for 25%

profile of v3, /device:TPU:1, one launch (start us, length us, event | category | flops | bytes accessed | tf_op | source)
XLA Modules:
  0.0 85.8 jit_solution(1751703299512150399)
XLA Ops:
  0.7 3.7 %summary_f.1 = (bf16[16,512,128]{2,1,0:T(8,128)(2,1)S(1)}, f32[8,136,128]{2,1,0:T(8,128)S(1)}, f32[8,136,128]{2,1,0:T(8,128)S(1)}, f32[16,128,128]{2,1,0:T(8,128...) custom-call(bf16[512,16,128]{2,1,0:T(8,128)(2,1)} %values.2, bf16[512,128]{1,0:T(8,128)(2,1)} %proj.5, ...), custom_call_target="tpu_custom_call" | custom-call | tf_op jit(solution)/shard_map/summary_f/pallas_call | solution.py:123
  4.4 3.3 %collective-permute-start = (f32[8,136,128]{2,1,0:T(8,128)S(1)}, f32[8,136,128]{2,1,0:T(8,128)S(1)}, u32[]{:S(2)}, u32[]{:S(2)}) collective-permute-start(f32[8,136,128]{2,1,0:T(8,128)S(1)} %get-tuple-element.57), channel_id=1, source_target_pairs={{0,4},{4,0},{8,12},{12,8},{16,20},{20,16},{24,28},{28,24},{32,36},... | collective-permute-start | bytes 1671176 | tf_op jit(solution)/shard_map/ppermute | solution.py:435
  7.7 1.7 %summary_b_send.1 = (bf16[16,512,128]{2,1,0:T(8,128)(2,1)S(1)}, f32[128,512]{1,0:T(8,128)S(1)}, f32[8,128,128]{2,1,0:T(8,128)S(1)}, f32[8,128,128]{2,1,0:T(8,128)S(1)}) custom-call(bf16[512,16,128]{2,1,0:T(8,128)(2,1)S(1)} %copy-done.2, bf16[512,128]{1,0:T(8,128)(2,1)S(1)} %copy-done, ...), custom_call_target="tpu_custom_call" | custom-call | tf_op jit(solution)/shard_map/summary_b_send/pallas_call | solution.py:181
  10.4 1.0 %collective-permute-done.1.refs_3_ = f32[8,128,128]{2,1,0:T(8,128)S(1)} collective-permute-done((f32[8,128,128]{2,1,0:T(8,128)S(1)}, f32[8,128,128]{2,1,0:T(8,128)S(1)}, u32[]{:S(2)}, u32[]{:S(2)}) %collective-permute-start.1) | collective-permute-done | bytes 524320 | tf_op jit(solution)/shard_map/ppermute | solution.py:435
  12.5 1.4 %collective-permute-start.3 = (f32[2,264,128]{2,1,0:T(8,128)S(1)}, f32[2,264,128]{2,1,0:T(8,128)S(1)}, u32[]{:S(2)}, u32[]{:S(2)}) collective-permute-start(f32[2,264,128]{2,1,0:T(8,128)S(1)} %get-tuple-element.65), channel_id=1, source_target_pairs={{0,24},{4,60},{8,16},{12,52},{16,8},{20,44},{24,0},{28,36},{32,56}... | collective-permute-start | bytes 811016 | tf_op jit(solution)/shard_map/ppermute | solution.py:435
  13.8 1.6 %collective-permute-start.4 = (f32[2,264,128]{2,1,0:T(8,128)S(1)}, f32[2,264,128]{2,1,0:T(8,128)S(1)}, u32[]{:S(2)}, u32[]{:S(2)}) collective-permute-start(f32[2,264,128]{2,1,0:T(8,128)S(1)} %get-tuple-element.66), channel_id=1, source_target_pairs={{0,16},{4,52},{8,24},{12,60},{16,0},{20,36},{24,8},{28,44},{32,48}... | collective-permute-start | bytes 811016 | tf_op jit(solution)/shard_map/ppermute | solution.py:435
  15.4 3.6 %collective-permute-start.5 = (f32[2,264,128]{2,1,0:T(8,128)S(1)}, f32[2,264,128]{2,1,0:T(8,128)S(1)}, u32[]{:S(2)}, u32[]{:S(2)}) collective-permute-start(f32[2,264,128]{2,1,0:T(8,128)S(1)} %get-tuple-element.67.refs_0_), channel_id=1, source_target_pairs={{0,0},{4,36},{8,8},{12,44},{16,16},{20,52},{24,24},{28,60},{32,32}... | collective-permute-start | bytes 811016 | tf_op jit(solution)/shard_map/ppermute | solution.py:435
  19.1 4.4 %intra0.1 = (f32[16,512,128]{2,1,0:T(8,128)S(1)}, f32[16,512,128]{2,1,0:T(8,128)S(1)}, bf16[16,128,512]{2,1,0:T(8,128)(2,1)S(1)}, bf16[16,128,512]{2,1,0:T(8,128...) custom-call(bf16[16,512,128]{2,1,0:T(8,128)(2,1)S(1)} %get-tuple-element.68.x_ref, ...), custom_call_target="tpu_custom_call" | custom-call | tf_op jit(solution)/shard_map/intra0/pallas_call | solution.py:258
  24.4 2.1 %collective-permute-done.5.refs_3_ = f32[2,264,128]{2,1,0:T(8,128)S(1)} collective-permute-done((f32[2,264,128]{2,1,0:T(8,128)S(1)}, f32[2,264,128]{2,1,0:T(8,128)S(1)}, u32[]{:S(2)}, u32[]{:S(2)}) %collective-permute-start.5) | collective-permute-done | bytes 270368 | tf_op jit(solution)/shard_map/ppermute | solution.py:435
  26.6 1.9 %collective-permute-start.6 = (f32[2,264,128]{2,1,0:T(8,128)S(1)}, f32[2,264,128]{2,1,0:T(8,128)S(1)}, u32[]{:S(2)}, u32[]{:S(2)}) collective-permute-start(f32[2,264,128]{2,1,0:T(8,128)S(1)} %slab_up.1.refs_0_.refs_4_), channel_id=1, source_target_pairs={{0,4},{4,0},{8,12},{12,8},{16,20},{20,16},{24,28},{28,24},{32,36},... | collective-permute-start | bytes 811016 | tf_op jit(solution)/shard_map/ppermute | solution.py:435
  28.5 1.2 %collective-permute-done.6.refs_1_.refs_5_ = f32[2,264,128]{2,1,0:T(8,128)S(1)} collective-permute-done((f32[2,264,128]{2,1,0:T(8,128)S(1)}, f32[2,264,128]{2,1,0:T(8,128)S(1)}, u32[]{:S(2)}, u32[]{:S(2)}) %collective-permute-start.6) | collective-permute-done | bytes 270368 | tf_op jit(solution)/shard_map/ppermute | solution.py:435
  29.8 5.8 %collective-permute-start.8 = (f32[2,136,128]{2,1,0:T(8,128)S(1)}, f32[2,136,128]{2,1,0:T(8,128)S(1)}, u32[]{:S(2)}, u32[]{:S(2)}) collective-permute-start(f32[2,136,128]{2,1,0:T(8,128)S(1)} %get-tuple-element.72), channel_id=1, source_target_pairs={{0,64},{4,196},{8,72},{12,204},{16,80},{20,212},{24,88},{28,220},{... | collective-permute-start | bytes 417800 | tf_op jit(solution)/shard_map/ppermute | solution.py:435
  35.5 1.0 %collective-permute-start.7 = (f32[136,128]{1,0:T(8,128)S(1)}, f32[136,128]{1,0:T(8,128)S(1)}, u32[]{:S(2)}, u32[]{:S(2)}) collective-permute-start(f32[136,128]{1,0:T(8,128)S(1)} %get-tuple-element.71), channel_id=1, source_target_pairs={{0,128},{4,132},{8,136},{12,140},{16,144},{20,148},{24,152},{28,15... | collective-permute-start | bytes 208904 | tf_op jit(solution)/shard_map/ppermute | solution.py:435
  36.5 4.8 %collective-permute-done.8.refs_7_ = f32[2,136,128]{2,1,0:T(8,128)S(1)} collective-permute-done((f32[2,136,128]{2,1,0:T(8,128)S(1)}, f32[2,136,128]{2,1,0:T(8,128)S(1)}, u32[]{:S(2)}, u32[]{:S(2)}) %collective-permute-start.8) | collective-permute-done | bytes 139296 | tf_op jit(solution)/shard_map/ppermute | solution.py:435
  41.3 2.6 %collective-permute-done.7.refs_6_ = f32[136,128]{1,0:T(8,128)S(1)} collective-permute-done((f32[136,128]{1,0:T(8,128)S(1)}, f32[136,128]{1,0:T(8,128)S(1)}, u32[]{:S(2)}, u32[]{:S(2)}) %collective-permute-start.7) | collective-permute-done | bytes 69664 | tf_op jit(solution)/shard_map/ppermute | solution.py:435
  46.5 2.0 %collective-permute-start.12 = (f32[2,256,128]{2,1,0:T(8,128)S(1)}, f32[2,256,128]{2,1,0:T(8,128)S(1)}, u32[]{:S(2)}, u32[]{:S(2)}) collective-permute-start(f32[2,256,128]{2,1,0:T(8,128)S(1)} %get-tuple-element.74), channel_id=1, source_target_pairs={{0,24},{4,60},{8,16},{12,52},{16,8},{20,44},{24,0},{28,36},{32,56}... | collective-permute-start | bytes 786440 | tf_op jit(solution)/shard_map/ppermute | solution.py:435
  48.5 1.6 %collective-permute-start.13 = (f32[2,256,128]{2,1,0:T(8,128)S(1)}, f32[2,256,128]{2,1,0:T(8,128)S(1)}, u32[]{:S(2)}, u32[]{:S(2)}) collective-permute-start(f32[2,256,128]{2,1,0:T(8,128)S(1)} %get-tuple-element.75), channel_id=1, source_target_pairs={{0,16},{4,52},{8,24},{12,60},{16,0},{20,36},{24,8},{28,44},{32,48}... | collective-permute-start | bytes 786440 | tf_op jit(solution)/shard_map/ppermute | solution.py:435
  50.2 3.3 %collective-permute-start.14 = (f32[2,256,128]{2,1,0:T(8,128)S(1)}, f32[2,256,128]{2,1,0:T(8,128)S(1)}, u32[]{:S(2)}, u32[]{:S(2)}) collective-permute-start(f32[2,256,128]{2,1,0:T(8,128)S(1)} %get-tuple-element.76.refs_0_), channel_id=1, source_target_pairs={{0,0},{4,36},{8,8},{12,44},{16,16},{20,52},{24,24},{28,60},{32,32}... | collective-permute-start | bytes 786440 | tf_op jit(solution)/shard_map/ppermute | solution.py:435
  53.4 4.4 %intra1.1 = (f32[16,512,128]{2,1,0:T(8,128)S(1)}, f32[16,512,128]{2,1,0:T(8,128)S(1)}, bf16[16,128,512]{2,1,0:T(8,128)(2,1)S(1)}, bf16[16,128,512]{2,1,0:T(8,128...) custom-call(bf16[16,512,128]{2,1,0:T(8,128)(2,1)S(1)} %get-tuple-ele, ...), custom_call_target="tpu_custom_call", output_to_operand_aliasing={{0}: (8, {}), {1}: (9, {}), {2}: (10, {}), {3}: (11, {}), {... | custom-call | tf_op jit(solution)/shard_map/intra1/pallas_call | solution.py:258
  57.8 1.6 %collective-permute-done.13.refs_6_ = f32[2,256,128]{2,1,0:T(8,128)S(1)} collective-permute-done((f32[2,256,128]{2,1,0:T(8,128)S(1)}, f32[2,256,128]{2,1,0:T(8,128)S(1)}, u32[]{:S(2)}, u32[]{:S(2)}) %collective-permute-start.13) | collective-permute-done | bytes 262176 | tf_op jit(solution)/shard_map/ppermute | solution.py:435
  60.5 2.6 %collective-permute-start.15 = (f32[8,256,128]{2,1,0:T(8,128)S(1)}, f32[8,256,128]{2,1,0:T(8,128)S(1)}, u32[]{:S(2)}, u32[]{:S(2)}) collective-permute-start(f32[8,256,128]{2,1,0:T(8,128)S(1)} %get-tuple-element.83), channel_id=1, source_target_pairs={{0,4},{4,0},{8,12},{12,8},{16,20},{20,16},{24,28},{28,24},{32,36},... | collective-permute-start | bytes 3145736 | tf_op jit(solution)/shard_map/ppermute | solution.py:435
  63.1 1.3 %grads_own.1 = (f32[256,512]{1,0:T(8,128)S(1)}, f32[8,512]{1,0:T(8,128)S(1)}) custom-call(f32[8,256,128]{2,1,0:T(8,128)S(1)} %get-tuple-element.84.refs_0_.mine.refs_1_, f32[16,128,128]{2,1,0:T(8,128)S(1)} %get-tuple-element.85.refs_1_.middle, f32[16,128,128]{2,1,0:T(8,128)S(1)} %get-tuple-element.87.refs_2_.middle, ...), custom_call_target="tpu_custom_call" | custom-call | tf_op jit(solution)/shard_map/grads_own/pallas_call | solution.py:293
  64.3 1.0 %collective-permute-done.15.refs_0_.got = f32[8,256,128]{2,1,0:T(8,128)S(1)} collective-permute-done((f32[8,256,128]{2,1,0:T(8,128)S(1)}, f32[8,256,128]{2,1,0:T(8,128)S(1)}, u32[]{:S(2)}, u32[]{:S(2)}) %collective-permute-start.15) | collective-permute-done | bytes 1048608 | tf_op jit(solution)/shard_map/ppermute | solution.py:435
  65.3 1.0 %grads_other.1 = (f32[128,256]{1,0:T(8,128)S(1)}, f32[128,256]{1,0:T(8,128)S(1)}, f32[128,256]{1,0:T(8,128)S(1)}, f32[128,256]{1,0:T(8,128)S(1)}) custom-call(f32[8,256,128]{2,1,0:T(8,128)S(1)} %collective-permute-done.15.refs_0_.got, f32[16,128,128]{2,1,0:T(8,128)S(1)} %get-tuple-element.85.refs_1_.middle, ...), custom_call_target="tpu_custom_call" | custom-call | tf_op jit(solution)/shard_map/grads_other/pallas_call | solution.py:293
  66.4 1.4 %collective-permute-start.16 = (f32[128,256]{1,0:T(8,128)S(1)}, f32[128,256]{1,0:T(8,128)S(1)}, u32[]{:S(2)}, u32[]{:S(2)}) collective-permute-start(f32[128,256]{1,0:T(8,128)S(1)} %get-tuple-element.95), channel_id=1, source_target_pairs={{0,1},{1,0},{2,3},{3,2},{4,5},{5,4},{6,7},{7,6},{8,9},{9,8},{10,11... | collective-permute-start | bytes 393224 | tf_op jit(solution)/shard_map/ppermute | solution.py:609
  67.8 1.9 %collective-permute-start.17 = (f32[128,256]{1,0:T(8,128)S(1)}, f32[128,256]{1,0:T(8,128)S(1)}, u32[]{:S(2)}, u32[]{:S(2)}) collective-permute-start(f32[128,256]{1,0:T(8,128)S(1)} %get-tuple-element.96), channel_id=1, source_target_pairs={{0,3},{1,2},{2,1},{3,0},{4,7},{5,6},{6,5},{7,4},{8,11},{9,10},{10,... | collective-permute-start | bytes 393224 | tf_op jit(solution)/shard_map/ppermute | solution.py:609
  70.4 3.5 %values_f.1 = (bf16[512,16,128]{2,1,0:T(8,128)(2,1)}, f32[8,128]{1,0:T(8,128)S(1)}) custom-call(f32[8,256,128]{2,1,0:T(8,128)S(1)} %collective-permute-done.15.refs_0_.got, f32[8,256,128]{2,1,0:T(8,128)S(1)} %get-tuple-element.84.refs_0_.mine.refs_1_, f32[16,128,128]{2,1,0:T(8,128)S(1)} %get-tuple-element.85.refs_1_.middle, ...), custom_call_target="tpu_custom_call" | custom-call | tf_op jit(solution)/shard_map/values_f/pallas_call | solution.py:563
  74.5 1.0 %cross_other.1.refs_4_.refs_2_ = f32[8,512]{1,0:T(8,128)S(1)} custom-call(f32[8,256,128]{2,1,0:T(8,128)S(1)} %collective-permute-done.15.refs_0_.got, f32[16,128,128]{2,1,0:T(8,128)S(1)} %get-tuple-element.85.refs_1_.middle, f32[16,128,128]{2,1,0:T(8,128)S(1)} %get-tuple-element.87.refs_2_.middle, ...), custom_call_target="tpu_custom_call" | custom-call | tf_op jit(solution)/shard_map/cross_other/pallas_call | solution.py:293
  76.5 1.8 %collective-permute-start.20 = (f32[128,256]{1,0:T(8,128)S(1)}, f32[128,256]{1,0:T(8,128)S(1)}, u32[]{:S(2)}, u32[]{:S(2)}) collective-permute-start(f32[128,256]{1,0:T(8,128)S(1)} %add.1._.refs_0_), channel_id=1, source_target_pairs={{0,3},{1,2},{2,1},{3,0},{4,7},{5,6},{6,5},{7,4},{8,11},{9,10},{10,... | collective-permute-start | bytes 393224 | tf_op jit(solution)/shard_map/ppermute | solution.py:609
  78.3 1.4 %collective-permute-start.19 = (f32[128,256]{1,0:T(8,128)S(1)}, f32[128,256]{1,0:T(8,128)S(1)}, u32[]{:S(2)}, u32[]{:S(2)}) collective-permute-start(f32[128,256]{1,0:T(8,128)S(1)} %add.1._.refs_0_), channel_id=1, source_target_pairs={{0,2},{1,3},{2,0},{3,1},{4,6},{5,7},{6,4},{7,5},{8,10},{9,11},{10,... | collective-permute-start | bytes 393224 | tf_op jit(solution)/shard_map/ppermute | solution.py:609
  79.7 3.4 %values_b.1 = (bf16[512,16,128]{2,1,0:T(8,128)(2,1)}, f32[8,128]{1,0:T(8,128)S(1)}) custom-call(f32[8,256,128]{2,1,0:T(8,128)S(1)} %collective-permute-done.15.refs_0_.got, f32[8,256,128]{2,1,0:T(8,128)S(1)} %get-tuple-element.84.refs_0_.mine.refs_1_, f32[16,128,128]{2,1,0:T(8,128)S(1)} %get-tuple-element.87.refs_2_.middle, ...), custom_call_target="tpu_custom_call" | custom-call | tf_op jit(solution)/shard_map/values_b/pallas_call | solution.py:563
  84.0 1.0 %collective-permute-done.19.refs_1_ = f32[128,256]{1,0:T(8,128)S(1)} collective-permute-done((f32[128,256]{1,0:T(8,128)S(1)}, f32[128,256]{1,0:T(8,128)S(1)}, u32[]{:S(2)}, u32[]{:S(2)}) %collective-permute-start.19) | collective-permute-done | bytes 131104 | tf_op jit(solution)/shard_map/ppermute | solution.py:609
  (39 shorter events, 10.6 us)
Async XLA Ops:
  0.6 7.1 %copy-start = (bf16[512,128]{1,0:T(8,128)(2,1)S(1)}, bf16[512,128]{1,0:T(8,128)(2,1)}, u32[]{:S(2)}) copy-start(bf16[512,128]{1,0:T(8,128)(2,1)} %proj.4) | copy-start | bytes 393220
  0.6 7.1 %copy-start.2 = (bf16[512,16,128]{2,1,0:T(8,128)(2,1)S(1)}, bf16[512,16,128]{2,1,0:T(8,128)(2,1)}, u32[]{:S(2)}) copy-start(bf16[512,16,128]{2,1,0:T(8,128)(2,1)} %values.3) | copy-start | bytes 6291460
  4.4 7.0 %collective-permute-start = (f32[8,136,128]{2,1,0:T(8,128)S(1)}, f32[8,136,128]{2,1,0:T(8,128)S(1)}, u32[]{:S(2)}, u32[]{:S(2)}) collective-permute-start(f32[8,136,128]{2,1,0:T(8,128)S(1)} %get-tuple-element.57), channel_id=1, source_target_pairs={{0,4},{4,0},{8,12},{12,8},{16,20},{20,16},{24,28},{28,24},{32,36},... | collective-permute-start | bytes 1671176 | tf_op jit(solution)/shard_map/ppermute | solution.py:435
  9.4 2.0 %collective-permute-start.1 = (f32[8,128,128]{2,1,0:T(8,128)S(1)}, f32[8,128,128]{2,1,0:T(8,128)S(1)}, u32[]{:S(2)}, u32[]{:S(2)}) collective-permute-start(f32[8,128,128]{2,1,0:T(8,128)S(1)} %get-tuple-element.63.refs_2_), channel_id=1, source_target_pairs={{0,4},{4,0},{8,12},{12,8},{16,20},{20,16},{24,28},{28,24},{32,36},... | collective-permute-start | bytes 1572872 | tf_op jit(solution)/shard_map/ppermute | solution.py:435
  9.5 9.5 %copy-start.1 = (bf16[512,128]{1,0:T(8,128)(2,1)S(1)}, bf16[512,128]{1,0:T(8,128)(2,1)}, u32[]{:S(2)}) copy-start(bf16[512,128]{1,0:T(8,128)(2,1)} %proj.5) | copy-start | bytes 393220
  9.5 9.6 %copy-start.3 = (f32[16]{0:T(128)S(1)}, f32[16]{0:T(128)}, u32[]{:S(2)}) copy-start(f32[16]{0:T(128)} %param.10) | copy-start | bytes 196
  11.6 11.9 %collective-permute-start.2 = (f32[2,264,128]{2,1,0:T(8,128)S(1)}, f32[2,264,128]{2,1,0:T(8,128)S(1)}, u32[]{:S(2)}, u32[]{:S(2)}) collective-permute-start(f32[2,264,128]{2,1,0:T(8,128)S(1)} %get-tuple-element.64), channel_id=1, source_target_pairs={{0,8},{4,44},{8,0},{12,36},{16,24},{20,60},{24,16},{28,52},{32,40}... | collective-permute-start | bytes 811016 | tf_op jit(solution)/shard_map/ppermute | solution.py:435
  12.5 11.0 %collective-permute-start.3 = (f32[2,264,128]{2,1,0:T(8,128)S(1)}, f32[2,264,128]{2,1,0:T(8,128)S(1)}, u32[]{:S(2)}, u32[]{:S(2)}) collective-permute-start(f32[2,264,128]{2,1,0:T(8,128)S(1)} %get-tuple-element.65), channel_id=1, source_target_pairs={{0,24},{4,60},{8,16},{12,52},{16,8},{20,44},{24,0},{28,36},{32,56}... | collective-permute-start | bytes 811016 | tf_op jit(solution)/shard_map/ppermute | solution.py:435
  13.8 10.5 %collective-permute-start.4 = (f32[2,264,128]{2,1,0:T(8,128)S(1)}, f32[2,264,128]{2,1,0:T(8,128)S(1)}, u32[]{:S(2)}, u32[]{:S(2)}) collective-permute-start(f32[2,264,128]{2,1,0:T(8,128)S(1)} %get-tuple-element.66), channel_id=1, source_target_pairs={{0,16},{4,52},{8,24},{12,60},{16,0},{20,36},{24,8},{28,44},{32,48}... | collective-permute-start | bytes 811016 | tf_op jit(solution)/shard_map/ppermute | solution.py:435
  15.4 11.0 %collective-permute-start.5 = (f32[2,264,128]{2,1,0:T(8,128)S(1)}, f32[2,264,128]{2,1,0:T(8,128)S(1)}, u32[]{:S(2)}, u32[]{:S(2)}) collective-permute-start(f32[2,264,128]{2,1,0:T(8,128)S(1)} %get-tuple-element.67.refs_0_), channel_id=1, source_target_pairs={{0,0},{4,36},{8,8},{12,44},{16,16},{20,52},{24,24},{28,60},{32,32}... | collective-permute-start | bytes 811016 | tf_op jit(solution)/shard_map/ppermute | solution.py:435
  26.6 3.1 %collective-permute-start.6 = (f32[2,264,128]{2,1,0:T(8,128)S(1)}, f32[2,264,128]{2,1,0:T(8,128)S(1)}, u32[]{:S(2)}, u32[]{:S(2)}) collective-permute-start(f32[2,264,128]{2,1,0:T(8,128)S(1)} %slab_up.1.refs_0_.refs_4_), channel_id=1, source_target_pairs={{0,4},{4,0},{8,12},{12,8},{16,20},{20,16},{24,28},{28,24},{32,36},... | collective-permute-start | bytes 811016 | tf_op jit(solution)/shard_map/ppermute | solution.py:435
  29.8 11.5 %collective-permute-start.8 = (f32[2,136,128]{2,1,0:T(8,128)S(1)}, f32[2,136,128]{2,1,0:T(8,128)S(1)}, u32[]{:S(2)}, u32[]{:S(2)}) collective-permute-start(f32[2,136,128]{2,1,0:T(8,128)S(1)} %get-tuple-element.72), channel_id=1, source_target_pairs={{0,64},{4,196},{8,72},{12,204},{16,80},{20,212},{24,88},{28,220},{... | collective-permute-start | bytes 417800 | tf_op jit(solution)/shard_map/ppermute | solution.py:435
  35.5 8.4 %collective-permute-start.7 = (f32[136,128]{1,0:T(8,128)S(1)}, f32[136,128]{1,0:T(8,128)S(1)}, u32[]{:S(2)}, u32[]{:S(2)}) collective-permute-start(f32[136,128]{1,0:T(8,128)S(1)} %get-tuple-element.71), channel_id=1, source_target_pairs={{0,128},{4,132},{8,136},{12,140},{16,144},{20,148},{24,152},{28,15... | collective-permute-start | bytes 208904 | tf_op jit(solution)/shard_map/ppermute | solution.py:435
  41.3 4.2 %collective-permute-start.10 = (f32[2,136,128]{2,1,0:T(8,128)S(1)}, f32[2,136,128]{2,1,0:T(8,128)S(1)}, u32[]{:S(2)}, u32[]{:S(2)}) collective-permute-start(f32[2,136,128]{2,1,0:T(8,128)S(1)} %collective-permute-done.8.refs_7_), channel_id=1, source_target_pairs={{0,4},{4,0},{8,12},{12,8},{16,20},{20,16},{24,28},{28,24},{32,36},... | collective-permute-start | bytes 417800 | tf_op jit(solution)/shard_map/ppermute | solution.py:435
  44.0 1.5 %collective-permute-start.9 = (f32[136,128]{1,0:T(8,128)S(1)}, f32[136,128]{1,0:T(8,128)S(1)}, u32[]{:S(2)}, u32[]{:S(2)}) collective-permute-start(f32[136,128]{1,0:T(8,128)S(1)} %collective-permute-done.7.refs_6_), channel_id=1, source_target_pairs={{0,4},{4,0},{8,12},{12,8},{16,20},{20,16},{24,28},{28,24},{32,36},... | collective-permute-start | bytes 208904 | tf_op jit(solution)/shard_map/ppermute | solution.py:435
  45.9 11.9 %collective-permute-start.11 = (f32[2,256,128]{2,1,0:T(8,128)S(1)}, f32[2,256,128]{2,1,0:T(8,128)S(1)}, u32[]{:S(2)}, u32[]{:S(2)}) collective-permute-start(f32[2,256,128]{2,1,0:T(8,128)S(1)} %get-tuple-element.73), channel_id=1, source_target_pairs={{0,8},{4,44},{8,0},{12,36},{16,24},{20,60},{24,16},{28,52},{32,40}... | collective-permute-start | bytes 786440 | tf_op jit(solution)/shard_map/ppermute | solution.py:435
  46.5 11.3 %collective-permute-start.12 = (f32[2,256,128]{2,1,0:T(8,128)S(1)}, f32[2,256,128]{2,1,0:T(8,128)S(1)}, u32[]{:S(2)}, u32[]{:S(2)}) collective-permute-start(f32[2,256,128]{2,1,0:T(8,128)S(1)} %get-tuple-element.74), channel_id=1, source_target_pairs={{0,24},{4,60},{8,16},{12,52},{16,8},{20,44},{24,0},{28,36},{32,56}... | collective-permute-start | bytes 786440 | tf_op jit(solution)/shard_map/ppermute | solution.py:435
  48.5 10.9 %collective-permute-start.13 = (f32[2,256,128]{2,1,0:T(8,128)S(1)}, f32[2,256,128]{2,1,0:T(8,128)S(1)}, u32[]{:S(2)}, u32[]{:S(2)}) collective-permute-start(f32[2,256,128]{2,1,0:T(8,128)S(1)} %get-tuple-element.75), channel_id=1, source_target_pairs={{0,16},{4,52},{8,24},{12,60},{16,0},{20,36},{24,8},{28,44},{32,48}... | collective-permute-start | bytes 786440 | tf_op jit(solution)/shard_map/ppermute | solution.py:435
  50.2 10.0 %collective-permute-start.14 = (f32[2,256,128]{2,1,0:T(8,128)S(1)}, f32[2,256,128]{2,1,0:T(8,128)S(1)}, u32[]{:S(2)}, u32[]{:S(2)}) collective-permute-start(f32[2,256,128]{2,1,0:T(8,128)S(1)} %get-tuple-element.76.refs_0_), channel_id=1, source_target_pairs={{0,0},{4,36},{8,8},{12,44},{16,16},{20,52},{24,24},{28,60},{32,32}... | collective-permute-start | bytes 786440 | tf_op jit(solution)/shard_map/ppermute | solution.py:435
  60.5 4.9 %collective-permute-start.15 = (f32[8,256,128]{2,1,0:T(8,128)S(1)}, f32[8,256,128]{2,1,0:T(8,128)S(1)}, u32[]{:S(2)}, u32[]{:S(2)}) collective-permute-start(f32[8,256,128]{2,1,0:T(8,128)S(1)} %get-tuple-element.83), channel_id=1, source_target_pairs={{0,4},{4,0},{8,12},{12,8},{16,20},{20,16},{24,28},{28,24},{32,36},... | collective-permute-start | bytes 3145736 | tf_op jit(solution)/shard_map/ppermute | solution.py:435
  66.4 9.1 %collective-permute-start.16 = (f32[128,256]{1,0:T(8,128)S(1)}, f32[128,256]{1,0:T(8,128)S(1)}, u32[]{:S(2)}, u32[]{:S(2)}) collective-permute-start(f32[128,256]{1,0:T(8,128)S(1)} %get-tuple-element.95), channel_id=1, source_target_pairs={{0,1},{1,0},{2,3},{3,2},{4,5},{5,4},{6,7},{7,6},{8,9},{9,8},{10,11... | collective-permute-start | bytes 393224 | tf_op jit(solution)/shard_map/ppermute | solution.py:609
  67.8 7.7 %collective-permute-start.17 = (f32[128,256]{1,0:T(8,128)S(1)}, f32[128,256]{1,0:T(8,128)S(1)}, u32[]{:S(2)}, u32[]{:S(2)}) collective-permute-start(f32[128,256]{1,0:T(8,128)S(1)} %get-tuple-element.96), channel_id=1, source_target_pairs={{0,3},{1,2},{2,1},{3,0},{4,7},{5,6},{6,5},{7,4},{8,11},{9,10},{10,... | collective-permute-start | bytes 393224 | tf_op jit(solution)/shard_map/ppermute | solution.py:609
  69.7 6.7 %collective-permute-start.18 = (f32[128,256]{1,0:T(8,128)S(1)}, f32[128,256]{1,0:T(8,128)S(1)}, u32[]{:S(2)}, u32[]{:S(2)}) collective-permute-start(f32[128,256]{1,0:T(8,128)S(1)} %get-tuple-element.97), channel_id=1, source_target_pairs={{0,2},{1,3},{2,0},{3,1},{4,6},{5,7},{6,4},{7,5},{8,10},{9,11},{10,... | collective-permute-start | bytes 393224 | tf_op jit(solution)/shard_map/ppermute | solution.py:609
  76.4 7.5 %collective-permute-start.21 = (f32[128,256]{1,0:T(8,128)S(1)}, f32[128,256]{1,0:T(8,128)S(1)}, u32[]{:S(2)}, u32[]{:S(2)}) collective-permute-start(f32[128,256]{1,0:T(8,128)S(1)} %add.1._.refs_0_), channel_id=1, source_target_pairs={{0,1},{1,0},{2,3},{3,2},{4,5},{5,4},{6,7},{7,6},{8,9},{9,8},{10,11... | collective-permute-start | bytes 393224 | tf_op jit(solution)/shard_map/ppermute | solution.py:609
  76.5 7.4 %collective-permute-start.20 = (f32[128,256]{1,0:T(8,128)S(1)}, f32[128,256]{1,0:T(8,128)S(1)}, u32[]{:S(2)}, u32[]{:S(2)}) collective-permute-start(f32[128,256]{1,0:T(8,128)S(1)} %add.1._.refs_0_), channel_id=1, source_target_pairs={{0,3},{1,2},{2,1},{3,0},{4,7},{5,6},{6,5},{7,4},{8,11},{9,10},{10,... | collective-permute-start | bytes 393224 | tf_op jit(solution)/shard_map/ppermute | solution.py:609
  78.3 6.6 %collective-permute-start.19 = (f32[128,256]{1,0:T(8,128)S(1)}, f32[128,256]{1,0:T(8,128)S(1)}, u32[]{:S(2)}, u32[]{:S(2)}) collective-permute-start(f32[128,256]{1,0:T(8,128)S(1)} %add.1._.refs_0_), channel_id=1, source_target_pairs={{0,2},{1,3},{2,0},{3,1},{4,6},{5,7},{6,4},{7,5},{8,10},{9,11},{10,... | collective-permute-start | bytes 393224 | tf_op jit(solution)/shard_map/ppermute | solution.py:609
